TPU v7x, 256 devices: a whole 4x4x8 slice. The times are simulated.
256 devices in a mesh: ctx: 32 (over z_lo, x, core), dp: 8 (over z_hi, y).
Axes of the slice: x: 4, y: 4, z: 8 (z_hi: 2, z_lo: 4; z = z_hi * 4 + z_lo), core: 2. Of those that a mesh axis runs over, the one named last changes fastest.
Arguments:
- q_nope: bfloat16 [4096, 8192], P('ctx', 'dp'), may hold values from -6 to 6
- q_rope: bfloat16 [4096, 4096], P('ctx', 'dp'), may hold values from -400 to 400
- latent: bfloat16 [4096, 512], P('ctx'), may hold values from -6 to 6
- rope_key: bfloat16 [4096, 64], P('ctx'), may hold values from -6 to 6
- segment_ids: int32 [4096], P('ctx'), may hold values from 0 to 3, as said below
- w_uk: bfloat16 [64, 128, 512], P('dp', 'ctx'), may hold values from -0.5 to 0.5
- w_uv: bfloat16 [64, 512, 128], P('dp', 'ctx'), may hold values from -0.25 to 0.25
- w_out: bfloat16 [8192, 7168], P('dp', 'ctx'), may hold values from -0.0625 to 0.0625
Outputs:
- mixed: bfloat16 [4096, 7168], P('ctx', 'dp')
- log_sum: float32 [4096, 64], P('ctx', 'dp')
Inputs may be any that keep to these rules, and one draw needn't show every extreme that they name: `segment_ids`: document numbers never fall along the positions and every number of 0 to 3 occurs; one document holds exactly 3072 positions, every other at least 1.
All inputs are finite; a program needn't handle non-finite values.
Results may differ from a plain program's by a relative error of at most 0.017.
Values may be sent and summed in bfloat16 or wider, within the bound.
No kernel may reach another device: no remote copies, remote signals or barrier semaphores. Data moves between devices by JAX's collectives and lax.ppermute only.
A program may use at most 128 MiB of HBM per device.

v0:
```python
import jax
import jax.numpy as jnp
from jax import lax
from jax.experimental import pallas as pl
from jax.experimental.pallas import tpu as pltpu
from jax.sharding import PartitionSpec as P

HEAD_DIM = 128
KV_RANK = 512
ROPE_DIM = 64
WIDE = 640
TILE = 512
CHUNK = 256
FAR = -1e30
LOG2E = 1.4426950408889634
SCALE = (HEAD_DIM + ROPE_DIM) ** (-0.5)
AXES = ("ctx", "dp")
MIB = 1024 * 1024
VMEM = pl.BlockSpec(memory_space=pltpu.VMEM)
SMEM = pl.BlockSpec(memory_space=pltpu.SMEM)
ANY = pl.BlockSpec(memory_space=pl.ANY)
HBM = pl.BlockSpec(memory_space=pltpu.HBM)


def moved(array, to):
    pairs = []
    for ctx in range(32):
        for dp in range(8):
            z, x, core, half, y = to(ctx // 8, ctx // 2 % 4, ctx % 2, dp // 4, dp % 4)
            pairs.append((ctx * 8 + dp, (z * 8 + x * 2 + core) * 8 + half * 4 + y))
    return lax.ppermute(array, AXES, pairs)


def along_x(by):
    return lambda z, x, core, half, y: (z, (x + by) % 4, core, half, y)


def along_y(by):
    return lambda z, x, core, half, y: (z, x, core, half, (y + by) % 4)


def along_z_ring(by):
    def to(z, x, core, half, y):
        whole = (half * 4 + z + by) % 8
        return (whole % 4, x, core, whole // 4, y)

    return to


def flip_z(bit):
    return lambda z, x, core, half, y: (z ^ bit, x, core, half, y)


def other_core(z, x, core, half, y):
    return (z, x, 1 - core, half, y)


def other_half(z, x, core, half, y):
    return (z, x, core, 1 - half, y)


def settle(cross, swap):
    def to(z, x, core, half, y):
        low = 1 - x % 2 if cross else x % 2
        return (z, y % 2 * 2 + low, 1 - core if swap else core, half, y // 2 * 2 + x // 2)

    return to


def contract_last(left, right):
    return lax.dot_general(left, right, (((1,), (1,)), ((), ())), preferred_element_type=jnp.float32)


def call(kernel, outs, in_specs, scratch=(), limit=32, flops=0, name=None):
    return pl.pallas_call(
        kernel,
        out_shape=tuple(jax.ShapeDtypeStruct(*out) for out in outs),
        in_specs=in_specs,
        out_specs=tuple(VMEM for _ in outs),
        scratch_shapes=list(scratch),
        compiler_params=pltpu.CompilerParams(vmem_limit_bytes=limit * MIB),
        cost_estimate=pl.CostEstimate(flops=flops, bytes_accessed=3 * MIB, transcendentals=0),
        name=name,
    )


def doc_columns(docs):
    return jnp.transpose(jnp.broadcast_to(docs.astype(jnp.float32), (128, 128)))


def fetched(pairs, sems):
    copies = [pltpu.make_async_copy(a, b, sems.at[n]) for n, (a, b) in enumerate(pairs)]
    for copy in copies:
        copy.start()
    return copies


def keys_kernel(latent_in, rope_in, docs_in, out, rope_key, docs, sems):
    copies = fetched(
        [(latent_in, out.at[:, 0:KV_RANK]), (rope_in, rope_key), (docs_in, docs)], sems
    )
    for copy in copies:
        copy.wait()
    rope = jnp.transpose(rope_key[...].astype(jnp.float32))
    doc = doc_columns(docs[...])
    lane = lax.broadcasted_iota(jnp.int32, (128, 128), 1)
    place = (lane - ROPE_DIM).astype(jnp.float32)
    tail = jnp.where(place == doc, 1.0, jnp.where(lane == ROPE_DIM + 4, doc, 0.0))
    tail = jnp.where(lane < ROPE_DIM, jnp.concatenate([rope, rope], axis=1), tail)
    out[:, KV_RANK:WIDE] = tail.astype(jnp.bfloat16)


def first_kernel(*refs):
    row, line = refs[-2:]
    for n in range(4):
        row[n] = refs[n][...]
        line[n] = refs[4 + n][...]


def second_kernel(row, plus, minus, *rest):
    ring, (low, high, twelve, ups) = rest[:4], rest[4:]
    low[...] = plus[0:2]
    high[...] = minus[2:4]
    for n, part in enumerate((row, plus, minus)):
        twelve[4 * n : 4 * n + 4] = part[...]
    for n in range(4):
        ups[n] = ring[n][...]


def gate_kernel(weight_in, low_in, high_in, token, weight, low, high, sems):
    copies = fetched([(weight_in, weight)], sems)
    low[...] = low_in[...]
    high[...] = high_in[...]
    for copy in copies:
        copy.wait()


def hold_kernel(values_in, weight_in, first, second, values, weight):
    values[...] = values_in[...]
    weight[...] = weight_in[...]


def queries_kernel(
    place, q_nope_in, q_rope_in, docs, mine, theirs, query, up_value, token, up_key, q_nope, q_rope, sems
):
    token[...] = jnp.zeros((8, 128), jnp.float32)
    copies = fetched([(q_nope_in, q_nope), (q_rope_in, q_rope)], sems)
    z, x, core = place[0], place[1], place[2]
    row = lax.broadcasted_iota(jnp.int32, (512, 1), 0)
    position = row % 128 // 4
    slot = ((position % 2) ^ core) * 16 + ((position // 2 % 4 - x) & 3) * 4 + ((position // 8) ^ z)
    wanted = slot * 16 + row // 128 * 4 + row % 4
    pick = (lax.broadcasted_iota(jnp.int32, (512, 512), 1) == wanted).astype(jnp.float32)
    pick = pick.astype(jnp.bfloat16)
    for h in range(0, 8, 2):
        both = [
            jnp.concatenate(
                [side[:, :, n].reshape(256, 128) for side in (mine, theirs)], axis=0
            )
            for n in (h, h + 1)
        ]
        ordered = jnp.dot(pick, jnp.concatenate(both, axis=1), preferred_element_type=jnp.float32)
        ordered = ordered.astype(jnp.bfloat16)
        for n in (0, 1):
            for j in range(4):
                up_key[h + n, :, j * 128 : j * 128 + 128] = ordered[
                    j * 128 : j * 128 + 128, n * 128 : n * 128 + 128
                ]
    for side, array in enumerate((mine, theirs)):
        for dx in range(4):
            for dz in range(4):
                at = (z ^ dz) * 8 + ((x + dx) & 3) * 2 + (core ^ side)
                up_value[:, pl.ds(pl.multiple_of(at * 16, 16), 16), :] = array[dx, dz, 8:16]
    doc = doc_columns(docs[...])
    lane = lax.broadcasted_iota(jnp.int32, (128, 128), 1)
    other_doc = (lane >= ROPE_DIM) & (lane < ROPE_DIM + 4)
    other_doc = other_doc & ((lane - ROPE_DIM).astype(jnp.float32) != doc)
    marks = jnp.where(other_doc, FAR, 0.0).astype(jnp.bfloat16)[:, ROPE_DIM:]
    for copy in copies:
        copy.wait()
    for h in range(8):
        rows = pl.ds(h * 128, 128)
        latent_part = jnp.dot(
            q_nope[:, h * 128 : h * 128 + 128], up_key[h], preferred_element_type=jnp.float32
        )
        query[rows, 0:KV_RANK] = latent_part.astype(jnp.bfloat16)
        query[rows, KV_RANK:WIDE] = jnp.concatenate(
            [q_rope[:, h * 64 : h * 64 + 64], marks], axis=1
        )


def attention_kernel(place, query, up_value, *rest):
    pieces, (values, log_sum, keys, score, total, peak, weighed, sems) = rest[:6], rest[6:]
    z, x, core = place[0], place[1], place[2]
    blocks = TILE // 128
    own_tile = lax.div(place[3], blocks)

    def copy_of(source, block):
        rows = pl.ds(pl.multiple_of(block * 128, 128), 128)
        return pltpu.make_async_copy(source, keys.at[rows], sems.at[block])

    for side in range(2):
        twelve, two_low, two_high = pieces[side * 3 : side * 3 + 3]
        for dz, dx in [(a, b) for a in range(4) for b in range(4)]:
            if dz == 2:
                source = two_low.at[dx] if dx < 2 else two_high.at[dx - 2]
            else:
                source = twelve.at[{0: 0, 1: 4, 3: 8}[dz] + dx]
            block = (((z + dz) & 3) * 4 + ((x + dx) & 3)) * 2 + (core ^ side)

            @pl.when(block < (own_tile + 1) * blocks)
            def _():
                copy_of(source, block).start()

    def arrived(block):
        copy_of(pieces[0].at[0], block).wait()

    for n in range(blocks):
        arrived(own_tile * blocks + n)

    def lane_groups(array, join):
        parts = [array[:, n * 128 : n * 128 + 128] for n in range(TILE // 128)]
        return join(join(parts[0], parts[1]), join(parts[2], parts[3]))

    def scores(tile, first):
        start = pl.multiple_of(tile * TILE, TILE)
        for part in range(1024 // CHUNK):
            rows = pl.ds(part * CHUNK, CHUNK)
            new = contract_last(query[rows, :], keys[pl.ds(start, TILE), :])
            if first:
                at = lax.broadcasted_iota(jnp.int32, (CHUNK, TILE), 0)
                row_place = place[3] * 128 + (at & 127)
                key_place = start + lax.broadcasted_iota(jnp.int32, (CHUNK, TILE), 1)
                new = jnp.where(key_place <= row_place, new, FAR)
            score[tile, rows, :] = new
            best = lane_groups(new, jnp.maximum)
            peak[rows, :] = best if first else jnp.maximum(peak[rows, :], best)

    def weigh(tile, first):
        start = pl.multiple_of(tile * TILE, TILE)
        for part in range(1024 // CHUNK):
            rows = pl.ds(part * CHUNK, CHUNK)
            top = peak[rows, :]
            top = jnp.concatenate([top] * (TILE // 128), axis=1)
            expon = jnp.exp2((score[tile, rows, :] - top) * (SCALE * LOG2E))
            lanes = lane_groups(expon, jnp.add)
            product = jnp.dot(
                expon.astype(jnp.bfloat16),
                keys[pl.ds(start, TILE), 0:KV_RANK],
                preferred_element_type=jnp.float32,
            )
            total[rows, :] = lanes if first else total[rows, :] + lanes
            weighed[rows, :] = product if first else weighed[rows, :] + product

    def each_before(do):
        lax.fori_loop(low, own_tile, lambda tile, carry: (do(tile, False), carry)[1], 0)

    scores(own_tile, True)
    lax.fori_loop(0, own_tile * blocks, lambda block, carry: (arrived(block), carry)[1], 0)
    lane = lax.broadcasted_iota(jnp.int32, (16, 128), 1)
    row_at = lax.broadcasted_iota(jnp.int32, (16, 128), 0)
    earlier = jnp.zeros((16, 128), jnp.float32)
    for tile in range(4096 // TILE):
        last = keys[tile * TILE + TILE - 16 : tile * TILE + TILE, KV_RANK:WIDE].astype(jnp.float32)
        before = (last < place[4].astype(jnp.float32)) & (jnp.int32(tile) < own_tile)
        earlier = earlier + jnp.where(before, 1.0, 0.0)
    here = (lane == ROPE_DIM + 4) & (row_at == 15)
    low = jnp.max(jnp.where(here, earlier, 0.0)).astype(jnp.int32)
    each_before(scores)
    for part in range(1024 // CHUNK):
        rows = pl.ds(part * CHUNK, CHUNK)
        top = jnp.max(peak[rows, :], axis=1, keepdims=True)
        peak[rows, :] = jnp.broadcast_to(top, (CHUNK, 128))
    weigh(own_tile, True)
    each_before(weigh)

    column = lax.broadcasted_iota(jnp.int32, (128, 128), 1)
    logs = jnp.zeros((128, 128), jnp.float32)
    for h in range(8):
        rows = pl.ds(h * 128, 128)
        whole = jnp.sum(total[rows, :], axis=1, keepdims=True)
        attended = (weighed[rows, :] / whole).astype(jnp.bfloat16)
        value = jnp.dot(attended, up_value[h], preferred_element_type=jnp.float32)
        values[h * 128 : h * 128 + 128, :] = jnp.transpose(value).astype(jnp.bfloat16)
        logs = jnp.where(column == h, peak[rows, :] * SCALE + jnp.log(whole), logs)
    log_sum[...] = jnp.transpose(logs)[0:8, :]


def third_kernel(place, *refs):
    for dx in range(4):
        refs[5][(place[0] + dx) & 3] = refs[dx][...]


def project_kernel(place, mine, theirs, *rest):
    blocks, outs, (weights, sems) = rest[:4], rest[4:12], rest[12:]
    copies = []
    for dz in range(4):
        at = place[0] ^ dz
        copies.append((blocks[dz], weights.at[at & 1, 1 - (lax.div(at, 2) ^ place[5])]))
    copies = fetched(copies, sems)
    for copy in copies:
        copy.wait()
    for n in range(4):
        which = place[1 + n]
        high, low = lax.div(which, 2), which & 1
        right = jnp.concatenate(
            [mine[2 * low], theirs[2 * low], mine[2 * low + 1], theirs[2 * low + 1]], axis=1
        )
        weight = weights[high].reshape(448, 1024)
        terms = jnp.dot(weight, right, preferred_element_type=jnp.float32).astype(jnp.bfloat16)
        for half in range(2):
            for at in range(2):
                outs[2 * n + half][at] = terms[
                    half * 224 : half * 224 + 224, at * 256 : at * 256 + 256
                ]


def sum_kernel(own, left, right, out):
    whole = own[...].astype(jnp.float32) + left[...].astype(jnp.float32)
    out[...] = (whole + right[...].astype(jnp.float32)).astype(jnp.bfloat16)


def settle_kernel(place, own, left, right, arrived, *rest):
    outs, summed = rest[:4], rest[4]
    whole = own[...].astype(jnp.float32) + left[...].astype(jnp.float32)
    whole = whole + right[...].astype(jnp.float32) + arrived[...].astype(jnp.float32)
    summed[...] = whole.astype(jnp.bfloat16)
    for n in range(4):
        outs[n][...] = summed[place[0] ^ (n // 2), :, n % 2 * 128 : n % 2 * 128 + 128]


def finish_kernel(place, *rest):
    arrays, (mixed, whole) = rest[:4], rest[4:]
    for n in range(4):
        at = (place[0] ^ (n // 2)) * 2 + (place[1] ^ (n % 2))
        whole[at] = arrays[n][...].astype(jnp.float32)
    mixed[...] = jnp.transpose(whole[...].reshape(896, 128)).astype(jnp.bfloat16)


def gather_ring(block):
    return [block] + [moved(block, along_x(-by)) for by in (1, 2, 3)]


def per_device(q_nope, q_rope, latent, rope_key, segment_ids, w_uk, w_uv, w_out):
    ctx, dp = lax.axis_index("ctx"), lax.axis_index("dp")
    z, x, core = ctx // 8, ctx // 2 % 4, ctx % 2
    half, y = dp // 4, dp % 4
    place = jnp.stack([z, x, core, ctx, segment_ids[0]]).astype(jnp.int32)
    docs = segment_ids.reshape(1, 128)

    (block,) = call(
        keys_kernel,
        [((128, WIDE), jnp.bfloat16)],
        [HBM] * 3,
        [
            pltpu.VMEM((ROPE_DIM, 128), jnp.bfloat16),
            pltpu.VMEM((1, 128), jnp.int32),
            pltpu.SemaphoreType.DMA((3,)),
        ],
        limit=8,
        name="keys",
    )(latent, rope_key.T, docs)
    up = w_uk.reshape(8, 4, 4, 128).transpose(0, 2, 1, 3).reshape(8, 16, 128)
    up = jnp.concatenate([up, w_uv])
    ring = gather_ring(block)
    line = [up] + [moved(up, flip_z(bits)) for bits in (1, 2, 3)]
    row, line = call(
        first_kernel,
        [((4, 128, WIDE), jnp.bfloat16), ((4, 16, 16, 128), jnp.bfloat16)],
        [VMEM] * 8,
        limit=16,
        name="first",
    )(*ring, *line)
    plus, minus = moved(row, along_z_ring(-1)), moved(row, along_z_ring(1))
    low, high, twelve, ups = call(
        second_kernel,
        [
            ((2, 128, WIDE), jnp.bfloat16),
            ((2, 128, WIDE), jnp.bfloat16),
            ((12, 128, WIDE), jnp.bfloat16),
            ((4, 4, 16, 16, 128), jnp.bfloat16),
        ],
        [VMEM] * 7,
        limit=16,
        name="second",
    )(row, plus, minus, *gather_ring(line))
    pieces = [twelve, moved(low, along_z_ring(-1)), moved(high, along_z_ring(1))]
    theirs = moved(twelve, other_core)

    query, up_value, token = call(
        queries_kernel,
        [
            ((1024, WIDE), jnp.bfloat16),
            ((8, KV_RANK, HEAD_DIM), jnp.bfloat16),
            ((8, 128), jnp.float32),
        ],
        [SMEM] + [HBM] * 2 + [VMEM] * 3,
        [
            pltpu.VMEM((8, HEAD_DIM, KV_RANK), jnp.bfloat16),
            pltpu.VMEM((128, 1024), jnp.bfloat16),
            pltpu.VMEM((128, 512), jnp.bfloat16),
            pltpu.SemaphoreType.DMA((2,)),
        ],
        limit=16,
        flops=700_000_000,
        name="queries",
    )(place, q_nope, q_rope, docs, ups, moved(ups, other_core))

    weight, low, high = call(
        gate_kernel,
        [((224, 1024), jnp.bfloat16)] + [((2, 128, WIDE), jnp.bfloat16)] * 2,
        [HBM] + [VMEM] * 3,
        [pltpu.SemaphoreType.DMA((1,))],
        limit=8,
        name="gate",
    )(w_out.T, *pieces[1:], token)
    weights = [weight, moved(weight, flip_z(1)), moved(weight, flip_z(2))]
    pieces = [twelve, low, high, theirs, moved(low, other_core), moved(high, other_core)]
    values, log_sum = call(
        attention_kernel,
        [((1024, 128), jnp.bfloat16), ((8, 128), jnp.float32)],
        [SMEM, VMEM, VMEM] + [ANY] * 6,
        [
            pltpu.VMEM((4096, WIDE), jnp.bfloat16),
            pltpu.VMEM((4096 // TILE, 1024, TILE), jnp.float32),
            pltpu.VMEM((1024, 128), jnp.float32),
            pltpu.VMEM((1024, 128), jnp.float32),
            pltpu.VMEM((1024, KV_RANK), jnp.float32),
            pltpu.SemaphoreType.DMA((32,)),
        ],
        limit=32,
        flops=10_000_000_000,
        name="attention",
    )(place, query, up_value, *pieces)

    values, weight = call(
        hold_kernel,
        [((1024, 128), jnp.bfloat16), ((224, 1024), jnp.bfloat16)],
        [VMEM] * 4,
        limit=8,
        name="hold",
    )(values, *weights)
    weights.append(moved(weight, flip_z(3)))
    (gathered,) = call(
        third_kernel, [((4, 1024, 128), jnp.bfloat16)], [SMEM] + [VMEM] * 5, limit=8, name="third"
    )(x.reshape(1).astype(jnp.int32), *gather_ring(values), weights[3])
    order = [z, (y + 2) % 4, (y + 1) % 4, (y + 3) % 4, y, half]
    terms = call(
        project_kernel,
        [((2, 224, 256), jnp.bfloat16)] * 8,
        [SMEM] + [VMEM] * 2 + [ANY] * 4,
        [pltpu.VMEM((2, 2, 224, 1024), jnp.bfloat16), pltpu.SemaphoreType.DMA((4,))],
        limit=24,
        flops=1_880_000_000,
        name="project",
    )(jnp.stack(order).astype(jnp.int32), gathered, moved(gathered, other_core), *weights)
    far, right, left, own = terms[0:2], terms[2:4], terms[4:6], terms[6:8]
    far = moved(far[0], along_y(1)), moved(far[1], along_y(-1))
    from_left = [moved(right[0] + far[0], along_y(1)), moved(right[1], along_y(1))]
    from_right = [moved(left[0], along_y(-1)), moved(left[1] + far[1], along_y(-1))]
    (give,) = call(
        sum_kernel, [((2, 224, 256), jnp.bfloat16)], [VMEM] * 3, limit=16, name="sums"
    )(own[0], from_left[0], from_right[0])
    arrived = moved(give, other_half)
    low = jnp.stack([x % 2, core]).astype(jnp.int32)
    sums = call(
        settle_kernel,
        [((224, 128), jnp.bfloat16)] * 4,
        [SMEM] + [VMEM] * 4,
        [pltpu.VMEM((2, 224, 256), jnp.bfloat16)],
        limit=16,
        name="settle",
    )(low, own[1], from_left[1], from_right[1], arrived)
    (mixed,) = call(
        finish_kernel,
        [((128, 896), jnp.bfloat16)],
        [SMEM] + [VMEM] * 4,
        [pltpu.VMEM((4, 224, 128), jnp.float32)],
        limit=16,
        name="finish",
    )(low, *[moved(term, settle(n // 2, n % 2)) for n, term in enumerate(sums)])
    return (mixed, log_sum.T)


def solution(mesh):
    return jax.shard_map(
        per_device,
        mesh=mesh,
        in_specs=(
            P("ctx", "dp"),
            P("ctx", "dp"),
            P("ctx", None),
            P("ctx", None),
            P("ctx"),
            P("dp", "ctx", None),
            P("dp", "ctx", None),
            P("dp", "ctx"),
        ),
        out_specs=(P("ctx", "dp"), P("ctx", "dp")),
        check_vma=False,
    )
```

profile of v0, /device:TPU:41, one launch (start us, length us, event | category | flops | bytes accessed | tf_op | source)
XLA Modules:
  0.0 150.0 jit_solution(9253800079914506614)
XLA Ops:
  0.6 0.9 copy-done.1
  1.5 0.7 copy-done.2
  2.3 0.7 copy-done.3
  2.9 0.2 keys.1.refs_0_
  3.1 2.6 %collective-permute-start = (bf16[128,640]{1,0:T(8,128)(2,1)S(1)}, bf16[128,640]{1,0:T(8,128)(2,1)S(1)}, u32[]{:S(2)}, u32[]{:S(2)}) collective-permute-start(bf16[128,640]{1,0:T(8,128)(2,1)S(1)} %keys.1.refs_0_), channel_id=1, source_target_pairs={{0,48},{1,49},{2,50},{3,51},{4,52},{5,53},{6,54},{7,55},{8,56},{9,... | collective-permute-start | bytes 491528 | tf_op jit(solution)/shard_map/ppermute | solution.py:31
  5.7 0.5 collective-permute-start.1
  6.2 0.6 collective-permute-start.2
  6.8 0.8 pad_maximum_fusion.refs_4_
  7.7 3.1 %collective-permute-start.4 = (bf16[16,16,128]{2,1,0:T(8,128)(2,1)S(1)}, bf16[16,16,128]{2,1,0:T(8,128)(2,1)S(1)}, u32[]{:S(2)}, u32[]{:S(2)}) collective-permute-start(bf16[16,16,128]{2,1,0:T(8,128)(2,1)S(1)} %pad_maximum_fusion.refs_4_), channel_id=1, source_target_pairs={{0,128},{1,129},{2,130},{3,131},{4,132},{5,133},{6,134},{7,135},{8... | collective-permute-start | bytes 196616 | tf_op jit(solution)/shard_map/ppermute | solution.py:31
  10.8 1.8 %collective-permute-start.5 = (bf16[16,16,128]{2,1,0:T(8,128)(2,1)S(1)}, bf16[16,16,128]{2,1,0:T(8,128)(2,1)S(1)}, u32[]{:S(2)}, u32[]{:S(2)}) collective-permute-start(bf16[16,16,128]{2,1,0:T(8,128)(2,1)S(1)} %pad_maximum_fusion.refs_4_), channel_id=1, source_target_pairs={{0,192},{1,193},{2,194},{3,195},{4,196},{5,197},{6,198},{7,199},{8... | collective-permute-start | bytes 196616 | tf_op jit(solution)/shard_map/ppermute | solution.py:31
  12.7 0.7 collective-permute-done.4.refs_6_
  13.4 3.0 %collective-permute-done.5.refs_7_ = bf16[16,16,128]{2,1,0:T(8,128)(2,1)S(1)} collective-permute-done((bf16[16,16,128]{2,1,0:T(8,128)(2,1)S(1)}, bf16[16,16,128]{2,1,0:T(8,128)(2,1)S(1)}, u32[]{:S(2)}, u32[]{:S(2)}) %collective-permute-start.5) | collective-permute-done | bytes 65568 | tf_op jit(solution)/shard_map/ppermute | solution.py:31
  16.4 0.4 collective-permute-done.2.refs_3_
  16.9 0.4 collective-permute-start.6
  17.3 1.4 collective-permute-start.7
  18.7 1.7 %collective-permute-start.8 = (bf16[4,16,16,128]{3,2,1,0:T(8,128)(2,1)S(1)}, bf16[4,16,16,128]{3,2,1,0:T(8,128)(2,1)S(1)}, u32[]{:S(2)}, u32[]{:S(2)}) collective-permute-start(bf16[4,16,16,128]{3,2,1,0:T(8,128)(2,1)S(1)} %get-tuple-element.31.rest_0_), channel_id=1, source_target_pairs={{0,48},{1,49},{2,50},{3,51},{4,52},{5,53},{6,54},{7,55},{8,56},{9,... | collective-permute-start | bytes 786440 | tf_op jit(solution)/shard_map/ppermute | solution.py:31
  20.4 1.2 collective-permute-start.9
  21.6 2.8 %collective-permute-done.8.rest_1_ = bf16[4,16,16,128]{3,2,1,0:T(8,128)(2,1)S(1)} collective-permute-done((bf16[4,16,16,128]{3,2,1,0:T(8,128)(2,1)S(1)}, bf16[4,16,16,128]{3,2,1,0:T(8,128)(2,1)S(1)}, u32[]{:S(2)}, u32[]{:S(2)}) %collective-permute-start.8) | collective-permute-done | bytes 262176 | tf_op jit(solution)/shard_map/ppermute | solution.py:31
  24.5 2.8 %collective-permute-done.9.rest_2_ = bf16[4,16,16,128]{3,2,1,0:T(8,128)(2,1)S(1)} collective-permute-done((bf16[4,16,16,128]{3,2,1,0:T(8,128)(2,1)S(1)}, bf16[4,16,16,128]{3,2,1,0:T(8,128)(2,1)S(1)}, u32[]{:S(2)}, u32[]{:S(2)}) %collective-permute-start.9) | collective-permute-done | bytes 262176 | tf_op jit(solution)/shard_map/ppermute | solution.py:31
  27.2 7.5 %collective-permute-done.10.rest_3_ = bf16[4,16,16,128]{3,2,1,0:T(8,128)(2,1)S(1)} collective-permute-done((bf16[4,16,16,128]{3,2,1,0:T(8,128)(2,1)S(1)}, bf16[4,16,16,128]{3,2,1,0:T(8,128)(2,1)S(1)}, u32[]{:S(2)}, u32[]{:S(2)}) %collective-permute-start.10) | collective-permute-done | bytes 262176 | tf_op jit(solution)/shard_map/ppermute | solution.py:31
  34.8 1.6 %second.1 = (bf16[2,128,640]{2,1,0:T(8,128)(2,1)S(1)}, bf16[2,128,640]{2,1,0:T(8,128)(2,1)S(1)}, bf16[12,128,640]{2,1,0:T(8,128)(2,1)}, bf16[4,4,16,16,128]{4,3,2,1,0:T(8,128)(2,1)S(1)}) custom-call(bf16[4,128,640]{2,1,0:T(8,128)(2,1)S(1)} %get-tuple-element.30.row, bf16[4,128,640]{2,1,0:T(8,128)(2,1)S(1)} %collective-permute-done.6.plus, ...), custom_call_target="tpu_custom_call" | custom-call | bytes 3145728 | tf_op jit(solution)/shard_map/second/pallas_call | solution.py:375
  36.3 3.3 %collective-permute-start.14 = (bf16[12,128,640]{2,1,0:T(8,128)(2,1)}, bf16[12,128,640]{2,1,0:T(8,128)(2,1)}, u32[]{:S(2)}, u32[]{:S(2)}) collective-permute-start(bf16[12,128,640]{2,1,0:T(8,128)(2,1)} %get-tuple-element.35.rest_0_), channel_id=1, source_target_pairs={{0,8},{1,9},{2,10},{3,11},{4,12},{5,13},{6,14},{7,15},{8,0},{9,1},... | collective-permute-start | bytes 5898248 | tf_op jit(solution)/shard_map/ppermute | solution.py:31
  39.7 2.7 %collective-permute-start.12 = (bf16[2,128,640]{2,1,0:T(8,128)(2,1)S(1)}, bf16[2,128,640]{2,1,0:T(8,128)(2,1)S(1)}, u32[]{:S(2)}, u32[]{:S(2)}) collective-permute-start(bf16[2,128,640]{2,1,0:T(8,128)(2,1)S(1)} %get-tuple-element.36), channel_id=1, source_target_pairs={{0,196},{1,197},{2,198},{3,199},{4,192},{5,193},{6,194},{7,195},{8... | collective-permute-start | bytes 983048 | tf_op jit(solution)/shard_map/ppermute | solution.py:31
  42.5 2.3 %collective-permute-done.11.theirs = bf16[4,4,16,16,128]{4,3,2,1,0:T(8,128)(2,1)} collective-permute-done((bf16[4,4,16,16,128]{4,3,2,1,0:T(8,128)(2,1)S(1)}, bf16[4,4,16,16,128]{4,3,2,1,0:T(8,128)(2,1)}, u32[]{:S(2)}, u32[]{:S(2)}) %collective-permute-start.11) | collective-permute-done | bytes 1048608 | tf_op jit(solution)/shard_map/ppermute | solution.py:31
  44.8 2.9 %queries.1 = (bf16[1024,640]{1,0:T(8,128)(2,1)S(1)}, bf16[8,512,128]{2,1,0:T(8,128)(2,1)S(1)}, f32[8,128]{1,0:T(8,128)S(1)}) custom-call(s32[5]{0:T(128)S(1)} %stack.50.place, bf16[128,1024]{1,0:T(8,128)(2,1)S(1)} %copy-done.5, bf16[128,512]{1,0:T(8,128)(2,1)S(1)} %copy-done.6, s32[1,128]{1,0:T(1,128)S(1)} %bitcast.24, ...), custom_call_target="tpu_custom_call" | custom-call | flops 700000000 | bytes 3145728 | tf_op jit(solution)/shard_map/queries/pallas_call | solution.py:390
  47.7 1.2 collective-permute-done.12.low_in
  48.9 2.0 %collective-permute-done.13.high_in = bf16[2,128,640]{2,1,0:T(8,128)(2,1)S(1)} collective-permute-done((bf16[2,128,640]{2,1,0:T(8,128)(2,1)S(1)}, bf16[2,128,640]{2,1,0:T(8,128)(2,1)S(1)}, u32[]{:S(2)}, u32[]{:S(2)}) %collective-permute-start.13) | collective-permute-done | bytes 327712 | tf_op jit(solution)/shard_map/ppermute | solution.py:31
  50.9 0.3 gate.1
  51.3 1.9 %collective-permute-start.15 = (bf16[2,128,640]{2,1,0:T(8,128)(2,1)S(1)}, bf16[2,128,640]{2,1,0:T(8,128)(2,1)S(1)}, u32[]{:S(2)}, u32[]{:S(2)}) collective-permute-start(bf16[2,128,640]{2,1,0:T(8,128)(2,1)S(1)} %get-tuple-element.39.rest_1_), channel_id=1, source_target_pairs={{0,8},{1,9},{2,10},{3,11},{4,12},{5,13},{6,14},{7,15},{8,0},{9,1},... | collective-permute-start | bytes 983048 | tf_op jit(solution)/shard_map/ppermute | solution.py:31
  53.2 2.7 %collective-permute-start.17 = (bf16[224,1024]{1,0:T(8,128)(2,1)S(1)}, bf16[224,1024]{1,0:T(8,128)(2,1)S(1)}, u32[]{:S(2)}, u32[]{:S(2)}) collective-permute-start(bf16[224,1024]{1,0:T(8,128)(2,1)S(1)} %get-tuple-element.42.weight_in.rest_0_), channel_id=1, source_target_pairs={{0,64},{1,65},{2,66},{3,67},{4,68},{5,69},{6,70},{7,71},{8,72},{9,... | collective-permute-start | bytes 1376264 | tf_op jit(solution)/shard_map/ppermute | solution.py:31
  55.9 7.1 %attention.1 = (bf16[1024,128]{1,0:T(8,128)(2,1)S(1)}, f32[8,128]{1,0:T(8,128)}) custom-call(s32[5]{0:T(128)S(1)} %stack.50.place, bf16[1024,640]{1,0:T(8,128)(2,1)S(1)} %get-tuple-element.33.query, bf16[8,512,128]{2,1,0:T(8,128)(2,1)S(1)} %get-tuple-element.34.up_value, bf16[12,128,640]{2,1,0:T(8,128)(2,1)} %get-tuple-element.35.rest_0_, ...), custom_call_target="tpu_custom_call" | custom-call | flops 10000000000 | bytes 3145728 | tf_op jit(solution)/shard_map/attention/pallas_call | solution.py:419
  63.1 9.5 %collective-permute-done.17.first.rest_1_ = bf16[224,1024]{1,0:T(8,128)(2,1)S(1)} collective-permute-done((bf16[224,1024]{1,0:T(8,128)(2,1)S(1)}, bf16[224,1024]{1,0:T(8,128)(2,1)S(1)}, u32[]{:S(2)}, u32[]{:S(2)}) %collective-permute-start.17) | collective-permute-done | bytes 458784 | tf_op jit(solution)/shard_map/ppermute | solution.py:31
  72.6 1.9 %collective-permute-done.18.second.rest_2_ = bf16[224,1024]{1,0:T(8,128)(2,1)S(1)} collective-permute-done((bf16[224,1024]{1,0:T(8,128)(2,1)S(1)}, bf16[224,1024]{1,0:T(8,128)(2,1)S(1)}, u32[]{:S(2)}, u32[]{:S(2)}) %collective-permute-start.18) | collective-permute-done | bytes 458784 | tf_op jit(solution)/shard_map/ppermute | solution.py:31
  74.5 3.1 %collective-permute-start.22 = (bf16[224,1024]{1,0:T(8,128)(2,1)S(1)}, bf16[224,1024]{1,0:T(8,128)(2,1)S(1)}, u32[]{:S(2)}, u32[]{:S(2)}) collective-permute-start(bf16[224,1024]{1,0:T(8,128)(2,1)S(1)} %get-tuple-element.44), channel_id=1, source_target_pairs={{0,192},{1,193},{2,194},{3,195},{4,196},{5,197},{6,198},{7,199},{8... | collective-permute-start | bytes 1376264 | tf_op jit(solution)/shard_map/ppermute | solution.py:31
  77.7 0.3 collective-permute-start.19
  78.0 1.2 collective-permute-start.20
  79.2 0.5 collective-permute-start.21
  79.6 4.5 %collective-permute-done.19.refs_1_ = bf16[1024,128]{1,0:T(8,128)(2,1)S(1)} collective-permute-done((bf16[1024,128]{1,0:T(8,128)(2,1)S(1)}, bf16[1024,128]{1,0:T(8,128)(2,1)S(1)}, u32[]{:S(2)}, u32[]{:S(2)}) %collective-permute-start.19) | collective-permute-done | bytes 262176 | tf_op jit(solution)/shard_map/ppermute | solution.py:31
  84.2 1.6 %collective-permute-done.20.refs_2_ = bf16[1024,128]{1,0:T(8,128)(2,1)S(1)} collective-permute-done((bf16[1024,128]{1,0:T(8,128)(2,1)S(1)}, bf16[1024,128]{1,0:T(8,128)(2,1)S(1)}, u32[]{:S(2)}, u32[]{:S(2)}) %collective-permute-start.20) | collective-permute-done | bytes 262176 | tf_op jit(solution)/shard_map/ppermute | solution.py:31
  85.8 7.5 %collective-permute-done.21.refs_3_ = bf16[1024,128]{1,0:T(8,128)(2,1)S(1)} collective-permute-done((bf16[1024,128]{1,0:T(8,128)(2,1)S(1)}, bf16[1024,128]{1,0:T(8,128)(2,1)S(1)}, u32[]{:S(2)}, u32[]{:S(2)}) %collective-permute-start.21) | collective-permute-done | bytes 262176 | tf_op jit(solution)/shard_map/ppermute | solution.py:31
  93.3 4.1 %collective-permute-done.22.refs_4_.rest_3_ = bf16[224,1024]{1,0:T(8,128)(2,1)S(1)} collective-permute-done((bf16[224,1024]{1,0:T(8,128)(2,1)S(1)}, bf16[224,1024]{1,0:T(8,128)(2,1)S(1)}, u32[]{:S(2)}, u32[]{:S(2)}) %collective-permute-start.22) | collective-permute-done | bytes 458784 | tf_op jit(solution)/shard_map/ppermute | solution.py:31
  97.5 1.7 %collective-permute-start.23 = (bf16[4,1024,128]{2,1,0:T(8,128)(2,1)S(1)}, bf16[4,1024,128]{2,1,0:T(8,128)(2,1)}, u32[]{:S(2)}, u32[]{:S(2)}) collective-permute-start(bf16[4,1024,128]{2,1,0:T(8,128)(2,1)S(1)} %third.1.mine), channel_id=1, source_target_pairs={{0,8},{1,9},{2,10},{3,11},{4,12},{5,13},{6,14},{7,15},{8,0},{9,1},... | collective-permute-start | bytes 3145736 | tf_op jit(solution)/shard_map/ppermute | solution.py:31
  99.2 2.3 %collective-permute-done.23.theirs = bf16[4,1024,128]{2,1,0:T(8,128)(2,1)} collective-permute-done((bf16[4,1024,128]{2,1,0:T(8,128)(2,1)S(1)}, bf16[4,1024,128]{2,1,0:T(8,128)(2,1)}, u32[]{:S(2)}, u32[]{:S(2)}) %collective-permute-start.23) | collective-permute-done | bytes 1048608 | tf_op jit(solution)/shard_map/ppermute | solution.py:31
  101.5 4.4 %project.1 = (bf16[2,224,256]{2,1,0:T(8,128)(2,1)S(1)}, bf16[2,224,256]{2,1,0:T(8,128)(2,1)S(1)}, bf16[2,224,256]{2,1,0:T(8,128)(2,1)S(1)}, bf16[2,224,256]{2,1,...) custom-call(s32[6]{0:T(128)S(1)} %stack.48.place, ...), custom_call_target="tpu_custom_call" | custom-call | flops 1880000000 | bytes 3145728 | tf_op jit(solution)/shard_map/project/pallas_call | solution.py:448
  106.0 1.4 collective-permute-start.27
  107.4 0.2 collective-permute-start.25
  107.5 1.5 %collective-permute-start.29 = (bf16[2,224,256]{2,1,0:T(8,128)(2,1)S(1)}, bf16[2,224,256]{2,1,0:T(8,128)(2,1)S(1)}, u32[]{:S(2)}, u32[]{:S(2)}) collective-permute-start(bf16[2,224,256]{2,1,0:T(8,128)(2,1)S(1)} %get-tuple-element.52), channel_id=1, source_target_pairs={{0,3},{1,0},{2,1},{3,2},{4,7},{5,4},{6,5},{7,6},{8,11},{9,8},{10,9... | collective-permute-start | bytes 688136 | tf_op jit(solution)/shard_map/ppermute | solution.py:31
  109.1 3.8 %collective-permute-done.27 = bf16[2,224,256]{2,1,0:T(8,128)(2,1)S(1)} collective-permute-done((bf16[2,224,256]{2,1,0:T(8,128)(2,1)S(1)}, bf16[2,224,256]{2,1,0:T(8,128)(2,1)S(1)}, u32[]{:S(2)}, u32[]{:S(2)}) %collective-permute-start.27) | collective-permute-done | bytes 229408 | tf_op jit(solution)/shard_map/ppermute | solution.py:31
  113.0 1.4 collective-permute-start.28
  114.3 1.0 collective-permute-start.24
  115.4 0.5 collective-permute-start.26
  115.9 2.8 %collective-permute-done.29.right = bf16[2,224,256]{2,1,0:T(8,128)(2,1)S(1)} collective-permute-done((bf16[2,224,256]{2,1,0:T(8,128)(2,1)S(1)}, bf16[2,224,256]{2,1,0:T(8,128)(2,1)S(1)}, u32[]{:S(2)}, u32[]{:S(2)}) %collective-permute-start.29) | collective-permute-done | bytes 229408 | tf_op jit(solution)/shard_map/ppermute | solution.py:31
  118.8 0.2 collective-permute-done.28.left
  119.1 2.2 %collective-permute-start.30 = (bf16[2,224,256]{2,1,0:T(8,128)(2,1)S(1)}, bf16[2,224,256]{2,1,0:T(8,128)(2,1)S(1)}, u32[]{:S(2)}, u32[]{:S(2)}) collective-permute-start(bf16[2,224,256]{2,1,0:T(8,128)(2,1)S(1)} %sums.1), channel_id=1, source_target_pairs={{0,4},{1,5},{2,6},{3,7},{4,0},{5,1},{6,2},{7,3},{8,12},{9,13},{10,... | collective-permute-start | bytes 688136 | tf_op jit(solution)/shard_map/ppermute | solution.py:31
  121.3 2.6 %collective-permute-done.24.left = bf16[2,224,256]{2,1,0:T(8,128)(2,1)S(1)} collective-permute-done((bf16[2,224,256]{2,1,0:T(8,128)(2,1)S(1)}, bf16[2,224,256]{2,1,0:T(8,128)(2,1)S(1)}, u32[]{:S(2)}, u32[]{:S(2)}) %collective-permute-start.24) | collective-permute-done | bytes 229408 | tf_op jit(solution)/shard_map/ppermute | solution.py:31
  123.9 6.5 %collective-permute-done.30.arrived = bf16[2,224,256]{2,1,0:T(8,128)(2,1)S(1)} collective-permute-done((bf16[2,224,256]{2,1,0:T(8,128)(2,1)S(1)}, bf16[2,224,256]{2,1,0:T(8,128)(2,1)S(1)}, u32[]{:S(2)}, u32[]{:S(2)}) %collective-permute-start.30) | collective-permute-done | bytes 229408 | tf_op jit(solution)/shard_map/ppermute | solution.py:31
  130.5 0.8 settle.1
  131.2 5.6 %collective-permute-start.31 = (bf16[224,128]{1,0:T(8,128)(2,1)S(1)}, bf16[224,128]{1,0:T(8,128)(2,1)S(1)}, u32[]{:S(2)}, u32[]{:S(2)}) collective-permute-start(bf16[224,128]{1,0:T(8,128)(2,1)S(1)} %get-tuple-element.53), channel_id=1, source_target_pairs={{0,0},{1,32},{2,2},{3,34},{4,4},{5,36},{6,6},{7,38},{8,8},{9,40},{... | collective-permute-start | bytes 172040 | tf_op jit(solution)/shard_map/ppermute | solution.py:31
  136.8 3.1 %collective-permute-start.32 = (bf16[224,128]{1,0:T(8,128)(2,1)S(1)}, bf16[224,128]{1,0:T(8,128)(2,1)S(1)}, u32[]{:S(2)}, u32[]{:S(2)}) collective-permute-start(bf16[224,128]{1,0:T(8,128)(2,1)S(1)} %get-tuple-element.54), channel_id=1, source_target_pairs={{0,8},{1,40},{2,10},{3,42},{4,12},{5,44},{6,14},{7,46},{8,0},{9,32... | collective-permute-start | bytes 172040 | tf_op jit(solution)/shard_map/ppermute | solution.py:31
  139.9 3.0 %collective-permute-start.33 = (bf16[224,128]{1,0:T(8,128)(2,1)S(1)}, bf16[224,128]{1,0:T(8,128)(2,1)S(1)}, u32[]{:S(2)}, u32[]{:S(2)}) collective-permute-start(bf16[224,128]{1,0:T(8,128)(2,1)S(1)} %get-tuple-element.55), channel_id=1, source_target_pairs={{0,16},{1,48},{2,18},{3,50},{4,20},{5,52},{6,22},{7,54},{8,24},{9,... | collective-permute-start | bytes 172040 | tf_op jit(solution)/shard_map/ppermute | solution.py:31
  142.9 0.7 collective-permute-start.34
  143.6 3.0 %collective-permute-done.33.rest_2_ = bf16[224,128]{1,0:T(8,128)(2,1)S(1)} collective-permute-done((bf16[224,128]{1,0:T(8,128)(2,1)S(1)}, bf16[224,128]{1,0:T(8,128)(2,1)S(1)}, u32[]{:S(2)}, u32[]{:S(2)}) %collective-permute-start.33) | collective-permute-done | bytes 57376 | tf_op jit(solution)/shard_map/ppermute | solution.py:31
  146.6 2.1 %collective-permute-done.34.rest_3_ = bf16[224,128]{1,0:T(8,128)(2,1)S(1)} collective-permute-done((bf16[224,128]{1,0:T(8,128)(2,1)S(1)}, bf16[224,128]{1,0:T(8,128)(2,1)S(1)}, u32[]{:S(2)}, u32[]{:S(2)}) %collective-permute-start.34) | collective-permute-done | bytes 57376 | tf_op jit(solution)/shard_map/ppermute | solution.py:31
  148.6 1.4 finish.1
  (38 shorter events, 0.9 us)
Async XLA Ops:
  0.6 0.9 copy-start.1
  1.5 0.7 copy-start.2
  2.3 0.7 copy-start.3
  3.1 13.2 %collective-permute-start = (bf16[128,640]{1,0:T(8,128)(2,1)S(1)}, bf16[128,640]{1,0:T(8,128)(2,1)S(1)}, u32[]{:S(2)}, u32[]{:S(2)}) collective-permute-start(bf16[128,640]{1,0:T(8,128)(2,1)S(1)} %keys.1.refs_0_), channel_id=1, source_target_pairs={{0,48},{1,49},{2,50},{3,51},{4,52},{5,53},{6,54},{7,55},{8,56},{9,... | collective-permute-start | bytes 491528 | tf_op jit(solution)/shard_map/ppermute | solution.py:31
  5.7 10.7 %collective-permute-start.1 = (bf16[128,640]{1,0:T(8,128)(2,1)S(1)}, bf16[128,640]{1,0:T(8,128)(2,1)S(1)}, u32[]{:S(2)}, u32[]{:S(2)}) collective-permute-start(bf16[128,640]{1,0:T(8,128)(2,1)S(1)} %keys.1.refs_0_), channel_id=1, source_target_pairs={{0,32},{1,33},{2,34},{3,35},{4,36},{5,37},{6,38},{7,39},{8,40},{9,... | collective-permute-start | bytes 491528 | tf_op jit(solution)/shard_map/ppermute | solution.py:31
  6.2 10.6 %collective-permute-start.2 = (bf16[128,640]{1,0:T(8,128)(2,1)S(1)}, bf16[128,640]{1,0:T(8,128)(2,1)S(1)}, u32[]{:S(2)}, u32[]{:S(2)}) collective-permute-start(bf16[128,640]{1,0:T(8,128)(2,1)S(1)} %keys.1.refs_0_), channel_id=1, source_target_pairs={{0,16},{1,17},{2,18},{3,19},{4,20},{5,21},{6,22},{7,23},{8,24},{9,... | collective-permute-start | bytes 491528 | tf_op jit(solution)/shard_map/ppermute | solution.py:31
  7.6 34.7 %copy-start.4 = (s32[128]{0:T(128)S(1)}, s32[128]{0:T(128)}, u32[]{:S(2)}) copy-start(s32[128]{0:T(128)} %param.12) | copy-start | bytes 1540
  7.6 37.1 %copy-start.5 = (bf16[128,1024]{1,0:T(8,128)(2,1)S(1)}, bf16[128,1024]{1,0:T(8,128)(2,1)}, u32[]{:S(2)}) copy-start(bf16[128,1024]{1,0:T(8,128)(2,1)} %q_nope_in.1) | copy-start | bytes 786436
  7.6 37.1 %copy-start.6 = (bf16[128,512]{1,0:T(8,128)(2,1)S(1)}, bf16[128,512]{1,0:T(8,128)(2,1)}, u32[]{:S(2)}) copy-start(bf16[128,512]{1,0:T(8,128)(2,1)} %q_rope_in.1) | copy-start | bytes 393220
  7.6 3.2 %collective-permute-start.3 = (bf16[16,16,128]{2,1,0:T(8,128)(2,1)S(1)}, bf16[16,16,128]{2,1,0:T(8,128)(2,1)S(1)}, u32[]{:S(2)}, u32[]{:S(2)}) collective-permute-start(bf16[16,16,128]{2,1,0:T(8,128)(2,1)S(1)} %pad_maximum_fusion.refs_4_), channel_id=1, source_target_pairs={{0,64},{1,65},{2,66},{3,67},{4,68},{5,69},{6,70},{7,71},{8,72},{9,... | collective-permute-start | bytes 196616 | tf_op jit(solution)/shard_map/ppermute | solution.py:31
  7.7 5.6 %collective-permute-start.4 = (bf16[16,16,128]{2,1,0:T(8,128)(2,1)S(1)}, bf16[16,16,128]{2,1,0:T(8,128)(2,1)S(1)}, u32[]{:S(2)}, u32[]{:S(2)}) collective-permute-start(bf16[16,16,128]{2,1,0:T(8,128)(2,1)S(1)} %pad_maximum_fusion.refs_4_), channel_id=1, source_target_pairs={{0,128},{1,129},{2,130},{3,131},{4,132},{5,133},{6,134},{7,135},{8... | collective-permute-start | bytes 196616 | tf_op jit(solution)/shard_map/ppermute | solution.py:31
  10.8 5.5 %collective-permute-start.5 = (bf16[16,16,128]{2,1,0:T(8,128)(2,1)S(1)}, bf16[16,16,128]{2,1,0:T(8,128)(2,1)S(1)}, u32[]{:S(2)}, u32[]{:S(2)}) collective-permute-start(bf16[16,16,128]{2,1,0:T(8,128)(2,1)S(1)} %pad_maximum_fusion.refs_4_), channel_id=1, source_target_pairs={{0,192},{1,193},{2,194},{3,195},{4,196},{5,197},{6,198},{7,199},{8... | collective-permute-start | bytes 196616 | tf_op jit(solution)/shard_map/ppermute | solution.py:31
  16.9 17.8 %collective-permute-start.6 = (bf16[4,128,640]{2,1,0:T(8,128)(2,1)S(1)}, bf16[4,128,640]{2,1,0:T(8,128)(2,1)S(1)}, u32[]{:S(2)}, u32[]{:S(2)}) collective-permute-start(bf16[4,128,640]{2,1,0:T(8,128)(2,1)S(1)} %get-tuple-element.30.row), channel_id=1, source_target_pairs={{0,196},{1,197},{2,198},{3,199},{4,192},{5,193},{6,194},{7,195},{8... | collective-permute-start | bytes 1966088 | tf_op jit(solution)/shard_map/ppermute | solution.py:31
  17.3 17.5 %collective-permute-start.7 = (bf16[4,128,640]{2,1,0:T(8,128)(2,1)S(1)}, bf16[4,128,640]{2,1,0:T(8,128)(2,1)S(1)}, u32[]{:S(2)}, u32[]{:S(2)}) collective-permute-start(bf16[4,128,640]{2,1,0:T(8,128)(2,1)S(1)} %get-tuple-element.30.row), channel_id=1, source_target_pairs={{0,64},{1,65},{2,66},{3,67},{4,68},{5,69},{6,70},{7,71},{8,72},{9,... | collective-permute-start | bytes 1966088 | tf_op jit(solution)/shard_map/ppermute | solution.py:31
  18.7 5.7 %collective-permute-start.8 = (bf16[4,16,16,128]{3,2,1,0:T(8,128)(2,1)S(1)}, bf16[4,16,16,128]{3,2,1,0:T(8,128)(2,1)S(1)}, u32[]{:S(2)}, u32[]{:S(2)}) collective-permute-start(bf16[4,16,16,128]{3,2,1,0:T(8,128)(2,1)S(1)} %get-tuple-element.31.rest_0_), channel_id=1, source_target_pairs={{0,48},{1,49},{2,50},{3,51},{4,52},{5,53},{6,54},{7,55},{8,56},{9,... | collective-permute-start | bytes 786440 | tf_op jit(solution)/shard_map/ppermute | solution.py:31
  20.4 6.8 %collective-permute-start.9 = (bf16[4,16,16,128]{3,2,1,0:T(8,128)(2,1)S(1)}, bf16[4,16,16,128]{3,2,1,0:T(8,128)(2,1)S(1)}, u32[]{:S(2)}, u32[]{:S(2)}) collective-permute-start(bf16[4,16,16,128]{3,2,1,0:T(8,128)(2,1)S(1)} %get-tuple-element.31.rest_0_), channel_id=1, source_target_pairs={{0,32},{1,33},{2,34},{3,35},{4,36},{5,37},{6,38},{7,39},{8,40},{9,... | collective-permute-start | bytes 786440 | tf_op jit(solution)/shard_map/ppermute | solution.py:31
  21.6 13.1 %collective-permute-start.10 = (bf16[4,16,16,128]{3,2,1,0:T(8,128)(2,1)S(1)}, bf16[4,16,16,128]{3,2,1,0:T(8,128)(2,1)S(1)}, u32[]{:S(2)}, u32[]{:S(2)}) collective-permute-start(bf16[4,16,16,128]{3,2,1,0:T(8,128)(2,1)S(1)} %get-tuple-element.31.rest_0_), channel_id=1, source_target_pairs={{0,16},{1,17},{2,18},{3,19},{4,20},{5,21},{6,22},{7,23},{8,24},{9,... | collective-permute-start | bytes 786440 | tf_op jit(solution)/shard_map/ppermute | solution.py:31
  36.3 14.6 %copy-start = (bf16[1024,224]{0,1:T(8,128)(2,1)S(1)}, bf16[1024,224]{0,1:T(8,128)(2,1)}, u32[]{:S(2)}) copy-start(bf16[1024,224]{0,1:T(8,128)(2,1)} %param.15) | copy-start | bytes 1376260
  36.3 19.6 %collective-permute-start.14 = (bf16[12,128,640]{2,1,0:T(8,128)(2,1)}, bf16[12,128,640]{2,1,0:T(8,128)(2,1)}, u32[]{:S(2)}, u32[]{:S(2)}) collective-permute-start(bf16[12,128,640]{2,1,0:T(8,128)(2,1)} %get-tuple-element.35.rest_0_), channel_id=1, source_target_pairs={{0,8},{1,9},{2,10},{3,11},{4,12},{5,13},{6,14},{7,15},{8,0},{9,1},... | collective-permute-start | bytes 5898248 | tf_op jit(solution)/shard_map/ppermute | solution.py:31
  39.7 5.1 %collective-permute-start.11 = (bf16[4,4,16,16,128]{4,3,2,1,0:T(8,128)(2,1)S(1)}, bf16[4,4,16,16,128]{4,3,2,1,0:T(8,128)(2,1)}, u32[]{:S(2)}, u32[]{:S(2)}) collective-permute-start(bf16[4,4,16,16,128]{4,3,2,1,0:T(8,128)(2,1)S(1)} %get-tuple-element.32.mine), channel_id=1, source_target_pairs={{0,8},{1,9},{2,10},{3,11},{4,12},{5,13},{6,14},{7,15},{8,0},{9,1},... | collective-permute-start | bytes 3145736 | tf_op jit(solution)/shard_map/ppermute | solution.py:31
  39.7 9.2 %collective-permute-start.12 = (bf16[2,128,640]{2,1,0:T(8,128)(2,1)S(1)}, bf16[2,128,640]{2,1,0:T(8,128)(2,1)S(1)}, u32[]{:S(2)}, u32[]{:S(2)}) collective-permute-start(bf16[2,128,640]{2,1,0:T(8,128)(2,1)S(1)} %get-tuple-element.36), channel_id=1, source_target_pairs={{0,196},{1,197},{2,198},{3,199},{4,192},{5,193},{6,194},{7,195},{8... | collective-permute-start | bytes 983048 | tf_op jit(solution)/shard_map/ppermute | solution.py:31
  42.3 8.6 %collective-permute-start.13 = (bf16[2,128,640]{2,1,0:T(8,128)(2,1)S(1)}, bf16[2,128,640]{2,1,0:T(8,128)(2,1)S(1)}, u32[]{:S(2)}, u32[]{:S(2)}) collective-permute-start(bf16[2,128,640]{2,1,0:T(8,128)(2,1)S(1)} %get-tuple-element.37), channel_id=1, source_target_pairs={{0,64},{1,65},{2,66},{3,67},{4,68},{5,69},{6,70},{7,71},{8,72},{9,... | collective-permute-start | bytes 983048 | tf_op jit(solution)/shard_map/ppermute | solution.py:31
  51.3 4.7 %collective-permute-start.15 = (bf16[2,128,640]{2,1,0:T(8,128)(2,1)S(1)}, bf16[2,128,640]{2,1,0:T(8,128)(2,1)S(1)}, u32[]{:S(2)}, u32[]{:S(2)}) collective-permute-start(bf16[2,128,640]{2,1,0:T(8,128)(2,1)S(1)} %get-tuple-element.39.rest_1_), channel_id=1, source_target_pairs={{0,8},{1,9},{2,10},{3,11},{4,12},{5,13},{6,14},{7,15},{8,0},{9,1},... | collective-permute-start | bytes 983048 | tf_op jit(solution)/shard_map/ppermute | solution.py:31
  53.1 2.8 %collective-permute-start.16 = (bf16[2,128,640]{2,1,0:T(8,128)(2,1)S(1)}, bf16[2,128,640]{2,1,0:T(8,128)(2,1)S(1)}, u32[]{:S(2)}, u32[]{:S(2)}) collective-permute-start(bf16[2,128,640]{2,1,0:T(8,128)(2,1)S(1)} %get-tuple-element.40.rest_2_), channel_id=1, source_target_pairs={{0,8},{1,9},{2,10},{3,11},{4,12},{5,13},{6,14},{7,15},{8,0},{9,1},... | collective-permute-start | bytes 983048 | tf_op jit(solution)/shard_map/ppermute | solution.py:31
  53.2 19.3 %collective-permute-start.17 = (bf16[224,1024]{1,0:T(8,128)(2,1)S(1)}, bf16[224,1024]{1,0:T(8,128)(2,1)S(1)}, u32[]{:S(2)}, u32[]{:S(2)}) collective-permute-start(bf16[224,1024]{1,0:T(8,128)(2,1)S(1)} %get-tuple-element.42.weight_in.rest_0_), channel_id=1, source_target_pairs={{0,64},{1,65},{2,66},{3,67},{4,68},{5,69},{6,70},{7,71},{8,72},{9,... | collective-permute-start | bytes 1376264 | tf_op jit(solution)/shard_map/ppermute | solution.py:31
  55.9 18.6 %collective-permute-start.18 = (bf16[224,1024]{1,0:T(8,128)(2,1)S(1)}, bf16[224,1024]{1,0:T(8,128)(2,1)S(1)}, u32[]{:S(2)}, u32[]{:S(2)}) collective-permute-start(bf16[224,1024]{1,0:T(8,128)(2,1)S(1)} %get-tuple-element.42.weight_in.rest_0_), channel_id=1, source_target_pairs={{0,128},{1,129},{2,130},{3,131},{4,132},{5,133},{6,134},{7,135},{8... | collective-permute-start | bytes 1376264 | tf_op jit(solution)/shard_map/ppermute | solution.py:31
  74.5 22.9 %collective-permute-start.22 = (bf16[224,1024]{1,0:T(8,128)(2,1)S(1)}, bf16[224,1024]{1,0:T(8,128)(2,1)S(1)}, u32[]{:S(2)}, u32[]{:S(2)}) collective-permute-start(bf16[224,1024]{1,0:T(8,128)(2,1)S(1)} %get-tuple-element.44), channel_id=1, source_target_pairs={{0,192},{1,193},{2,194},{3,195},{4,196},{5,197},{6,198},{7,199},{8... | collective-permute-start | bytes 1376264 | tf_op jit(solution)/shard_map/ppermute | solution.py:31
  77.7 6.5 %collective-permute-start.19 = (bf16[1024,128]{1,0:T(8,128)(2,1)S(1)}, bf16[1024,128]{1,0:T(8,128)(2,1)S(1)}, u32[]{:S(2)}, u32[]{:S(2)}) collective-permute-start(bf16[1024,128]{1,0:T(8,128)(2,1)S(1)} %get-tuple-element.43.refs_0_), channel_id=1, source_target_pairs={{0,48},{1,49},{2,50},{3,51},{4,52},{5,53},{6,54},{7,55},{8,56},{9,... | collective-permute-start | bytes 786440 | tf_op jit(solution)/shard_map/ppermute | solution.py:31
  78.0 7.8 %collective-permute-start.20 = (bf16[1024,128]{1,0:T(8,128)(2,1)S(1)}, bf16[1024,128]{1,0:T(8,128)(2,1)S(1)}, u32[]{:S(2)}, u32[]{:S(2)}) collective-permute-start(bf16[1024,128]{1,0:T(8,128)(2,1)S(1)} %get-tuple-element.43.refs_0_), channel_id=1, source_target_pairs={{0,32},{1,33},{2,34},{3,35},{4,36},{5,37},{6,38},{7,39},{8,40},{9,... | collective-permute-start | bytes 786440 | tf_op jit(solution)/shard_map/ppermute | solution.py:31
  79.2 14.2 %collective-permute-start.21 = (bf16[1024,128]{1,0:T(8,128)(2,1)S(1)}, bf16[1024,128]{1,0:T(8,128)(2,1)S(1)}, u32[]{:S(2)}, u32[]{:S(2)}) collective-permute-start(bf16[1024,128]{1,0:T(8,128)(2,1)S(1)} %get-tuple-element.43.refs_0_), channel_id=1, source_target_pairs={{0,16},{1,17},{2,18},{3,19},{4,20},{5,21},{6,22},{7,23},{8,24},{9,... | collective-permute-start | bytes 786440 | tf_op jit(solution)/shard_map/ppermute | solution.py:31
  97.5 4.1 %collective-permute-start.23 = (bf16[4,1024,128]{2,1,0:T(8,128)(2,1)S(1)}, bf16[4,1024,128]{2,1,0:T(8,128)(2,1)}, u32[]{:S(2)}, u32[]{:S(2)}) collective-permute-start(bf16[4,1024,128]{2,1,0:T(8,128)(2,1)S(1)} %third.1.mine), channel_id=1, source_target_pairs={{0,8},{1,9},{2,10},{3,11},{4,12},{5,13},{6,14},{7,15},{8,0},{9,1},... | collective-permute-start | bytes 3145736 | tf_op jit(solution)/shard_map/ppermute | solution.py:31
  106.0 6.9 %collective-permute-start.27 = (bf16[2,224,256]{2,1,0:T(8,128)(2,1)S(1)}, bf16[2,224,256]{2,1,0:T(8,128)(2,1)S(1)}, u32[]{:S(2)}, u32[]{:S(2)}) collective-permute-start(bf16[2,224,256]{2,1,0:T(8,128)(2,1)S(1)} %get-tuple-element.51), channel_id=1, source_target_pairs={{0,1},{1,2},{2,3},{3,0},{4,5},{5,6},{6,7},{7,4},{8,9},{9,10},{10,1... | collective-permute-start | bytes 688136 | tf_op jit(solution)/shard_map/ppermute | solution.py:31
  107.4 8.0 %collective-permute-start.25 = (bf16[2,224,256]{2,1,0:T(8,128)(2,1)S(1)}, bf16[2,224,256]{2,1,0:T(8,128)(2,1)S(1)}, u32[]{:S(2)}, u32[]{:S(2)}) collective-permute-start(bf16[2,224,256]{2,1,0:T(8,128)(2,1)S(1)} %get-tuple-element.48), channel_id=1, source_target_pairs={{0,3},{1,0},{2,1},{3,2},{4,7},{5,4},{6,5},{7,6},{8,11},{9,8},{10,9... | collective-permute-start | bytes 688136 | tf_op jit(solution)/shard_map/ppermute | solution.py:31
  107.5 11.2 %collective-permute-start.29 = (bf16[2,224,256]{2,1,0:T(8,128)(2,1)S(1)}, bf16[2,224,256]{2,1,0:T(8,128)(2,1)S(1)}, u32[]{:S(2)}, u32[]{:S(2)}) collective-permute-start(bf16[2,224,256]{2,1,0:T(8,128)(2,1)S(1)} %get-tuple-element.52), channel_id=1, source_target_pairs={{0,3},{1,0},{2,1},{3,2},{4,7},{5,4},{6,5},{7,6},{8,11},{9,8},{10,9... | collective-permute-start | bytes 688136 | tf_op jit(solution)/shard_map/ppermute | solution.py:31
  113.0 6.1 %collective-permute-start.28 = (bf16[2,224,256]{2,1,0:T(8,128)(2,1)S(1)}, bf16[2,224,256]{2,1,0:T(8,128)(2,1)S(1)}, u32[]{:S(2)}, u32[]{:S(2)}) collective-permute-start(bf16[2,224,256]{2,1,0:T(8,128)(2,1)S(1)} %add.51), channel_id=1, source_target_pairs={{0,1},{1,2},{2,3},{3,0},{4,5},{5,6},{6,7},{7,4},{8,9},{9,10},{10,1... | collective-permute-start | bytes 688136 | tf_op jit(solution)/shard_map/ppermute | solution.py:31
  114.3 9.6 %collective-permute-start.24 = (bf16[2,224,256]{2,1,0:T(8,128)(2,1)S(1)}, bf16[2,224,256]{2,1,0:T(8,128)(2,1)S(1)}, u32[]{:S(2)}, u32[]{:S(2)}) collective-permute-start(bf16[2,224,256]{2,1,0:T(8,128)(2,1)S(1)} %get-tuple-element.46), channel_id=1, source_target_pairs={{0,1},{1,2},{2,3},{3,0},{4,5},{5,6},{6,7},{7,4},{8,9},{9,10},{10,1... | collective-permute-start | bytes 688136 | tf_op jit(solution)/shard_map/ppermute | solution.py:31
  115.4 8.5 %collective-permute-start.26 = (bf16[2,224,256]{2,1,0:T(8,128)(2,1)S(1)}, bf16[2,224,256]{2,1,0:T(8,128)(2,1)S(1)}, u32[]{:S(2)}, u32[]{:S(2)}) collective-permute-start(bf16[2,224,256]{2,1,0:T(8,128)(2,1)S(1)} %add.50), channel_id=1, source_target_pairs={{0,3},{1,0},{2,1},{3,2},{4,7},{5,4},{6,5},{7,6},{8,11},{9,8},{10,9... | collective-permute-start | bytes 688136 | tf_op jit(solution)/shard_map/ppermute | solution.py:31
  119.1 11.3 %collective-permute-start.30 = (bf16[2,224,256]{2,1,0:T(8,128)(2,1)S(1)}, bf16[2,224,256]{2,1,0:T(8,128)(2,1)S(1)}, u32[]{:S(2)}, u32[]{:S(2)}) collective-permute-start(bf16[2,224,256]{2,1,0:T(8,128)(2,1)S(1)} %sums.1), channel_id=1, source_target_pairs={{0,4},{1,5},{2,6},{3,7},{4,0},{5,1},{6,2},{7,3},{8,12},{9,13},{10,... | collective-permute-start | bytes 688136 | tf_op jit(solution)/shard_map/ppermute | solution.py:31
  131.2 12.4 %collective-permute-start.31 = (bf16[224,128]{1,0:T(8,128)(2,1)S(1)}, bf16[224,128]{1,0:T(8,128)(2,1)S(1)}, u32[]{:S(2)}, u32[]{:S(2)}) collective-permute-start(bf16[224,128]{1,0:T(8,128)(2,1)S(1)} %get-tuple-element.53), channel_id=1, source_target_pairs={{0,0},{1,32},{2,2},{3,34},{4,4},{5,36},{6,6},{7,38},{8,8},{9,40},{... | collective-permute-start | bytes 172040 | tf_op jit(solution)/shard_map/ppermute | solution.py:31
  136.8 6.8 %collective-permute-start.32 = (bf16[224,128]{1,0:T(8,128)(2,1)S(1)}, bf16[224,128]{1,0:T(8,128)(2,1)S(1)}, u32[]{:S(2)}, u32[]{:S(2)}) collective-permute-start(bf16[224,128]{1,0:T(8,128)(2,1)S(1)} %get-tuple-element.54), channel_id=1, source_target_pairs={{0,8},{1,40},{2,10},{3,42},{4,12},{5,44},{6,14},{7,46},{8,0},{9,32... | collective-permute-start | bytes 172040 | tf_op jit(solution)/shard_map/ppermute | solution.py:31
  139.9 6.6 %collective-permute-start.33 = (bf16[224,128]{1,0:T(8,128)(2,1)S(1)}, bf16[224,128]{1,0:T(8,128)(2,1)S(1)}, u32[]{:S(2)}, u32[]{:S(2)}) collective-permute-start(bf16[224,128]{1,0:T(8,128)(2,1)S(1)} %get-tuple-element.55), channel_id=1, source_target_pairs={{0,16},{1,48},{2,18},{3,50},{4,20},{5,52},{6,22},{7,54},{8,24},{9,... | collective-permute-start | bytes 172040 | tf_op jit(solution)/shard_map/ppermute | solution.py:31
  142.9 5.7 %collective-permute-start.34 = (bf16[224,128]{1,0:T(8,128)(2,1)S(1)}, bf16[224,128]{1,0:T(8,128)(2,1)S(1)}, u32[]{:S(2)}, u32[]{:S(2)}) collective-permute-start(bf16[224,128]{1,0:T(8,128)(2,1)S(1)} %get-tuple-element.56), channel_id=1, source_target_pairs={{0,24},{1,56},{2,26},{3,58},{4,28},{5,60},{6,30},{7,62},{8,16},{9,... | collective-permute-start | bytes 172040 | tf_op jit(solution)/shard_map/ppermute | solution.py:31
where the time goes:
time: 150 us
  waiting for transfers between devices  75.4 us (50%)
  starting transfers between devices  51.3 us (34%)
  Pallas kernels  19.1 us (13%)
  local copies, waits for them, and re-layouts  2.49 us (2%)
    ppermute x35, waiting for transfers between devices, moved(): return lax.ppermute(array, AXES, pairs)  75.4 us
    ppermute x35, starting transfers between devices, moved(): return lax.ppermute(array, AXES, pairs)  51.3 us
    pallas_call x1, Pallas kernels, per_device(): call(attention_kernel, [((1024, 128), jnp.bfloat16), ((8, 128), jnp.float...  7.14 us
    pallas_call x1, Pallas kernels, per_device(): call(project_kernel, [((2, 224, 256), jnp.bfloat16)] * 8, [SMEM] + [VMEM]...  4.45 us
  transfers between devices with their start and end apart: 35, of which 23 were waited for; matrix products, arithmetic and copies ran while one was open for 1% of the time, Pallas kernels for 7%

commit v1 on v0

--- a/solution.py
+++ b/solution.py
@@ -55,14 +55,10 @@
     return (z, x, 1 - core, half, y)
 
 
-def other_half(z, x, core, half, y):
-    return (z, x, core, 1 - half, y)
-
-
-def settle(cross, swap):
+def settle(cross, over):
     def to(z, x, core, half, y):
         low = 1 - x % 2 if cross else x % 2
-        return (z, y % 2 * 2 + low, 1 - core if swap else core, half, y // 2 * 2 + x // 2)
+        return (z, y % 2 * 2 + low, core, 1 - half if over else half, y // 2 * 2 + x // 2)
 
     return to
 
@@ -127,24 +123,24 @@
         ups[n] = ring[n][...]
 
 
-def gate_kernel(weight_in, low_in, high_in, token, weight, low, high, sems):
-    copies = fetched([(weight_in, weight)], sems)
+def outer_kernel(right, left, low, high):
+    low[...] = right[0:512]
+    high[...] = left[512:1024]
+
+
+def gate_kernel(low_in, high_in, token, low, high):
     low[...] = low_in[...]
     high[...] = high_in[...]
-    for copy in copies:
-        copy.wait()
-
-
-def hold_kernel(values_in, weight_in, first, second, values, weight):
+
+
+def hold_kernel(values_in, weight, values):
     values[...] = values_in[...]
-    weight[...] = weight_in[...]
-
-
-def queries_kernel(
-    place, q_nope_in, q_rope_in, docs, mine, theirs, query, up_value, token, up_key, q_nope, q_rope, sems
-):
+
+
+def queries_kernel(place, q_nope_in, q_rope_in, weight_in, docs, mine, theirs, *rest):
+    query, up_value, weight, token, up_key, q_nope, q_rope, sems = rest
     token[...] = jnp.zeros((8, 128), jnp.float32)
-    copies = fetched([(q_nope_in, q_nope), (q_rope_in, q_rope)], sems)
+    copies = fetched([(q_nope_in, q_nope), (q_rope_in, q_rope), (weight_in, weight)], sems)
     z, x, core = place[0], place[1], place[2]
     row = lax.broadcasted_iota(jnp.int32, (512, 1), 0)
     position = row % 128 // 4
@@ -190,33 +186,23 @@
 
 
 def attention_kernel(place, query, up_value, *rest):
-    pieces, (values, log_sum, keys, score, total, peak, weighed, sems) = rest[:6], rest[6:]
+    pieces, (values, log_sum, keys, score, total, peak, weighed) = rest[:6], rest[6:]
     z, x, core = place[0], place[1], place[2]
     blocks = TILE // 128
     own_tile = lax.div(place[3], blocks)
 
-    def copy_of(source, block):
-        rows = pl.ds(pl.multiple_of(block * 128, 128), 128)
-        return pltpu.make_async_copy(source, keys.at[rows], sems.at[block])
-
     for side in range(2):
         twelve, two_low, two_high = pieces[side * 3 : side * 3 + 3]
         for dz, dx in [(a, b) for a in range(4) for b in range(4)]:
-            if dz == 2:
-                source = two_low.at[dx] if dx < 2 else two_high.at[dx - 2]
-            else:
-                source = twelve.at[{0: 0, 1: 4, 3: 8}[dz] + dx]
             block = (((z + dz) & 3) * 4 + ((x + dx) & 3)) * 2 + (core ^ side)
 
             @pl.when(block < (own_tile + 1) * blocks)
             def _():
-                copy_of(source, block).start()
-
-    def arrived(block):
-        copy_of(pieces[0].at[0], block).wait()
-
-    for n in range(blocks):
-        arrived(own_tile * blocks + n)
+                rows = pl.ds(pl.multiple_of(block * 128, 128), 128)
+                if dz == 2:
+                    keys[rows, :] = two_low[dx] if dx < 2 else two_high[dx - 2]
+                else:
+                    keys[rows, :] = twelve[{0: 0, 1: 4, 3: 8}[dz] + dx]
 
     def lane_groups(array, join):
         parts = [array[:, n * 128 : n * 128 + 128] for n in range(TILE // 128)]
@@ -256,7 +242,6 @@
         lax.fori_loop(low, own_tile, lambda tile, carry: (do(tile, False), carry)[1], 0)
 
     scores(own_tile, True)
-    lax.fori_loop(0, own_tile * blocks, lambda block, carry: (arrived(block), carry)[1], 0)
     lane = lax.broadcasted_iota(jnp.int32, (16, 128), 1)
     row_at = lax.broadcasted_iota(jnp.int32, (16, 128), 0)
     earlier = jnp.zeros((16, 128), jnp.float32)
@@ -279,20 +264,40 @@
     for h in range(8):
         rows = pl.ds(h * 128, 128)
         whole = jnp.sum(total[rows, :], axis=1, keepdims=True)
-        attended = (weighed[rows, :] / whole).astype(jnp.bfloat16)
+        attended = (weighed[rows, :] * (1.0 / whole)).astype(jnp.bfloat16)
         value = jnp.dot(attended, up_value[h], preferred_element_type=jnp.float32)
         values[h * 128 : h * 128 + 128, :] = jnp.transpose(value).astype(jnp.bfloat16)
         logs = jnp.where(column == h, peak[rows, :] * SCALE + jnp.log(whole), logs)
     log_sum[...] = jnp.transpose(logs)[0:8, :]
 
 
-def third_kernel(place, *refs):
-    for dx in range(4):
-        refs[5][(place[0] + dx) & 3] = refs[dx][...]
-
-
-def project_kernel(place, mine, theirs, *rest):
-    blocks, outs, (weights, sems) = rest[:4], rest[4:12], rest[12:]
+def third_kernel(place, own, right, left, low, high, *rest):
+    out = rest[-1]
+    for dx, array in ((0, own), (1, right), (3, left)):
+        out[(place[0] + dx) & 3] = array[...]
+    out[(place[0] + 2) & 3, 0:512] = low[...]
+    out[(place[0] + 2) & 3, 512:1024] = high[...]
+
+
+def project_kernel(wanted, place, mine, theirs, weights, outs):
+    for chip in sorted({chip for chip, _ in wanted}):
+        high, low = lax.div(place[1 + chip], 2), place[1 + chip] & 1
+        right = jnp.concatenate(
+            [mine[2 * low], theirs[2 * low], mine[2 * low + 1], theirs[2 * low + 1]], axis=1
+        )
+        halves = [half for other, half in wanted if other == chip]
+        weight = weights[high, halves[0] : halves[-1] + 1].reshape(224 * len(halves), 1024)
+        terms = jnp.dot(weight, right, preferred_element_type=jnp.float32).astype(jnp.bfloat16)
+        for n, half in enumerate(halves):
+            out = outs[wanted.index((chip, half))]
+            for low_bit in range(2):
+                out[low_bit] = terms[
+                    n * 224 : n * 224 + 224, low_bit * 256 : low_bit * 256 + 256
+                ]
+
+
+def first_terms_kernel(place, mine, theirs, *rest):
+    blocks, (far_give, left_give, weights, sems) = rest[:4], rest[4:]
     copies = []
     for dz in range(4):
         at = place[0] ^ dz
@@ -300,40 +305,52 @@
     copies = fetched(copies, sems)
     for copy in copies:
         copy.wait()
-    for n in range(4):
-        which = place[1 + n]
-        high, low = lax.div(which, 2), which & 1
-        right = jnp.concatenate(
-            [mine[2 * low], theirs[2 * low], mine[2 * low + 1], theirs[2 * low + 1]], axis=1
-        )
-        weight = weights[high].reshape(448, 1024)
-        terms = jnp.dot(weight, right, preferred_element_type=jnp.float32).astype(jnp.bfloat16)
-        for half in range(2):
-            for at in range(2):
-                outs[2 * n + half][at] = terms[
-                    half * 224 : half * 224 + 224, at * 256 : at * 256 + 256
-                ]
-
-
-def sum_kernel(own, left, right, out):
-    whole = own[...].astype(jnp.float32) + left[...].astype(jnp.float32)
-    out[...] = (whole + right[...].astype(jnp.float32)).astype(jnp.bfloat16)
-
-
-def settle_kernel(place, own, left, right, arrived, *rest):
-    outs, summed = rest[:4], rest[4]
-    whole = own[...].astype(jnp.float32) + left[...].astype(jnp.float32)
-    whole = whole + right[...].astype(jnp.float32) + arrived[...].astype(jnp.float32)
-    summed[...] = whole.astype(jnp.bfloat16)
-    for n in range(4):
-        outs[n][...] = summed[place[0] ^ (n // 2), :, n % 2 * 128 : n % 2 * 128 + 128]
-
-
-def finish_kernel(place, *rest):
-    arrays, (mixed, whole) = rest[:4], rest[4:]
-    for n in range(4):
-        at = (place[0] ^ (n // 2)) * 2 + (place[1] ^ (n % 2))
-        whole[at] = arrays[n][...].astype(jnp.float32)
+    project_kernel([(0, 0), (2, 0)], place, mine, theirs, weights, [far_give, left_give])
+
+
+def other_terms_kernel(place, mine, theirs, weights, out):
+    wanted = [(0, 1), (1, 0), (1, 1), (2, 1), (3, 0), (3, 1)]
+    project_kernel(wanted, place, mine, theirs, weights, [out.at[n] for n in range(6)])
+
+
+def summed(*arrays):
+    whole = arrays[0][...].astype(jnp.float32)
+    for array in arrays[1:]:
+        whole = whole + array[...].astype(jnp.float32)
+    return whole.astype(jnp.bfloat16)
+
+
+def early_kernel(terms, far_give, left_give, out, far_out):
+    out[...] = summed(terms.at[1], far_give)
+    far_out[...] = terms[0]
+
+
+def give_kernel(place, terms, left, right, far_keep, *outs):
+    same, cross, left_out, right_out, whole = outs
+    whole[...] = summed(terms.at[4], left, right)
+    same[...] = whole[place[0]]
+    cross[...] = whole[1 - place[0]]
+    left_out[...] = summed(terms.at[3], far_keep)
+    right_out[...] = terms[2]
+
+
+def keep_kernel(place, terms, left, right, same, cross, whole):
+    whole[...] = summed(terms.at[5], left, right)
+    same[...] = whole[place[0]]
+    cross[...] = whole[1 - place[0]]
+
+
+def halves_kernel(give_same, give_cross, keep_same, keep_cross, mine, theirs):
+    for cross, pair in enumerate(((keep_same, give_same), (keep_cross, give_cross))):
+        whole = summed(*pair)
+        mine[cross] = whole[:, 0:128]
+        theirs[cross] = whole[:, 128:256]
+
+
+def finish_kernel(place, mine, theirs, mixed, whole):
+    for cross in range(2):
+        for side, array in enumerate((mine, theirs)):
+            whole[(place[0] ^ cross) * 2 + (place[1] ^ side)] = array[cross].astype(jnp.float32)
     mixed[...] = jnp.transpose(whole[...].reshape(896, 128)).astype(jnp.bfloat16)
 
 
@@ -387,98 +404,116 @@
     pieces = [twelve, moved(low, along_z_ring(-1)), moved(high, along_z_ring(1))]
     theirs = moved(twelve, other_core)
 
-    query, up_value, token = call(
+    query, up_value, weight, token = call(
         queries_kernel,
         [
             ((1024, WIDE), jnp.bfloat16),
             ((8, KV_RANK, HEAD_DIM), jnp.bfloat16),
+            ((224, 1024), jnp.bfloat16),
             ((8, 128), jnp.float32),
         ],
-        [SMEM] + [HBM] * 2 + [VMEM] * 3,
+        [SMEM] + [HBM] * 3 + [VMEM] * 3,
         [
             pltpu.VMEM((8, HEAD_DIM, KV_RANK), jnp.bfloat16),
             pltpu.VMEM((128, 1024), jnp.bfloat16),
             pltpu.VMEM((128, 512), jnp.bfloat16),
-            pltpu.SemaphoreType.DMA((2,)),
+            pltpu.SemaphoreType.DMA((3,)),
         ],
         limit=16,
         flops=700_000_000,
         name="queries",
-    )(place, q_nope, q_rope, docs, ups, moved(ups, other_core))
-
-    weight, low, high = call(
+    )(place, q_nope, q_rope, w_out.T, docs, ups, moved(ups, other_core))
+
+    low, high = call(
         gate_kernel,
-        [((224, 1024), jnp.bfloat16)] + [((2, 128, WIDE), jnp.bfloat16)] * 2,
-        [HBM] + [VMEM] * 3,
-        [pltpu.SemaphoreType.DMA((1,))],
+        [((2, 128, WIDE), jnp.bfloat16)] * 2,
+        [VMEM] * 3,
         limit=8,
         name="gate",
-    )(w_out.T, *pieces[1:], token)
-    weights = [weight, moved(weight, flip_z(1)), moved(weight, flip_z(2))]
+    )(*pieces[1:], token)
+    weights = [weight] + [moved(weight, flip_z(bits)) for bits in (1, 2, 3)]
     pieces = [twelve, low, high, theirs, moved(low, other_core), moved(high, other_core)]
     values, log_sum = call(
         attention_kernel,
         [((1024, 128), jnp.bfloat16), ((8, 128), jnp.float32)],
-        [SMEM, VMEM, VMEM] + [ANY] * 6,
+        [SMEM] + [VMEM] * 8,
         [
             pltpu.VMEM((4096, WIDE), jnp.bfloat16),
             pltpu.VMEM((4096 // TILE, 1024, TILE), jnp.float32),
             pltpu.VMEM((1024, 128), jnp.float32),
             pltpu.VMEM((1024, 128), jnp.float32),
             pltpu.VMEM((1024, KV_RANK), jnp.float32),
-            pltpu.SemaphoreType.DMA((32,)),
         ],
         limit=32,
         flops=10_000_000_000,
         name="attention",
     )(place, query, up_value, *pieces)
 
-    values, weight = call(
-        hold_kernel,
-        [((1024, 128), jnp.bfloat16), ((224, 1024), jnp.bfloat16)],
-        [VMEM] * 4,
-        limit=8,
-        name="hold",
-    )(values, *weights)
-    weights.append(moved(weight, flip_z(3)))
+    (values,) = call(
+        hold_kernel, [((1024, 128), jnp.bfloat16)], [VMEM] * 2, limit=8, name="hold"
+    )(values, weights[1])
+    right, left = moved(values, along_x(-1)), moved(values, along_x(1))
+    low, high = call(
+        outer_kernel, [((512, 128), jnp.bfloat16)] * 2, [VMEM] * 2, limit=8, name="outer"
+    )(right, left)
+    low, high = moved(low, along_x(-1)), moved(high, along_x(1))
     (gathered,) = call(
-        third_kernel, [((4, 1024, 128), jnp.bfloat16)], [SMEM] + [VMEM] * 5, limit=8, name="third"
-    )(x.reshape(1).astype(jnp.int32), *gather_ring(values), weights[3])
-    order = [z, (y + 2) % 4, (y + 1) % 4, (y + 3) % 4, y, half]
-    terms = call(
-        project_kernel,
-        [((2, 224, 256), jnp.bfloat16)] * 8,
+        third_kernel, [((4, 1024, 128), jnp.bfloat16)], [SMEM] + [VMEM] * 7, limit=8, name="third"
+    )(x.reshape(1).astype(jnp.int32), values, right, left, low, high, *weights[2:])
+    order = jnp.stack([z, (y + 2) % 4, (y + 1) % 4, (y + 3) % 4, y, half]).astype(jnp.int32)
+    theirs = moved(gathered, other_core)
+    term, pair = ((2, 224, 256), jnp.bfloat16), [((224, 256), jnp.bfloat16)] * 2
+    far_give, left_give, held = call(
+        first_terms_kernel,
+        [term] * 2 + [((2, 2, 224, 1024), jnp.bfloat16)],
         [SMEM] + [VMEM] * 2 + [ANY] * 4,
-        [pltpu.VMEM((2, 2, 224, 1024), jnp.bfloat16), pltpu.SemaphoreType.DMA((4,))],
-        limit=24,
-        flops=1_880_000_000,
+        [pltpu.SemaphoreType.DMA((4,))],
+        limit=16,
+        flops=470_000_000,
         name="project",
-    )(jnp.stack(order).astype(jnp.int32), gathered, moved(gathered, other_core), *weights)
-    far, right, left, own = terms[0:2], terms[2:4], terms[4:6], terms[6:8]
-    far = moved(far[0], along_y(1)), moved(far[1], along_y(-1))
-    from_left = [moved(right[0] + far[0], along_y(1)), moved(right[1], along_y(1))]
-    from_right = [moved(left[0], along_y(-1)), moved(left[1] + far[1], along_y(-1))]
-    (give,) = call(
-        sum_kernel, [((2, 224, 256), jnp.bfloat16)], [VMEM] * 3, limit=16, name="sums"
-    )(own[0], from_left[0], from_right[0])
-    arrived = moved(give, other_half)
+    )(order, gathered, theirs, *weights)
+    (terms,) = call(
+        other_terms_kernel,
+        [((6, 2, 224, 256), jnp.bfloat16)],
+        [SMEM] + [VMEM] * 3,
+        limit=16,
+        flops=1_410_000_000,
+        name="others",
+    )(order, gathered, theirs, held)
     low = jnp.stack([x % 2, core]).astype(jnp.int32)
-    sums = call(
-        settle_kernel,
-        [((224, 128), jnp.bfloat16)] * 4,
+    left_give = moved(left_give, along_y(-1))
+    right_give, far_keep = call(
+        early_kernel, [term] * 2, [VMEM] * 3, limit=16, name="early"
+    )(terms, moved(far_give, along_y(1)), left_give)
+    same, cross, left_keep, right_keep = call(
+        give_kernel,
+        pair + [term] * 2,
         [SMEM] + [VMEM] * 4,
         [pltpu.VMEM((2, 224, 256), jnp.bfloat16)],
         limit=16,
-        name="settle",
-    )(low, own[1], from_left[1], from_right[1], arrived)
+        name="give",
+    )(low, terms, moved(right_give, along_y(1)), left_give, moved(far_keep, along_y(-1)))
+    give = [moved(same, settle(False, True)), moved(cross, settle(True, True))]
+    same, cross = call(
+        keep_kernel,
+        pair,
+        [SMEM] + [VMEM] * 3,
+        [pltpu.VMEM((2, 224, 256), jnp.bfloat16)],
+        limit=16,
+        name="keep",
+    )(low, terms, moved(right_keep, along_y(1)), moved(left_keep, along_y(-1)))
+    keep = [moved(same, settle(False, False)), moved(cross, settle(True, False))]
+    mine, theirs = call(
+        halves_kernel, [((2, 224, 128), jnp.bfloat16)] * 2, [VMEM] * 4, limit=16, name="halves"
+    )(*give, *keep)
     (mixed,) = call(
         finish_kernel,
         [((128, 896), jnp.bfloat16)],
-        [SMEM] + [VMEM] * 4,
+        [SMEM] + [VMEM] * 2,
         [pltpu.VMEM((4, 224, 128), jnp.float32)],
         limit=16,
         name="finish",
-    )(low, *[moved(term, settle(n // 2, n % 2)) for n, term in enumerate(sums)])
+    )(low, mine, moved(theirs, other_core))
     return (mixed, log_sum.T)
 
 

time: 150 us -> 149 us (level)
  waiting for transfers between devices: 75.4 us -> 69.7 us
  local copies, waits for them, and re-layouts: 2.49 us -> 6.03 us
  Pallas kernels: 19.1 us -> 21.1 us
    ppermute x35 -> x36, waiting for transfers between devices: 75.4 us -> 69.7 us  [moved(): return lax.ppermute(array, AXES, pairs)]
    unnamed x14 -> x22, local copies, waits for them, and re-layouts: 2.29 us -> 5.83 us
    pallas_call x1, Pallas kernels: 7.14 us -> 8.96 us  [per_device(): call(attention_kernel, [((1024, 128), jnp.bfloat16), ((8, 128), jnp.float...]
    ppermute x35 -> x36, starting transfers between devices: 51.3 us -> 50.2 us  [moved(): return lax.ppermute(array, AXES, pairs)]
    pallas_call x7 -> x11, Pallas kernels: 7.15 us -> 7.7 us  [the longest x1 2.35 us: per_device(): call(first_terms_kernel, [term] * 2 + [((2, 2, 224, 1024), jnp.bfloat16)]...]
  transfers between devices with their start and end apart: 35 -> 36, of which waited for: 23 -> 22; matrix products, arithmetic and copies ran while one was open for 1% -> 1% of each run, Pallas kernels for 7% -> 10%
where the time goes in v1:
time: 149 us
  waiting for transfers between devices  69.7 us (47%)
  starting transfers between devices  50.2 us (34%)
  Pallas kernels  21.1 us (14%)
  local copies, waits for them, and re-layouts  6.03 us (4%)
    ppermute x36, waiting for transfers between devices, moved(): return lax.ppermute(array, AXES, pairs)  69.7 us
    ppermute x36, starting transfers between devices, moved(): return lax.ppermute(array, AXES, pairs)  50.2 us
    pallas_call x1, Pallas kernels, per_device(): call(attention_kernel, [((1024, 128), jnp.bfloat16), ((8, 128), jnp.float...  8.96 us
    unnamed x22, local copies, waits for them, and re-layouts  5.83 us
  transfers between devices with their start and end apart: 36, of which 22 were waited for; matrix products, arithmetic and copies ran while one was open for 1% of the time, Pallas kernels for 10%

profile of v1, /device:TPU:41, one launch (start us, length us, event | category | flops | bytes accessed | tf_op | source)
XLA Modules:
  0.0 148.8 jit_solution(84892491660019780)
XLA Ops:
  0.6 0.9 copy-done.6
  1.5 0.7 copy-done.8
  2.3 0.7 copy-done.9
  3.1 2.6 %collective-permute-start = (bf16[128,640]{1,0:T(8,128)(2,1)S(1)}, bf16[128,640]{1,0:T(8,128)(2,1)S(1)}, u32[]{:S(2)}, u32[]{:S(2)}) collective-permute-start(bf16[128,640]{1,0:T(8,128)(2,1)S(1)} %keys.1.refs_0_), channel_id=1, source_target_pairs={{0,48},{1,49},{2,50},{3,51},{4,52},{5,53},{6,54},{7,55},{8,56},{9,... | collective-permute-start | bytes 491528 | tf_op jit(solution)/shard_map/ppermute | solution.py:31
  5.7 0.5 collective-permute-start.1
  6.2 0.6 collective-permute-start.2
  6.8 0.8 pad_maximum_fusion.refs_4_
  7.7 3.1 %collective-permute-start.4 = (bf16[16,16,128]{2,1,0:T(8,128)(2,1)S(1)}, bf16[16,16,128]{2,1,0:T(8,128)(2,1)S(1)}, u32[]{:S(2)}, u32[]{:S(2)}) collective-permute-start(bf16[16,16,128]{2,1,0:T(8,128)(2,1)S(1)} %pad_maximum_fusion.refs_4_), channel_id=1, source_target_pairs={{0,128},{1,129},{2,130},{3,131},{4,132},{5,133},{6,134},{7,135},{8... | collective-permute-start | bytes 196616 | tf_op jit(solution)/shard_map/ppermute | solution.py:31
  10.8 1.8 %collective-permute-start.5 = (bf16[16,16,128]{2,1,0:T(8,128)(2,1)S(1)}, bf16[16,16,128]{2,1,0:T(8,128)(2,1)S(1)}, u32[]{:S(2)}, u32[]{:S(2)}) collective-permute-start(bf16[16,16,128]{2,1,0:T(8,128)(2,1)S(1)} %pad_maximum_fusion.refs_4_), channel_id=1, source_target_pairs={{0,192},{1,193},{2,194},{3,195},{4,196},{5,197},{6,198},{7,199},{8... | collective-permute-start | bytes 196616 | tf_op jit(solution)/shard_map/ppermute | solution.py:31
  12.7 0.7 collective-permute-done.4.refs_6_
  13.4 3.0 %collective-permute-done.5.refs_7_ = bf16[16,16,128]{2,1,0:T(8,128)(2,1)S(1)} collective-permute-done((bf16[16,16,128]{2,1,0:T(8,128)(2,1)S(1)}, bf16[16,16,128]{2,1,0:T(8,128)(2,1)S(1)}, u32[]{:S(2)}, u32[]{:S(2)}) %collective-permute-start.5) | collective-permute-done | bytes 65568 | tf_op jit(solution)/shard_map/ppermute | solution.py:31
  16.4 0.4 collective-permute-done.2.refs_3_
  16.9 0.4 collective-permute-start.6
  17.3 1.4 collective-permute-start.7
  18.7 1.7 %collective-permute-start.8 = (bf16[4,16,16,128]{3,2,1,0:T(8,128)(2,1)S(1)}, bf16[4,16,16,128]{3,2,1,0:T(8,128)(2,1)S(1)}, u32[]{:S(2)}, u32[]{:S(2)}) collective-permute-start(bf16[4,16,16,128]{3,2,1,0:T(8,128)(2,1)S(1)} %get-tuple-element.32.rest_0_), channel_id=1, source_target_pairs={{0,48},{1,49},{2,50},{3,51},{4,52},{5,53},{6,54},{7,55},{8,56},{9,... | collective-permute-start | bytes 786440 | tf_op jit(solution)/shard_map/ppermute | solution.py:31
  20.4 1.2 collective-permute-start.9
  21.6 2.8 %collective-permute-done.8.rest_1_ = bf16[4,16,16,128]{3,2,1,0:T(8,128)(2,1)S(1)} collective-permute-done((bf16[4,16,16,128]{3,2,1,0:T(8,128)(2,1)S(1)}, bf16[4,16,16,128]{3,2,1,0:T(8,128)(2,1)S(1)}, u32[]{:S(2)}, u32[]{:S(2)}) %collective-permute-start.8) | collective-permute-done | bytes 262176 | tf_op jit(solution)/shard_map/ppermute | solution.py:31
  24.5 2.8 %collective-permute-done.9.rest_2_ = bf16[4,16,16,128]{3,2,1,0:T(8,128)(2,1)S(1)} collective-permute-done((bf16[4,16,16,128]{3,2,1,0:T(8,128)(2,1)S(1)}, bf16[4,16,16,128]{3,2,1,0:T(8,128)(2,1)S(1)}, u32[]{:S(2)}, u32[]{:S(2)}) %collective-permute-start.9) | collective-permute-done | bytes 262176 | tf_op jit(solution)/shard_map/ppermute | solution.py:31
  27.2 7.5 %collective-permute-done.10.rest_3_ = bf16[4,16,16,128]{3,2,1,0:T(8,128)(2,1)S(1)} collective-permute-done((bf16[4,16,16,128]{3,2,1,0:T(8,128)(2,1)S(1)}, bf16[4,16,16,128]{3,2,1,0:T(8,128)(2,1)S(1)}, u32[]{:S(2)}, u32[]{:S(2)}) %collective-permute-start.10) | collective-permute-done | bytes 262176 | tf_op jit(solution)/shard_map/ppermute | solution.py:31
  34.8 1.7 %second.1 = (bf16[2,128,640]{2,1,0:T(8,128)(2,1)}, bf16[2,128,640]{2,1,0:T(8,128)(2,1)}, bf16[12,128,640]{2,1,0:T(8,128)(2,1)}, bf16[4,4,16,16,128]{4,3,2,1,0:T(8,128)(2,1)S(1)}) custom-call(bf16[4,128,640]{2,1,0:T(8,128)(2,1)S(1)} %get-tuple-element.31.row, bf16[4,128,640]{2,1,0:T(8,128)(2,1)S(1)} %collective-permute-done.6.plus, ...), custom_call_target="tpu_custom_call" | custom-call | bytes 3145728 | tf_op jit(solution)/shard_map/second/pallas_call | solution.py:392
  36.5 3.3 %collective-permute-start.14 = (bf16[12,128,640]{2,1,0:T(8,128)(2,1)}, bf16[12,128,640]{2,1,0:T(8,128)(2,1)}, u32[]{:S(2)}, u32[]{:S(2)}) collective-permute-start(bf16[12,128,640]{2,1,0:T(8,128)(2,1)} %get-tuple-element.36.rest_0_), channel_id=1, source_target_pairs={{0,8},{1,9},{2,10},{3,11},{4,12},{5,13},{6,14},{7,15},{8,0},{9,1},... | collective-permute-start | bytes 5898248 | tf_op jit(solution)/shard_map/ppermute | solution.py:31
  39.8 2.7 %collective-permute-start.12 = (bf16[2,128,640]{2,1,0:T(8,128)(2,1)}, bf16[2,128,640]{2,1,0:T(8,128)(2,1)S(1)}, u32[]{:S(2)}, u32[]{:S(2)}) collective-permute-start(bf16[2,128,640]{2,1,0:T(8,128)(2,1)} %get-tuple-element.37), channel_id=1, source_target_pairs={{0,196},{1,197},{2,198},{3,199},{4,192},{5,193},{6,194},{7,195},{8... | collective-permute-start | bytes 983048 | tf_op jit(solution)/shard_map/ppermute | solution.py:31
  42.6 2.2 %collective-permute-done.11.theirs = bf16[4,4,16,16,128]{4,3,2,1,0:T(8,128)(2,1)S(1)} collective-permute-done((bf16[4,4,16,16,128]{4,3,2,1,0:T(8,128)(2,1)S(1)}, bf16[4,4,16,16,128]{4,3,2,1,0:T(8,128)(2,1)S(1)}, u32[]{:S(2)}, u32[]{:S(2)}) %collective-permute-start.11) | collective-permute-done | bytes 1048608 | tf_op jit(solution)/shard_map/ppermute | solution.py:31
  44.8 0.9 copy-done.7
  45.7 2.5 %queries.1 = (bf16[1024,640]{1,0:T(8,128)(2,1)S(1)}, bf16[8,512,128]{2,1,0:T(8,128)(2,1)S(1)}, bf16[224,1024]{1,0:T(8,128)(2,1)S(1)}, f32[8,128]{1,0:T(8,128)S(1)}) custom-call(s32[5]{0:T(128)S(1)} %stack.50.place, bf16[128,1024]{1,0:T(8,128)(2,1)S(1)} %copy-done.5, bf16[128,512]{1,0:T(8,128)(2,1)S(1)} %copy-done.7, bf16[224,1024]{1,0:T(8,128)(2,1)S(1)} %bitcast.20, ...), custom_call_target="tpu_custom_call" | custom-call | flops 700000000 | bytes 3145728 | tf_op jit(solution)/shard_map/queries/pallas_call | solution.py:407
  48.2 1.2 collective-permute-done.12.low_in
  49.3 1.9 %collective-permute-done.13.high_in = bf16[2,128,640]{2,1,0:T(8,128)(2,1)S(1)} collective-permute-done((bf16[2,128,640]{2,1,0:T(8,128)(2,1)}, bf16[2,128,640]{2,1,0:T(8,128)(2,1)S(1)}, u32[]{:S(2)}, u32[]{:S(2)}) %collective-permute-start.13) | collective-permute-done | bytes 327712 | tf_op jit(solution)/shard_map/ppermute | solution.py:31
  51.3 1.9 %collective-permute-start.15 = (bf16[2,128,640]{2,1,0:T(8,128)(2,1)S(1)}, bf16[2,128,640]{2,1,0:T(8,128)(2,1)S(1)}, u32[]{:S(2)}, u32[]{:S(2)}) collective-permute-start(bf16[2,128,640]{2,1,0:T(8,128)(2,1)S(1)} %get-tuple-element.40.rest_1_), channel_id=1, source_target_pairs={{0,8},{1,9},{2,10},{3,11},{4,12},{5,13},{6,14},{7,15},{8,0},{9,1},... | collective-permute-start | bytes 983048 | tf_op jit(solution)/shard_map/ppermute | solution.py:31
  53.3 2.7 %collective-permute-start.17 = (bf16[224,1024]{1,0:T(8,128)(2,1)S(1)}, bf16[224,1024]{1,0:T(8,128)(2,1)S(1)}, u32[]{:S(2)}, u32[]{:S(2)}) collective-permute-start(bf16[224,1024]{1,0:T(8,128)(2,1)S(1)} %get-tuple-element.43.rest_0_), channel_id=1, source_target_pairs={{0,64},{1,65},{2,66},{3,67},{4,68},{5,69},{6,70},{7,71},{8,72},{9,... | collective-permute-start | bytes 1376264 | tf_op jit(solution)/shard_map/ppermute | solution.py:31
  56.0 1.2 collective-permute-start.23
  57.1 9.0 %attention.1 = (bf16[1024,128]{1,0:T(8,128)(2,1)S(1)}, f32[8,128]{1,0:T(8,128)}) custom-call(s32[5]{0:T(128)S(1)} %stack.50.place, bf16[1024,640]{1,0:T(8,128)(2,1)S(1)} %get-tuple-element.34.query, bf16[8,512,128]{2,1,0:T(8,128)(2,1)S(1)} %get-tuple-element.35.up_value, bf16[12,128,640]{2,1,0:T(8,128)(2,1)} %get-tuple-element.36.rest_0_, ...), custom_call_target="tpu_custom_call" | custom-call | flops 10000000000 | bytes 3145728 | tf_op jit(solution)/shard_map/attention/pallas_call | solution.py:436
  66.1 6.5 %collective-permute-done.17.weight.rest_1_ = bf16[224,1024]{1,0:T(8,128)(2,1)S(1)} collective-permute-done((bf16[224,1024]{1,0:T(8,128)(2,1)S(1)}, bf16[224,1024]{1,0:T(8,128)(2,1)S(1)}, u32[]{:S(2)}, u32[]{:S(2)}) %collective-permute-start.17) | collective-permute-done | bytes 458784 | tf_op jit(solution)/shard_map/ppermute | solution.py:31
  72.6 1.4 collective-permute-start.18
  74.2 5.1 %collective-permute-done.18.right = bf16[1024,128]{1,0:T(8,128)(2,1)S(1)} collective-permute-done((bf16[1024,128]{1,0:T(8,128)(2,1)S(1)}, bf16[1024,128]{1,0:T(8,128)(2,1)S(1)}, u32[]{:S(2)}, u32[]{:S(2)}) %collective-permute-start.18) | collective-permute-done | bytes 262176 | tf_op jit(solution)/shard_map/ppermute | solution.py:31
  79.2 2.2 %collective-permute-done.19.left = bf16[1024,128]{1,0:T(8,128)(2,1)S(1)} collective-permute-done((bf16[1024,128]{1,0:T(8,128)(2,1)S(1)}, bf16[1024,128]{1,0:T(8,128)(2,1)S(1)}, u32[]{:S(2)}, u32[]{:S(2)}) %collective-permute-start.19) | collective-permute-done | bytes 262176 | tf_op jit(solution)/shard_map/ppermute | solution.py:31
  81.9 1.2 collective-permute-start.21
  83.1 13.8 %collective-permute-done.23.rest_1_.rest_3_ = bf16[224,1024]{1,0:T(8,128)(2,1)S(1)} collective-permute-done((bf16[224,1024]{1,0:T(8,128)(2,1)S(1)}, bf16[224,1024]{1,0:T(8,128)(2,1)S(1)}, u32[]{:S(2)}, u32[]{:S(2)}) %collective-permute-start.23) | collective-permute-done | bytes 458784 | tf_op jit(solution)/shard_map/ppermute | solution.py:31
  97.0 1.3 collective-permute-start.24
  98.4 2.2 %collective-permute-done.24.theirs = bf16[4,1024,128]{2,1,0:T(8,128)(2,1)S(1)} collective-permute-done((bf16[4,1024,128]{2,1,0:T(8,128)(2,1)S(1)}, bf16[4,1024,128]{2,1,0:T(8,128)(2,1)S(1)}, u32[]{:S(2)}, u32[]{:S(2)}) %collective-permute-start.24) | collective-permute-done | bytes 1048608 | tf_op jit(solution)/shard_map/ppermute | solution.py:31
  100.6 1.0 copy-done.4
  101.6 2.3 %project.1 = (bf16[2,224,256]{2,1,0:T(8,128)(2,1)S(1)}, bf16[2,224,256]{2,1,0:T(8,128)(2,1)S(1)}, bf16[2,2,224,1024]{3,2,1,0:T(8,128)(2,1)S(1)}) custom-call(s32[6]{0:T(128)S(1)} %stack.48.place, bf16[4,1024,128]{2,1,0:T(8,128)(2,1)S(1)} %third.1.mine, bf16[4,1024,128]{2,1,0:T(8,128)(2,1)S(1)} %collective-permute-done.24.theirs, ...), custom_call_target="tpu_custom_call" | custom-call | flops 470000000 | bytes 3145728 | tf_op jit(solution)/shard_map/project/pallas_call | solution.py:466
  104.0 1.4 collective-permute-start.25
  105.5 2.2 %others.1.terms = bf16[6,2,224,256]{3,2,1,0:T(8,128)(2,1)S(1)} custom-call(s32[6]{0:T(128)S(1)} %stack.48.place, bf16[4,1024,128]{2,1,0:T(8,128)(2,1)S(1)} %third.1.mine, bf16[4,1024,128]{2,1,0:T(8,128)(2,1)S(1)} %collective-permute-done.24.theirs, bf16[2,2,224,1024]{3,2,1,0:T(8,128)(2,1)S(1)} %get-tuple-element.46.weights), custom_call_target="tpu_custom_call" | custom-call | flops 1410000000 | bytes 3145728 | tf_op jit(solution)/shard_map/others/pallas_call | solution.py:475
  107.7 3.2 %collective-permute-done.25.far_give = bf16[2,224,256]{2,1,0:T(8,128)(2,1)S(1)} collective-permute-done((bf16[2,224,256]{2,1,0:T(8,128)(2,1)S(1)}, bf16[2,224,256]{2,1,0:T(8,128)(2,1)S(1)}, u32[]{:S(2)}, u32[]{:S(2)}) %collective-permute-start.25) | collective-permute-done | bytes 229408 | tf_op jit(solution)/shard_map/ppermute | solution.py:31
  110.9 1.0 collective-permute-done.26.left_give.right
  111.9 0.7 copy-done
  112.6 1.0 collective-permute-start.27
  113.6 0.5 collective-permute-start.28
  114.1 4.0 %collective-permute-done.27.left = bf16[2,224,256]{2,1,0:T(8,128)(2,1)S(1)} collective-permute-done((bf16[2,224,256]{2,1,0:T(8,128)(2,1)S(1)}, bf16[2,224,256]{2,1,0:T(8,128)(2,1)S(1)}, u32[]{:S(2)}, u32[]{:S(2)}) %collective-permute-start.27) | collective-permute-done | bytes 229408 | tf_op jit(solution)/shard_map/ppermute | solution.py:31
  118.2 1.5 collective-permute-done.28.far_keep
  119.7 0.9 copy-done.1
  120.6 0.8 give.1
  121.4 1.5 collective-permute-start.31
  122.9 4.3 %collective-permute-start.29 = (bf16[224,256]{1,0:T(8,128)(2,1)S(1)}, bf16[224,256]{1,0:T(8,128)(2,1)S(1)}, u32[]{:S(2)}, u32[]{:S(2)}) collective-permute-start(bf16[224,256]{1,0:T(8,128)(2,1)S(1)} %get-tuple-element.51), channel_id=1, source_target_pairs={{0,4},{1,36},{2,6},{3,38},{4,0},{5,32},{6,2},{7,34},{8,12},{9,44},... | collective-permute-start | bytes 344072 | tf_op jit(solution)/shard_map/ppermute | solution.py:31
  127.3 3.5 %collective-permute-start.30 = (bf16[224,256]{1,0:T(8,128)(2,1)S(1)}, bf16[224,256]{1,0:T(8,128)(2,1)S(1)}, u32[]{:S(2)}, u32[]{:S(2)}) collective-permute-start(bf16[224,256]{1,0:T(8,128)(2,1)S(1)} %get-tuple-element.52), channel_id=1, source_target_pairs={{0,20},{1,52},{2,22},{3,54},{4,16},{5,48},{6,18},{7,50},{8,28},{9,... | collective-permute-start | bytes 344072 | tf_op jit(solution)/shard_map/ppermute | solution.py:31
  130.8 0.7 keep.1
  131.5 4.5 %collective-permute-start.33 = (bf16[224,256]{1,0:T(8,128)(2,1)S(1)}, bf16[224,256]{1,0:T(8,128)(2,1)S(1)}, u32[]{:S(2)}, u32[]{:S(2)}) collective-permute-start(bf16[224,256]{1,0:T(8,128)(2,1)S(1)} %get-tuple-element.55), channel_id=1, source_target_pairs={{0,0},{1,32},{2,2},{3,34},{4,4},{5,36},{6,6},{7,38},{8,8},{9,40},{... | collective-permute-start | bytes 344072 | tf_op jit(solution)/shard_map/ppermute | solution.py:31
  136.0 1.3 collective-permute-start.34
  137.3 2.0 %collective-permute-done.30.give_cross = bf16[224,256]{1,0:T(8,128)(2,1)S(1)} collective-permute-done((bf16[224,256]{1,0:T(8,128)(2,1)S(1)}, bf16[224,256]{1,0:T(8,128)(2,1)S(1)}, u32[]{:S(2)}, u32[]{:S(2)}) %collective-permute-start.30) | collective-permute-done | bytes 114720 | tf_op jit(solution)/shard_map/ppermute | solution.py:31
  139.3 1.4 collective-permute-done.33.keep_same
  140.7 3.2 %collective-permute-done.34.keep_cross = bf16[224,256]{1,0:T(8,128)(2,1)S(1)} collective-permute-done((bf16[224,256]{1,0:T(8,128)(2,1)S(1)}, bf16[224,256]{1,0:T(8,128)(2,1)S(1)}, u32[]{:S(2)}, u32[]{:S(2)}) %collective-permute-start.34) | collective-permute-done | bytes 114720 | tf_op jit(solution)/shard_map/ppermute | solution.py:31
  144.0 2.4 %collective-permute-start.35 = (bf16[2,224,128]{2,1,0:T(8,128)(2,1)S(1)}, bf16[2,224,128]{2,1,0:T(8,128)(2,1)S(1)}, u32[]{:S(2)}, u32[]{:S(2)}) collective-permute-start(bf16[2,224,128]{2,1,0:T(8,128)(2,1)S(1)} %get-tuple-element.58), channel_id=1, source_target_pairs={{0,8},{1,9},{2,10},{3,11},{4,12},{5,13},{6,14},{7,15},{8,0},{9,1},... | collective-permute-start | bytes 344072 | tf_op jit(solution)/shard_map/ppermute | solution.py:31
  146.4 1.0 collective-permute-done.35.theirs
  147.4 1.4 finish.1
  (50 shorter events, 1.9 us)
Async XLA Ops:
  0.6 0.9 copy-start.6
  1.5 0.7 copy-start.8
  2.3 0.7 copy-start.9
  3.1 13.2 %collective-permute-start = (bf16[128,640]{1,0:T(8,128)(2,1)S(1)}, bf16[128,640]{1,0:T(8,128)(2,1)S(1)}, u32[]{:S(2)}, u32[]{:S(2)}) collective-permute-start(bf16[128,640]{1,0:T(8,128)(2,1)S(1)} %keys.1.refs_0_), channel_id=1, source_target_pairs={{0,48},{1,49},{2,50},{3,51},{4,52},{5,53},{6,54},{7,55},{8,56},{9,... | collective-permute-start | bytes 491528 | tf_op jit(solution)/shard_map/ppermute | solution.py:31
  5.7 10.7 %collective-permute-start.1 = (bf16[128,640]{1,0:T(8,128)(2,1)S(1)}, bf16[128,640]{1,0:T(8,128)(2,1)S(1)}, u32[]{:S(2)}, u32[]{:S(2)}) collective-permute-start(bf16[128,640]{1,0:T(8,128)(2,1)S(1)} %keys.1.refs_0_), channel_id=1, source_target_pairs={{0,32},{1,33},{2,34},{3,35},{4,36},{5,37},{6,38},{7,39},{8,40},{9,... | collective-permute-start | bytes 491528 | tf_op jit(solution)/shard_map/ppermute | solution.py:31
  6.2 10.6 %collective-permute-start.2 = (bf16[128,640]{1,0:T(8,128)(2,1)S(1)}, bf16[128,640]{1,0:T(8,128)(2,1)S(1)}, u32[]{:S(2)}, u32[]{:S(2)}) collective-permute-start(bf16[128,640]{1,0:T(8,128)(2,1)S(1)} %keys.1.refs_0_), channel_id=1, source_target_pairs={{0,16},{1,17},{2,18},{3,19},{4,20},{5,21},{6,22},{7,23},{8,24},{9,... | collective-permute-start | bytes 491528 | tf_op jit(solution)/shard_map/ppermute | solution.py:31
  7.6 34.8 %copy-start.10 = (s32[128]{0:T(128)S(1)}, s32[128]{0:T(128)}, u32[]{:S(2)}) copy-start(s32[128]{0:T(128)} %param.12) | copy-start | bytes 1540
  7.6 37.1 %copy-start.2 = (bf16[1024,224]{0,1:T(8,128)(2,1)S(1)}, bf16[1024,224]{0,1:T(8,128)(2,1)}, u32[]{:S(2)}) copy-start(bf16[1024,224]{0,1:T(8,128)(2,1)} %param.15) | copy-start | bytes 1376260
  7.6 37.1 %copy-start.5 = (bf16[128,1024]{1,0:T(8,128)(2,1)S(1)}, bf16[128,1024]{1,0:T(8,128)(2,1)}, u32[]{:S(2)}) copy-start(bf16[128,1024]{1,0:T(8,128)(2,1)} %q_nope_in.1) | copy-start | bytes 786436
  7.6 3.2 %collective-permute-start.3 = (bf16[16,16,128]{2,1,0:T(8,128)(2,1)S(1)}, bf16[16,16,128]{2,1,0:T(8,128)(2,1)S(1)}, u32[]{:S(2)}, u32[]{:S(2)}) collective-permute-start(bf16[16,16,128]{2,1,0:T(8,128)(2,1)S(1)} %pad_maximum_fusion.refs_4_), channel_id=1, source_target_pairs={{0,64},{1,65},{2,66},{3,67},{4,68},{5,69},{6,70},{7,71},{8,72},{9,... | collective-permute-start | bytes 196616 | tf_op jit(solution)/shard_map/ppermute | solution.py:31
  7.7 5.6 %collective-permute-start.4 = (bf16[16,16,128]{2,1,0:T(8,128)(2,1)S(1)}, bf16[16,16,128]{2,1,0:T(8,128)(2,1)S(1)}, u32[]{:S(2)}, u32[]{:S(2)}) collective-permute-start(bf16[16,16,128]{2,1,0:T(8,128)(2,1)S(1)} %pad_maximum_fusion.refs_4_), channel_id=1, source_target_pairs={{0,128},{1,129},{2,130},{3,131},{4,132},{5,133},{6,134},{7,135},{8... | collective-permute-start | bytes 196616 | tf_op jit(solution)/shard_map/ppermute | solution.py:31
  10.8 5.5 %collective-permute-start.5 = (bf16[16,16,128]{2,1,0:T(8,128)(2,1)S(1)}, bf16[16,16,128]{2,1,0:T(8,128)(2,1)S(1)}, u32[]{:S(2)}, u32[]{:S(2)}) collective-permute-start(bf16[16,16,128]{2,1,0:T(8,128)(2,1)S(1)} %pad_maximum_fusion.refs_4_), channel_id=1, source_target_pairs={{0,192},{1,193},{2,194},{3,195},{4,196},{5,197},{6,198},{7,199},{8... | collective-permute-start | bytes 196616 | tf_op jit(solution)/shard_map/ppermute | solution.py:31
  16.9 17.8 %collective-permute-start.6 = (bf16[4,128,640]{2,1,0:T(8,128)(2,1)S(1)}, bf16[4,128,640]{2,1,0:T(8,128)(2,1)S(1)}, u32[]{:S(2)}, u32[]{:S(2)}) collective-permute-start(bf16[4,128,640]{2,1,0:T(8,128)(2,1)S(1)} %get-tuple-element.31.row), channel_id=1, source_target_pairs={{0,196},{1,197},{2,198},{3,199},{4,192},{5,193},{6,194},{7,195},{8... | collective-permute-start | bytes 1966088 | tf_op jit(solution)/shard_map/ppermute | solution.py:31
  17.3 17.5 %collective-permute-start.7 = (bf16[4,128,640]{2,1,0:T(8,128)(2,1)S(1)}, bf16[4,128,640]{2,1,0:T(8,128)(2,1)S(1)}, u32[]{:S(2)}, u32[]{:S(2)}) collective-permute-start(bf16[4,128,640]{2,1,0:T(8,128)(2,1)S(1)} %get-tuple-element.31.row), channel_id=1, source_target_pairs={{0,64},{1,65},{2,66},{3,67},{4,68},{5,69},{6,70},{7,71},{8,72},{9,... | collective-permute-start | bytes 1966088 | tf_op jit(solution)/shard_map/ppermute | solution.py:31
  18.7 5.7 %collective-permute-start.8 = (bf16[4,16,16,128]{3,2,1,0:T(8,128)(2,1)S(1)}, bf16[4,16,16,128]{3,2,1,0:T(8,128)(2,1)S(1)}, u32[]{:S(2)}, u32[]{:S(2)}) collective-permute-start(bf16[4,16,16,128]{3,2,1,0:T(8,128)(2,1)S(1)} %get-tuple-element.32.rest_0_), channel_id=1, source_target_pairs={{0,48},{1,49},{2,50},{3,51},{4,52},{5,53},{6,54},{7,55},{8,56},{9,... | collective-permute-start | bytes 786440 | tf_op jit(solution)/shard_map/ppermute | solution.py:31
  20.4 6.8 %collective-permute-start.9 = (bf16[4,16,16,128]{3,2,1,0:T(8,128)(2,1)S(1)}, bf16[4,16,16,128]{3,2,1,0:T(8,128)(2,1)S(1)}, u32[]{:S(2)}, u32[]{:S(2)}) collective-permute-start(bf16[4,16,16,128]{3,2,1,0:T(8,128)(2,1)S(1)} %get-tuple-element.32.rest_0_), channel_id=1, source_target_pairs={{0,32},{1,33},{2,34},{3,35},{4,36},{5,37},{6,38},{7,39},{8,40},{9,... | collective-permute-start | bytes 786440 | tf_op jit(solution)/shard_map/ppermute | solution.py:31
  21.6 13.1 %collective-permute-start.10 = (bf16[4,16,16,128]{3,2,1,0:T(8,128)(2,1)S(1)}, bf16[4,16,16,128]{3,2,1,0:T(8,128)(2,1)S(1)}, u32[]{:S(2)}, u32[]{:S(2)}) collective-permute-start(bf16[4,16,16,128]{3,2,1,0:T(8,128)(2,1)S(1)} %get-tuple-element.32.rest_0_), channel_id=1, source_target_pairs={{0,16},{1,17},{2,18},{3,19},{4,20},{5,21},{6,22},{7,23},{8,24},{9,... | collective-permute-start | bytes 786440 | tf_op jit(solution)/shard_map/ppermute | solution.py:31
  36.5 20.7 %collective-permute-start.14 = (bf16[12,128,640]{2,1,0:T(8,128)(2,1)}, bf16[12,128,640]{2,1,0:T(8,128)(2,1)}, u32[]{:S(2)}, u32[]{:S(2)}) collective-permute-start(bf16[12,128,640]{2,1,0:T(8,128)(2,1)} %get-tuple-element.36.rest_0_), channel_id=1, source_target_pairs={{0,8},{1,9},{2,10},{3,11},{4,12},{5,13},{6,14},{7,15},{8,0},{9,1},... | collective-permute-start | bytes 5898248 | tf_op jit(solution)/shard_map/ppermute | solution.py:31
  39.8 5.0 %collective-permute-start.11 = (bf16[4,4,16,16,128]{4,3,2,1,0:T(8,128)(2,1)S(1)}, bf16[4,4,16,16,128]{4,3,2,1,0:T(8,128)(2,1)S(1)}, u32[]{:S(2)}, u32[]{:S(2)}) collective-permute-start(bf16[4,4,16,16,128]{4,3,2,1,0:T(8,128)(2,1)S(1)} %get-tuple-element.33.mine), channel_id=1, source_target_pairs={{0,8},{1,9},{2,10},{3,11},{4,12},{5,13},{6,14},{7,15},{8,0},{9,1},... | collective-permute-start | bytes 3145736 | tf_op jit(solution)/shard_map/ppermute | solution.py:31
  39.8 9.6 %collective-permute-start.12 = (bf16[2,128,640]{2,1,0:T(8,128)(2,1)}, bf16[2,128,640]{2,1,0:T(8,128)(2,1)S(1)}, u32[]{:S(2)}, u32[]{:S(2)}) collective-permute-start(bf16[2,128,640]{2,1,0:T(8,128)(2,1)} %get-tuple-element.37), channel_id=1, source_target_pairs={{0,196},{1,197},{2,198},{3,199},{4,192},{5,193},{6,194},{7,195},{8... | collective-permute-start | bytes 983048 | tf_op jit(solution)/shard_map/ppermute | solution.py:31
  42.5 8.8 %collective-permute-start.13 = (bf16[2,128,640]{2,1,0:T(8,128)(2,1)}, bf16[2,128,640]{2,1,0:T(8,128)(2,1)S(1)}, u32[]{:S(2)}, u32[]{:S(2)}) collective-permute-start(bf16[2,128,640]{2,1,0:T(8,128)(2,1)} %get-tuple-element.38), channel_id=1, source_target_pairs={{0,64},{1,65},{2,66},{3,67},{4,68},{5,69},{6,70},{7,71},{8,72},{9,... | collective-permute-start | bytes 983048 | tf_op jit(solution)/shard_map/ppermute | solution.py:31
  44.7 0.9 copy-start.7
  48.1 18.0 %copy-start.3 = (bf16[224,1024]{1,0:T(8,128)(2,1)}, bf16[224,1024]{1,0:T(8,128)(2,1)S(1)}, u32[]{:S(2)}) copy-start(bf16[224,1024]{1,0:T(8,128)(2,1)S(1)} %get-tuple-element.43.rest_0_) | copy-start | bytes 1376260
  51.3 4.7 %collective-permute-start.15 = (bf16[2,128,640]{2,1,0:T(8,128)(2,1)S(1)}, bf16[2,128,640]{2,1,0:T(8,128)(2,1)S(1)}, u32[]{:S(2)}, u32[]{:S(2)}) collective-permute-start(bf16[2,128,640]{2,1,0:T(8,128)(2,1)S(1)} %get-tuple-element.40.rest_1_), channel_id=1, source_target_pairs={{0,8},{1,9},{2,10},{3,11},{4,12},{5,13},{6,14},{7,15},{8,0},{9,1},... | collective-permute-start | bytes 983048 | tf_op jit(solution)/shard_map/ppermute | solution.py:31
  53.2 4.0 %collective-permute-start.16 = (bf16[2,128,640]{2,1,0:T(8,128)(2,1)S(1)}, bf16[2,128,640]{2,1,0:T(8,128)(2,1)S(1)}, u32[]{:S(2)}, u32[]{:S(2)}) collective-permute-start(bf16[2,128,640]{2,1,0:T(8,128)(2,1)S(1)} %get-tuple-element.41.rest_2_), channel_id=1, source_target_pairs={{0,8},{1,9},{2,10},{3,11},{4,12},{5,13},{6,14},{7,15},{8,0},{9,1},... | collective-permute-start | bytes 983048 | tf_op jit(solution)/shard_map/ppermute | solution.py:31
  53.3 19.3 %collective-permute-start.17 = (bf16[224,1024]{1,0:T(8,128)(2,1)S(1)}, bf16[224,1024]{1,0:T(8,128)(2,1)S(1)}, u32[]{:S(2)}, u32[]{:S(2)}) collective-permute-start(bf16[224,1024]{1,0:T(8,128)(2,1)S(1)} %get-tuple-element.43.rest_0_), channel_id=1, source_target_pairs={{0,64},{1,65},{2,66},{3,67},{4,68},{5,69},{6,70},{7,71},{8,72},{9,... | collective-permute-start | bytes 1376264 | tf_op jit(solution)/shard_map/ppermute | solution.py:31
  56.0 27.1 %collective-permute-start.22 = (bf16[224,1024]{1,0:T(8,128)(2,1)S(1)}, bf16[224,1024]{1,0:T(8,128)(2,1)S(1)}, u32[]{:S(2)}, u32[]{:S(2)}) collective-permute-start(bf16[224,1024]{1,0:T(8,128)(2,1)S(1)} %get-tuple-element.43.rest_0_), channel_id=1, source_target_pairs={{0,128},{1,129},{2,130},{3,131},{4,132},{5,133},{6,134},{7,135},{8... | collective-permute-start | bytes 1376264 | tf_op jit(solution)/shard_map/ppermute | solution.py:31
  56.0 40.9 %collective-permute-start.23 = (bf16[224,1024]{1,0:T(8,128)(2,1)S(1)}, bf16[224,1024]{1,0:T(8,128)(2,1)S(1)}, u32[]{:S(2)}, u32[]{:S(2)}) collective-permute-start(bf16[224,1024]{1,0:T(8,128)(2,1)S(1)} %get-tuple-element.43.rest_0_), channel_id=1, source_target_pairs={{0,192},{1,193},{2,194},{3,195},{4,196},{5,197},{6,198},{7,199},{8... | collective-permute-start | bytes 1376264 | tf_op jit(solution)/shard_map/ppermute | solution.py:31
  72.6 6.6 %collective-permute-start.18 = (bf16[1024,128]{1,0:T(8,128)(2,1)S(1)}, bf16[1024,128]{1,0:T(8,128)(2,1)S(1)}, u32[]{:S(2)}, u32[]{:S(2)}) collective-permute-start(bf16[1024,128]{1,0:T(8,128)(2,1)S(1)} %hold.1.own), channel_id=1, source_target_pairs={{0,48},{1,49},{2,50},{3,51},{4,52},{5,53},{6,54},{7,55},{8,56},{9,... | collective-permute-start | bytes 786440 | tf_op jit(solution)/shard_map/ppermute | solution.py:31
  74.0 7.5 %collective-permute-start.19 = (bf16[1024,128]{1,0:T(8,128)(2,1)S(1)}, bf16[1024,128]{1,0:T(8,128)(2,1)S(1)}, u32[]{:S(2)}, u32[]{:S(2)}) collective-permute-start(bf16[1024,128]{1,0:T(8,128)(2,1)S(1)} %hold.1.own), channel_id=1, source_target_pairs={{0,16},{1,17},{2,18},{3,19},{4,20},{5,21},{6,22},{7,23},{8,24},{9,... | collective-permute-start | bytes 786440 | tf_op jit(solution)/shard_map/ppermute | solution.py:31
  81.5 15.4 %collective-permute-start.20 = (bf16[512,128]{1,0:T(8,128)(2,1)S(1)}, bf16[512,128]{1,0:T(8,128)(2,1)S(1)}, u32[]{:S(2)}, u32[]{:S(2)}) collective-permute-start(bf16[512,128]{1,0:T(8,128)(2,1)S(1)} %get-tuple-element.44), channel_id=1, source_target_pairs={{0,48},{1,49},{2,50},{3,51},{4,52},{5,53},{6,54},{7,55},{8,56},{9,... | collective-permute-start | bytes 393224 | tf_op jit(solution)/shard_map/ppermute | solution.py:31
  81.9 15.0 %collective-permute-start.21 = (bf16[512,128]{1,0:T(8,128)(2,1)S(1)}, bf16[512,128]{1,0:T(8,128)(2,1)S(1)}, u32[]{:S(2)}, u32[]{:S(2)}) collective-permute-start(bf16[512,128]{1,0:T(8,128)(2,1)S(1)} %get-tuple-element.45), channel_id=1, source_target_pairs={{0,16},{1,17},{2,18},{3,19},{4,20},{5,21},{6,22},{7,23},{8,24},{9,... | collective-permute-start | bytes 393224 | tf_op jit(solution)/shard_map/ppermute | solution.py:31
  97.0 3.6 %collective-permute-start.24 = (bf16[4,1024,128]{2,1,0:T(8,128)(2,1)S(1)}, bf16[4,1024,128]{2,1,0:T(8,128)(2,1)S(1)}, u32[]{:S(2)}, u32[]{:S(2)}) collective-permute-start(bf16[4,1024,128]{2,1,0:T(8,128)(2,1)S(1)} %third.1.mine), channel_id=1, source_target_pairs={{0,8},{1,9},{2,10},{3,11},{4,12},{5,13},{6,14},{7,15},{8,0},{9,1},... | collective-permute-start | bytes 3145736 | tf_op jit(solution)/shard_map/ppermute | solution.py:31
  100.6 1.0 copy-start.4
  104.0 6.9 %collective-permute-start.25 = (bf16[2,224,256]{2,1,0:T(8,128)(2,1)S(1)}, bf16[2,224,256]{2,1,0:T(8,128)(2,1)S(1)}, u32[]{:S(2)}, u32[]{:S(2)}) collective-permute-start(bf16[2,224,256]{2,1,0:T(8,128)(2,1)S(1)} %get-tuple-element.47), channel_id=1, source_target_pairs={{0,1},{1,2},{2,3},{3,0},{4,5},{5,6},{6,7},{7,4},{8,9},{9,10},{10,1... | collective-permute-start | bytes 688136 | tf_op jit(solution)/shard_map/ppermute | solution.py:31
  105.4 6.5 %collective-permute-start.26 = (bf16[2,224,256]{2,1,0:T(8,128)(2,1)S(1)}, bf16[2,224,256]{2,1,0:T(8,128)(2,1)S(1)}, u32[]{:S(2)}, u32[]{:S(2)}) collective-permute-start(bf16[2,224,256]{2,1,0:T(8,128)(2,1)S(1)} %get-tuple-element.48), channel_id=1, source_target_pairs={{0,3},{1,0},{2,1},{3,2},{4,7},{5,4},{6,5},{7,6},{8,11},{9,8},{10,9... | collective-permute-start | bytes 688136 | tf_op jit(solution)/shard_map/ppermute | solution.py:31
  111.9 0.7 copy-start
  112.6 5.6 %collective-permute-start.27 = (bf16[2,224,256]{2,1,0:T(8,128)(2,1)S(1)}, bf16[2,224,256]{2,1,0:T(8,128)(2,1)S(1)}, u32[]{:S(2)}, u32[]{:S(2)}) collective-permute-start(bf16[2,224,256]{2,1,0:T(8,128)(2,1)S(1)} %get-tuple-element.49), channel_id=1, source_target_pairs={{0,1},{1,2},{2,3},{3,0},{4,5},{5,6},{6,7},{7,4},{8,9},{9,10},{10,1... | collective-permute-start | bytes 688136 | tf_op jit(solution)/shard_map/ppermute | solution.py:31
  113.6 6.0 %collective-permute-start.28 = (bf16[2,224,256]{2,1,0:T(8,128)(2,1)S(1)}, bf16[2,224,256]{2,1,0:T(8,128)(2,1)S(1)}, u32[]{:S(2)}, u32[]{:S(2)}) collective-permute-start(bf16[2,224,256]{2,1,0:T(8,128)(2,1)S(1)} %get-tuple-element.50), channel_id=1, source_target_pairs={{0,3},{1,0},{2,1},{3,2},{4,7},{5,4},{6,5},{7,6},{8,11},{9,8},{10,9... | collective-permute-start | bytes 688136 | tf_op jit(solution)/shard_map/ppermute | solution.py:31
  119.7 0.9 copy-start.1
  121.4 9.4 %collective-permute-start.31 = (bf16[2,224,256]{2,1,0:T(8,128)(2,1)S(1)}, bf16[2,224,256]{2,1,0:T(8,128)(2,1)S(1)}, u32[]{:S(2)}, u32[]{:S(2)}) collective-permute-start(bf16[2,224,256]{2,1,0:T(8,128)(2,1)S(1)} %get-tuple-element.53), channel_id=1, source_target_pairs={{0,1},{1,2},{2,3},{3,0},{4,5},{5,6},{6,7},{7,4},{8,9},{9,10},{10,1... | collective-permute-start | bytes 688136 | tf_op jit(solution)/shard_map/ppermute | solution.py:31
  122.9 7.9 %collective-permute-start.32 = (bf16[2,224,256]{2,1,0:T(8,128)(2,1)S(1)}, bf16[2,224,256]{2,1,0:T(8,128)(2,1)S(1)}, u32[]{:S(2)}, u32[]{:S(2)}) collective-permute-start(bf16[2,224,256]{2,1,0:T(8,128)(2,1)S(1)} %get-tuple-element.54), channel_id=1, source_target_pairs={{0,3},{1,0},{2,1},{3,2},{4,7},{5,4},{6,5},{7,6},{8,11},{9,8},{10,9... | collective-permute-start | bytes 688136 | tf_op jit(solution)/shard_map/ppermute | solution.py:31
  122.9 14.4 %collective-permute-start.29 = (bf16[224,256]{1,0:T(8,128)(2,1)S(1)}, bf16[224,256]{1,0:T(8,128)(2,1)S(1)}, u32[]{:S(2)}, u32[]{:S(2)}) collective-permute-start(bf16[224,256]{1,0:T(8,128)(2,1)S(1)} %get-tuple-element.51), channel_id=1, source_target_pairs={{0,4},{1,36},{2,6},{3,38},{4,0},{5,32},{6,2},{7,34},{8,12},{9,44},... | collective-permute-start | bytes 344072 | tf_op jit(solution)/shard_map/ppermute | solution.py:31
  127.3 12.1 %collective-permute-start.30 = (bf16[224,256]{1,0:T(8,128)(2,1)S(1)}, bf16[224,256]{1,0:T(8,128)(2,1)S(1)}, u32[]{:S(2)}, u32[]{:S(2)}) collective-permute-start(bf16[224,256]{1,0:T(8,128)(2,1)S(1)} %get-tuple-element.52), channel_id=1, source_target_pairs={{0,20},{1,52},{2,22},{3,54},{4,16},{5,48},{6,18},{7,50},{8,28},{9,... | collective-permute-start | bytes 344072 | tf_op jit(solution)/shard_map/ppermute | solution.py:31
  131.5 9.2 %collective-permute-start.33 = (bf16[224,256]{1,0:T(8,128)(2,1)S(1)}, bf16[224,256]{1,0:T(8,128)(2,1)S(1)}, u32[]{:S(2)}, u32[]{:S(2)}) collective-permute-start(bf16[224,256]{1,0:T(8,128)(2,1)S(1)} %get-tuple-element.55), channel_id=1, source_target_pairs={{0,0},{1,32},{2,2},{3,34},{4,4},{5,36},{6,6},{7,38},{8,8},{9,40},{... | collective-permute-start | bytes 344072 | tf_op jit(solution)/shard_map/ppermute | solution.py:31
  136.0 7.9 %collective-permute-start.34 = (bf16[224,256]{1,0:T(8,128)(2,1)S(1)}, bf16[224,256]{1,0:T(8,128)(2,1)S(1)}, u32[]{:S(2)}, u32[]{:S(2)}) collective-permute-start(bf16[224,256]{1,0:T(8,128)(2,1)S(1)} %get-tuple-element.56), channel_id=1, source_target_pairs={{0,16},{1,48},{2,18},{3,50},{4,20},{5,52},{6,22},{7,54},{8,24},{9,... | collective-permute-start | bytes 344072 | tf_op jit(solution)/shard_map/ppermute | solution.py:31
  144.0 3.3 %collective-permute-start.35 = (bf16[2,224,128]{2,1,0:T(8,128)(2,1)S(1)}, bf16[2,224,128]{2,1,0:T(8,128)(2,1)S(1)}, u32[]{:S(2)}, u32[]{:S(2)}) collective-permute-start(bf16[2,224,128]{2,1,0:T(8,128)(2,1)S(1)} %get-tuple-element.58), channel_id=1, source_target_pairs={{0,8},{1,9},{2,10},{3,11},{4,12},{5,13},{6,14},{7,15},{8,0},{9,1},... | collective-permute-start | bytes 344072 | tf_op jit(solution)/shard_map/ppermute | solution.py:31

commit v2 on v1

--- a/solution.py
+++ b/solution.py
@@ -320,14 +320,15 @@
     return whole.astype(jnp.bfloat16)
 
 
-def early_kernel(terms, far_give, left_give, out, far_out):
+def early_kernel(terms, far_give, left_give, out, far_out, part):
+    part[...] = terms[4].astype(jnp.float32) + left_give[...].astype(jnp.float32)
     out[...] = summed(terms.at[1], far_give)
     far_out[...] = terms[0]
 
 
 def give_kernel(place, terms, left, right, far_keep, *outs):
     same, cross, left_out, right_out, whole = outs
-    whole[...] = summed(terms.at[4], left, right)
+    whole[...] = summed(left, right)
     same[...] = whole[place[0]]
     cross[...] = whole[1 - place[0]]
     left_out[...] = summed(terms.at[3], far_keep)
@@ -482,8 +483,8 @@
     )(order, gathered, theirs, held)
     low = jnp.stack([x % 2, core]).astype(jnp.int32)
     left_give = moved(left_give, along_y(-1))
-    right_give, far_keep = call(
-        early_kernel, [term] * 2, [VMEM] * 3, limit=16, name="early"
+    right_give, far_keep, left_give = call(
+        early_kernel, [term] * 2 + [((2, 224, 256), jnp.float32)], [VMEM] * 3, limit=16, name="early"
     )(terms, moved(far_give, along_y(1)), left_give)
     same, cross, left_keep, right_keep = call(
         give_kernel,

time: 149 us -> 148 us (level)
  waiting for transfers between devices: 69.7 us -> 73.2 us
  Pallas kernels: 21.1 us -> 17.7 us
  local copies, waits for them, and re-layouts: 6.03 us -> 4.41 us
    pallas_call x1, Pallas kernels: 8.96 us -> 5.45 us  [per_device(): call(attention_kernel, [((1024, 128), jnp.bfloat16), ((8, 128), jnp.float...]
    ppermute x36, waiting for transfers between devices: 69.7 us -> 73.2 us  [moved(): return lax.ppermute(array, AXES, pairs)]
    unnamed x22 -> x18, local copies, waits for them, and re-layouts: 5.83 us -> 4.21 us
  transfers between devices with their start and end apart: 36 -> 36, of which waited for: 22 -> 22; matrix products, arithmetic and copies ran while one was open for 1% -> 1% of each run, Pallas kernels for 10% -> 7%
where the time goes in v2:
time: 148 us; the launch traced here: 147 us
  waiting for transfers between devices  73.2 us (49%)
  starting transfers between devices  50.3 us (34%)
  Pallas kernels  17.7 us (12%)
  local copies, waits for them, and re-layouts  4.41 us (3%)
    ppermute x36, waiting for transfers between devices, moved(): return lax.ppermute(array, AXES, pairs)  73.2 us
    ppermute x36, starting transfers between devices, moved(): return lax.ppermute(array, AXES, pairs)  50.3 us
    pallas_call x1, Pallas kernels, per_device(): call(attention_kernel, [((1024, 128), jnp.bfloat16), ((8, 128), jnp.float...  5.45 us
    unnamed x18, local copies, waits for them, and re-layouts  4.21 us
  transfers between devices with their start and end apart: 36, of which 22 were waited for; matrix products, arithmetic and copies ran while one was open for 1% of the time, Pallas kernels for 7%

profile of v2, /device:TPU:41, one launch (start us, length us, event | category | flops | bytes accessed | tf_op | source)
XLA Modules:
  0.0 147.2 jit_solution(15969500466530092136)
XLA Ops:
  0.6 0.9 copy-done.4
  1.5 0.7 copy-done.6
  2.3 0.7 copy-done.7
  2.9 0.2 keys.1.refs_0_
  3.1 2.6 %collective-permute-start = (bf16[128,640]{1,0:T(8,128)(2,1)S(1)}, bf16[128,640]{1,0:T(8,128)(2,1)S(1)}, u32[]{:S(2)}, u32[]{:S(2)}) collective-permute-start(bf16[128,640]{1,0:T(8,128)(2,1)S(1)} %keys.1.refs_0_), channel_id=1, source_target_pairs={{0,48},{1,49},{2,50},{3,51},{4,52},{5,53},{6,54},{7,55},{8,56},{9,... | collective-permute-start | bytes 491528 | tf_op jit(solution)/shard_map/ppermute | solution.py:31
  5.7 0.5 collective-permute-start.1
  6.2 0.6 collective-permute-start.2
  6.8 0.8 pad_maximum_fusion.refs_4_
  7.7 3.1 %collective-permute-start.4 = (bf16[16,16,128]{2,1,0:T(8,128)(2,1)S(1)}, bf16[16,16,128]{2,1,0:T(8,128)(2,1)S(1)}, u32[]{:S(2)}, u32[]{:S(2)}) collective-permute-start(bf16[16,16,128]{2,1,0:T(8,128)(2,1)S(1)} %pad_maximum_fusion.refs_4_), channel_id=1, source_target_pairs={{0,128},{1,129},{2,130},{3,131},{4,132},{5,133},{6,134},{7,135},{8... | collective-permute-start | bytes 196616 | tf_op jit(solution)/shard_map/ppermute | solution.py:31
  10.8 1.8 %collective-permute-start.5 = (bf16[16,16,128]{2,1,0:T(8,128)(2,1)S(1)}, bf16[16,16,128]{2,1,0:T(8,128)(2,1)S(1)}, u32[]{:S(2)}, u32[]{:S(2)}) collective-permute-start(bf16[16,16,128]{2,1,0:T(8,128)(2,1)S(1)} %pad_maximum_fusion.refs_4_), channel_id=1, source_target_pairs={{0,192},{1,193},{2,194},{3,195},{4,196},{5,197},{6,198},{7,199},{8... | collective-permute-start | bytes 196616 | tf_op jit(solution)/shard_map/ppermute | solution.py:31
  12.7 0.7 collective-permute-done.4.refs_6_
  13.4 3.0 %collective-permute-done.5.refs_7_ = bf16[16,16,128]{2,1,0:T(8,128)(2,1)S(1)} collective-permute-done((bf16[16,16,128]{2,1,0:T(8,128)(2,1)S(1)}, bf16[16,16,128]{2,1,0:T(8,128)(2,1)S(1)}, u32[]{:S(2)}, u32[]{:S(2)}) %collective-permute-start.5) | collective-permute-done | bytes 65568 | tf_op jit(solution)/shard_map/ppermute | solution.py:31
  16.4 0.4 collective-permute-done.2.refs_3_
  16.9 0.4 collective-permute-start.6
  17.3 1.4 collective-permute-start.7
  18.7 1.7 %collective-permute-start.8 = (bf16[4,16,16,128]{3,2,1,0:T(8,128)(2,1)S(1)}, bf16[4,16,16,128]{3,2,1,0:T(8,128)(2,1)S(1)}, u32[]{:S(2)}, u32[]{:S(2)}) collective-permute-start(bf16[4,16,16,128]{3,2,1,0:T(8,128)(2,1)S(1)} %get-tuple-element.33.rest_0_), channel_id=1, source_target_pairs={{0,48},{1,49},{2,50},{3,51},{4,52},{5,53},{6,54},{7,55},{8,56},{9,... | collective-permute-start | bytes 786440 | tf_op jit(solution)/shard_map/ppermute | solution.py:31
  20.4 1.2 collective-permute-start.9
  21.6 2.8 %collective-permute-done.8.rest_1_ = bf16[4,16,16,128]{3,2,1,0:T(8,128)(2,1)S(1)} collective-permute-done((bf16[4,16,16,128]{3,2,1,0:T(8,128)(2,1)S(1)}, bf16[4,16,16,128]{3,2,1,0:T(8,128)(2,1)S(1)}, u32[]{:S(2)}, u32[]{:S(2)}) %collective-permute-start.8) | collective-permute-done | bytes 262176 | tf_op jit(solution)/shard_map/ppermute | solution.py:31
  24.5 2.8 %collective-permute-done.9.rest_2_ = bf16[4,16,16,128]{3,2,1,0:T(8,128)(2,1)S(1)} collective-permute-done((bf16[4,16,16,128]{3,2,1,0:T(8,128)(2,1)S(1)}, bf16[4,16,16,128]{3,2,1,0:T(8,128)(2,1)S(1)}, u32[]{:S(2)}, u32[]{:S(2)}) %collective-permute-start.9) | collective-permute-done | bytes 262176 | tf_op jit(solution)/shard_map/ppermute | solution.py:31
  27.2 7.5 %collective-permute-done.10.rest_3_ = bf16[4,16,16,128]{3,2,1,0:T(8,128)(2,1)S(1)} collective-permute-done((bf16[4,16,16,128]{3,2,1,0:T(8,128)(2,1)S(1)}, bf16[4,16,16,128]{3,2,1,0:T(8,128)(2,1)S(1)}, u32[]{:S(2)}, u32[]{:S(2)}) %collective-permute-start.10) | collective-permute-done | bytes 262176 | tf_op jit(solution)/shard_map/ppermute | solution.py:31
  34.8 1.7 %second.1 = (bf16[2,128,640]{2,1,0:T(8,128)(2,1)}, bf16[2,128,640]{2,1,0:T(8,128)(2,1)}, bf16[12,128,640]{2,1,0:T(8,128)(2,1)}, bf16[4,4,16,16,128]{4,3,2,1,0:T(8,128)(2,1)S(1)}) custom-call(bf16[4,128,640]{2,1,0:T(8,128)(2,1)S(1)} %get-tuple-element.32.row, bf16[4,128,640]{2,1,0:T(8,128)(2,1)S(1)} %collective-permute-done.6.plus, ...), custom_call_target="tpu_custom_call" | custom-call | bytes 3145728 | tf_op jit(solution)/shard_map/second/pallas_call | solution.py:393
  36.5 3.3 %collective-permute-start.14 = (bf16[12,128,640]{2,1,0:T(8,128)(2,1)}, bf16[12,128,640]{2,1,0:T(8,128)(2,1)}, u32[]{:S(2)}, u32[]{:S(2)}) collective-permute-start(bf16[12,128,640]{2,1,0:T(8,128)(2,1)} %get-tuple-element.37.rest_0_), channel_id=1, source_target_pairs={{0,8},{1,9},{2,10},{3,11},{4,12},{5,13},{6,14},{7,15},{8,0},{9,1},... | collective-permute-start | bytes 5898248 | tf_op jit(solution)/shard_map/ppermute | solution.py:31
  39.8 2.7 %collective-permute-start.12 = (bf16[2,128,640]{2,1,0:T(8,128)(2,1)}, bf16[2,128,640]{2,1,0:T(8,128)(2,1)S(1)}, u32[]{:S(2)}, u32[]{:S(2)}) collective-permute-start(bf16[2,128,640]{2,1,0:T(8,128)(2,1)} %get-tuple-element.38), channel_id=1, source_target_pairs={{0,196},{1,197},{2,198},{3,199},{4,192},{5,193},{6,194},{7,195},{8... | collective-permute-start | bytes 983048 | tf_op jit(solution)/shard_map/ppermute | solution.py:31
  42.6 2.2 %collective-permute-done.11.theirs = bf16[4,4,16,16,128]{4,3,2,1,0:T(8,128)(2,1)S(1)} collective-permute-done((bf16[4,4,16,16,128]{4,3,2,1,0:T(8,128)(2,1)S(1)}, bf16[4,4,16,16,128]{4,3,2,1,0:T(8,128)(2,1)S(1)}, u32[]{:S(2)}, u32[]{:S(2)}) %collective-permute-start.11) | collective-permute-done | bytes 1048608 | tf_op jit(solution)/shard_map/ppermute | solution.py:31
  44.8 0.9 copy-done.5
  45.7 2.5 %queries.1 = (bf16[1024,640]{1,0:T(8,128)(2,1)S(1)}, bf16[8,512,128]{2,1,0:T(8,128)(2,1)S(1)}, bf16[224,1024]{1,0:T(8,128)(2,1)S(1)}, f32[8,128]{1,0:T(8,128)S(1)}) custom-call(s32[5]{0:T(128)S(1)} %stack.50.place, bf16[128,1024]{1,0:T(8,128)(2,1)S(1)} %copy-done.3, bf16[128,512]{1,0:T(8,128)(2,1)S(1)} %copy-done.5, bf16[224,1024]{1,0:T(8,128)(2,1)S(1)} %bitcast.20, ...), custom_call_target="tpu_custom_call" | custom-call | flops 700000000 | bytes 3145728 | tf_op jit(solution)/shard_map/queries/pallas_call | solution.py:408
  48.2 1.2 collective-permute-done.12.low_in
  49.3 1.9 %collective-permute-done.13.high_in = bf16[2,128,640]{2,1,0:T(8,128)(2,1)S(1)} collective-permute-done((bf16[2,128,640]{2,1,0:T(8,128)(2,1)}, bf16[2,128,640]{2,1,0:T(8,128)(2,1)S(1)}, u32[]{:S(2)}, u32[]{:S(2)}) %collective-permute-start.13) | collective-permute-done | bytes 327712 | tf_op jit(solution)/shard_map/ppermute | solution.py:31
  51.3 1.9 %collective-permute-start.15 = (bf16[2,128,640]{2,1,0:T(8,128)(2,1)S(1)}, bf16[2,128,640]{2,1,0:T(8,128)(2,1)S(1)}, u32[]{:S(2)}, u32[]{:S(2)}) collective-permute-start(bf16[2,128,640]{2,1,0:T(8,128)(2,1)S(1)} %get-tuple-element.41.rest_1_), channel_id=1, source_target_pairs={{0,8},{1,9},{2,10},{3,11},{4,12},{5,13},{6,14},{7,15},{8,0},{9,1},... | collective-permute-start | bytes 983048 | tf_op jit(solution)/shard_map/ppermute | solution.py:31
  53.3 2.7 %collective-permute-start.17 = (bf16[224,1024]{1,0:T(8,128)(2,1)S(1)}, bf16[224,1024]{1,0:T(8,128)(2,1)S(1)}, u32[]{:S(2)}, u32[]{:S(2)}) collective-permute-start(bf16[224,1024]{1,0:T(8,128)(2,1)S(1)} %get-tuple-element.44.rest_0_), channel_id=1, source_target_pairs={{0,64},{1,65},{2,66},{3,67},{4,68},{5,69},{6,70},{7,71},{8,72},{9,... | collective-permute-start | bytes 1376264 | tf_op jit(solution)/shard_map/ppermute | solution.py:31
  56.0 1.2 collective-permute-start.23
  57.2 5.5 %attention.1 = (bf16[1024,128]{1,0:T(8,128)(2,1)S(1)}, f32[8,128]{1,0:T(8,128)}) custom-call(s32[5]{0:T(128)S(1)} %stack.50.place, bf16[1024,640]{1,0:T(8,128)(2,1)S(1)} %get-tuple-element.35.query, bf16[8,512,128]{2,1,0:T(8,128)(2,1)S(1)} %get-tuple-element.36.up_value, bf16[12,128,640]{2,1,0:T(8,128)(2,1)} %get-tuple-element.37.rest_0_, ...), custom_call_target="tpu_custom_call" | custom-call | flops 10000000000 | bytes 3145728 | tf_op jit(solution)/shard_map/attention/pallas_call | solution.py:437
  62.6 10.0 %collective-permute-done.17.weight.rest_1_ = bf16[224,1024]{1,0:T(8,128)(2,1)S(1)} collective-permute-done((bf16[224,1024]{1,0:T(8,128)(2,1)S(1)}, bf16[224,1024]{1,0:T(8,128)(2,1)S(1)}, u32[]{:S(2)}, u32[]{:S(2)}) %collective-permute-start.17) | collective-permute-done | bytes 458784 | tf_op jit(solution)/shard_map/ppermute | solution.py:31
  72.6 1.4 collective-permute-start.18
  74.2 5.1 %collective-permute-done.18.right = bf16[1024,128]{1,0:T(8,128)(2,1)S(1)} collective-permute-done((bf16[1024,128]{1,0:T(8,128)(2,1)S(1)}, bf16[1024,128]{1,0:T(8,128)(2,1)S(1)}, u32[]{:S(2)}, u32[]{:S(2)}) %collective-permute-start.18) | collective-permute-done | bytes 262176 | tf_op jit(solution)/shard_map/ppermute | solution.py:31
  79.3 2.2 %collective-permute-done.19.left = bf16[1024,128]{1,0:T(8,128)(2,1)S(1)} collective-permute-done((bf16[1024,128]{1,0:T(8,128)(2,1)S(1)}, bf16[1024,128]{1,0:T(8,128)(2,1)S(1)}, u32[]{:S(2)}, u32[]{:S(2)}) %collective-permute-start.19) | collective-permute-done | bytes 262176 | tf_op jit(solution)/shard_map/ppermute | solution.py:31
  81.5 0.4 collective-permute-start.20
  81.9 1.2 collective-permute-start.21
  83.1 13.8 %collective-permute-done.23.rest_1_.rest_3_ = bf16[224,1024]{1,0:T(8,128)(2,1)S(1)} collective-permute-done((bf16[224,1024]{1,0:T(8,128)(2,1)S(1)}, bf16[224,1024]{1,0:T(8,128)(2,1)S(1)}, u32[]{:S(2)}, u32[]{:S(2)}) %collective-permute-start.23) | collective-permute-done | bytes 458784 | tf_op jit(solution)/shard_map/ppermute | solution.py:31
  97.0 1.3 collective-permute-start.24
  98.4 2.2 %collective-permute-done.24.theirs = bf16[4,1024,128]{2,1,0:T(8,128)(2,1)S(1)} collective-permute-done((bf16[4,1024,128]{2,1,0:T(8,128)(2,1)S(1)}, bf16[4,1024,128]{2,1,0:T(8,128)(2,1)S(1)}, u32[]{:S(2)}, u32[]{:S(2)}) %collective-permute-start.24) | collective-permute-done | bytes 1048608 | tf_op jit(solution)/shard_map/ppermute | solution.py:31
  100.6 1.0 copy-done.2
  101.6 2.3 %project.1 = (bf16[2,224,256]{2,1,0:T(8,128)(2,1)S(1)}, bf16[2,224,256]{2,1,0:T(8,128)(2,1)S(1)}, bf16[2,2,224,1024]{3,2,1,0:T(8,128)(2,1)S(1)}) custom-call(s32[6]{0:T(128)S(1)} %stack.48.place, bf16[4,1024,128]{2,1,0:T(8,128)(2,1)S(1)} %third.1.mine, bf16[4,1024,128]{2,1,0:T(8,128)(2,1)S(1)} %collective-permute-done.24.theirs, ...), custom_call_target="tpu_custom_call" | custom-call | flops 470000000 | bytes 3145728 | tf_op jit(solution)/shard_map/project/pallas_call | solution.py:467
  104.0 1.4 collective-permute-start.25
  105.5 2.2 %others.1.terms = bf16[6,2,224,256]{3,2,1,0:T(8,128)(2,1)S(1)} custom-call(s32[6]{0:T(128)S(1)} %stack.48.place, bf16[4,1024,128]{2,1,0:T(8,128)(2,1)S(1)} %third.1.mine, bf16[4,1024,128]{2,1,0:T(8,128)(2,1)S(1)} %collective-permute-done.24.theirs, bf16[2,2,224,1024]{3,2,1,0:T(8,128)(2,1)S(1)} %get-tuple-element.47.weights), custom_call_target="tpu_custom_call" | custom-call | flops 1410000000 | bytes 3145728 | tf_op jit(solution)/shard_map/others/pallas_call | solution.py:476
  107.7 3.2 %collective-permute-done.25.far_give = bf16[2,224,256]{2,1,0:T(8,128)(2,1)S(1)} collective-permute-done((bf16[2,224,256]{2,1,0:T(8,128)(2,1)S(1)}, bf16[2,224,256]{2,1,0:T(8,128)(2,1)S(1)}, u32[]{:S(2)}, u32[]{:S(2)}) %collective-permute-start.25) | collective-permute-done | bytes 229408 | tf_op jit(solution)/shard_map/ppermute | solution.py:31
  110.9 1.0 collective-permute-done.26.left_give
  112.0 1.1 collective-permute-start.27
  113.1 0.5 collective-permute-start.28
  113.6 4.0 %collective-permute-done.27.left = bf16[2,224,256]{2,1,0:T(8,128)(2,1)S(1)} collective-permute-done((bf16[2,224,256]{2,1,0:T(8,128)(2,1)S(1)}, bf16[2,224,256]{2,1,0:T(8,128)(2,1)S(1)}, u32[]{:S(2)}, u32[]{:S(2)}) %collective-permute-start.27) | collective-permute-done | bytes 229408 | tf_op jit(solution)/shard_map/ppermute | solution.py:31
  117.6 1.5 %collective-permute-done.28.far_keep = bf16[2,224,256]{2,1,0:T(8,128)(2,1)S(1)} collective-permute-done((bf16[2,224,256]{2,1,0:T(8,128)(2,1)S(1)}, bf16[2,224,256]{2,1,0:T(8,128)(2,1)S(1)}, u32[]{:S(2)}, u32[]{:S(2)}) %collective-permute-start.28) | collective-permute-done | bytes 229408 | tf_op jit(solution)/shard_map/ppermute | solution.py:31
  119.1 0.7 give.1
  119.8 1.5 %collective-permute-start.31 = (bf16[2,224,256]{2,1,0:T(8,128)(2,1)S(1)}, bf16[2,224,256]{2,1,0:T(8,128)(2,1)S(1)}, u32[]{:S(2)}, u32[]{:S(2)}) collective-permute-start(bf16[2,224,256]{2,1,0:T(8,128)(2,1)S(1)} %get-tuple-element.55), channel_id=1, source_target_pairs={{0,1},{1,2},{2,3},{3,0},{4,5},{5,6},{6,7},{7,4},{8,9},{9,10},{10,1... | collective-permute-start | bytes 688136 | tf_op jit(solution)/shard_map/ppermute | solution.py:31
  121.4 4.3 %collective-permute-start.29 = (bf16[224,256]{1,0:T(8,128)(2,1)S(1)}, bf16[224,256]{1,0:T(8,128)(2,1)S(1)}, u32[]{:S(2)}, u32[]{:S(2)}) collective-permute-start(bf16[224,256]{1,0:T(8,128)(2,1)S(1)} %get-tuple-element.53), channel_id=1, source_target_pairs={{0,4},{1,36},{2,6},{3,38},{4,0},{5,32},{6,2},{7,34},{8,12},{9,44},... | collective-permute-start | bytes 344072 | tf_op jit(solution)/shard_map/ppermute | solution.py:31
  125.7 3.5 %collective-permute-start.30 = (bf16[224,256]{1,0:T(8,128)(2,1)S(1)}, bf16[224,256]{1,0:T(8,128)(2,1)S(1)}, u32[]{:S(2)}, u32[]{:S(2)}) collective-permute-start(bf16[224,256]{1,0:T(8,128)(2,1)S(1)} %get-tuple-element.54), channel_id=1, source_target_pairs={{0,20},{1,52},{2,22},{3,54},{4,16},{5,48},{6,18},{7,50},{8,28},{9,... | collective-permute-start | bytes 344072 | tf_op jit(solution)/shard_map/ppermute | solution.py:31
  129.2 0.7 keep.1
  129.9 4.6 %collective-permute-start.33 = (bf16[224,256]{1,0:T(8,128)(2,1)S(1)}, bf16[224,256]{1,0:T(8,128)(2,1)S(1)}, u32[]{:S(2)}, u32[]{:S(2)}) collective-permute-start(bf16[224,256]{1,0:T(8,128)(2,1)S(1)} %get-tuple-element.57), channel_id=1, source_target_pairs={{0,0},{1,32},{2,2},{3,34},{4,4},{5,36},{6,6},{7,38},{8,8},{9,40},{... | collective-permute-start | bytes 344072 | tf_op jit(solution)/shard_map/ppermute | solution.py:31
  134.5 1.3 collective-permute-start.34
  135.8 2.0 %collective-permute-done.30.give_cross = bf16[224,256]{1,0:T(8,128)(2,1)S(1)} collective-permute-done((bf16[224,256]{1,0:T(8,128)(2,1)S(1)}, bf16[224,256]{1,0:T(8,128)(2,1)S(1)}, u32[]{:S(2)}, u32[]{:S(2)}) %collective-permute-start.30) | collective-permute-done | bytes 114720 | tf_op jit(solution)/shard_map/ppermute | solution.py:31
  137.8 1.4 collective-permute-done.33.keep_same
  139.1 3.2 %collective-permute-done.34.keep_cross = bf16[224,256]{1,0:T(8,128)(2,1)S(1)} collective-permute-done((bf16[224,256]{1,0:T(8,128)(2,1)S(1)}, bf16[224,256]{1,0:T(8,128)(2,1)S(1)}, u32[]{:S(2)}, u32[]{:S(2)}) %collective-permute-start.34) | collective-permute-done | bytes 114720 | tf_op jit(solution)/shard_map/ppermute | solution.py:31
  142.5 2.4 %collective-permute-start.35 = (bf16[2,224,128]{2,1,0:T(8,128)(2,1)S(1)}, bf16[2,224,128]{2,1,0:T(8,128)(2,1)S(1)}, u32[]{:S(2)}, u32[]{:S(2)}) collective-permute-start(bf16[2,224,128]{2,1,0:T(8,128)(2,1)S(1)} %get-tuple-element.60), channel_id=1, source_target_pairs={{0,8},{1,9},{2,10},{3,11},{4,12},{5,13},{6,14},{7,15},{8,0},{9,1},... | collective-permute-start | bytes 344072 | tf_op jit(solution)/shard_map/ppermute | solution.py:31
  144.9 1.0 collective-permute-done.35.theirs
  145.8 1.4 finish.1
  (46 shorter events, 1.4 us)
Async XLA Ops:
  0.6 0.9 copy-start.4
  1.5 0.7 copy-start.6
  2.3 0.7 copy-start.7
  3.1 13.2 %collective-permute-start = (bf16[128,640]{1,0:T(8,128)(2,1)S(1)}, bf16[128,640]{1,0:T(8,128)(2,1)S(1)}, u32[]{:S(2)}, u32[]{:S(2)}) collective-permute-start(bf16[128,640]{1,0:T(8,128)(2,1)S(1)} %keys.1.refs_0_), channel_id=1, source_target_pairs={{0,48},{1,49},{2,50},{3,51},{4,52},{5,53},{6,54},{7,55},{8,56},{9,... | collective-permute-start | bytes 491528 | tf_op jit(solution)/shard_map/ppermute | solution.py:31
  5.7 10.7 %collective-permute-start.1 = (bf16[128,640]{1,0:T(8,128)(2,1)S(1)}, bf16[128,640]{1,0:T(8,128)(2,1)S(1)}, u32[]{:S(2)}, u32[]{:S(2)}) collective-permute-start(bf16[128,640]{1,0:T(8,128)(2,1)S(1)} %keys.1.refs_0_), channel_id=1, source_target_pairs={{0,32},{1,33},{2,34},{3,35},{4,36},{5,37},{6,38},{7,39},{8,40},{9,... | collective-permute-start | bytes 491528 | tf_op jit(solution)/shard_map/ppermute | solution.py:31
  6.2 10.6 %collective-permute-start.2 = (bf16[128,640]{1,0:T(8,128)(2,1)S(1)}, bf16[128,640]{1,0:T(8,128)(2,1)S(1)}, u32[]{:S(2)}, u32[]{:S(2)}) collective-permute-start(bf16[128,640]{1,0:T(8,128)(2,1)S(1)} %keys.1.refs_0_), channel_id=1, source_target_pairs={{0,16},{1,17},{2,18},{3,19},{4,20},{5,21},{6,22},{7,23},{8,24},{9,... | collective-permute-start | bytes 491528 | tf_op jit(solution)/shard_map/ppermute | solution.py:31
  7.6 34.9 %copy-start.8 = (s32[128]{0:T(128)S(1)}, s32[128]{0:T(128)}, u32[]{:S(2)}) copy-start(s32[128]{0:T(128)} %param.12) | copy-start | bytes 1540
  7.6 37.1 %copy-start = (bf16[1024,224]{0,1:T(8,128)(2,1)S(1)}, bf16[1024,224]{0,1:T(8,128)(2,1)}, u32[]{:S(2)}) copy-start(bf16[1024,224]{0,1:T(8,128)(2,1)} %param.15) | copy-start | bytes 1376260
  7.6 37.1 %copy-start.3 = (bf16[128,1024]{1,0:T(8,128)(2,1)S(1)}, bf16[128,1024]{1,0:T(8,128)(2,1)}, u32[]{:S(2)}) copy-start(bf16[128,1024]{1,0:T(8,128)(2,1)} %q_nope_in.1) | copy-start | bytes 786436
  7.6 3.2 %collective-permute-start.3 = (bf16[16,16,128]{2,1,0:T(8,128)(2,1)S(1)}, bf16[16,16,128]{2,1,0:T(8,128)(2,1)S(1)}, u32[]{:S(2)}, u32[]{:S(2)}) collective-permute-start(bf16[16,16,128]{2,1,0:T(8,128)(2,1)S(1)} %pad_maximum_fusion.refs_4_), channel_id=1, source_target_pairs={{0,64},{1,65},{2,66},{3,67},{4,68},{5,69},{6,70},{7,71},{8,72},{9,... | collective-permute-start | bytes 196616 | tf_op jit(solution)/shard_map/ppermute | solution.py:31
  7.7 5.6 %collective-permute-start.4 = (bf16[16,16,128]{2,1,0:T(8,128)(2,1)S(1)}, bf16[16,16,128]{2,1,0:T(8,128)(2,1)S(1)}, u32[]{:S(2)}, u32[]{:S(2)}) collective-permute-start(bf16[16,16,128]{2,1,0:T(8,128)(2,1)S(1)} %pad_maximum_fusion.refs_4_), channel_id=1, source_target_pairs={{0,128},{1,129},{2,130},{3,131},{4,132},{5,133},{6,134},{7,135},{8... | collective-permute-start | bytes 196616 | tf_op jit(solution)/shard_map/ppermute | solution.py:31
  10.8 5.5 %collective-permute-start.5 = (bf16[16,16,128]{2,1,0:T(8,128)(2,1)S(1)}, bf16[16,16,128]{2,1,0:T(8,128)(2,1)S(1)}, u32[]{:S(2)}, u32[]{:S(2)}) collective-permute-start(bf16[16,16,128]{2,1,0:T(8,128)(2,1)S(1)} %pad_maximum_fusion.refs_4_), channel_id=1, source_target_pairs={{0,192},{1,193},{2,194},{3,195},{4,196},{5,197},{6,198},{7,199},{8... | collective-permute-start | bytes 196616 | tf_op jit(solution)/shard_map/ppermute | solution.py:31
  16.9 17.8 %collective-permute-start.6 = (bf16[4,128,640]{2,1,0:T(8,128)(2,1)S(1)}, bf16[4,128,640]{2,1,0:T(8,128)(2,1)S(1)}, u32[]{:S(2)}, u32[]{:S(2)}) collective-permute-start(bf16[4,128,640]{2,1,0:T(8,128)(2,1)S(1)} %get-tuple-element.32.row), channel_id=1, source_target_pairs={{0,196},{1,197},{2,198},{3,199},{4,192},{5,193},{6,194},{7,195},{8... | collective-permute-start | bytes 1966088 | tf_op jit(solution)/shard_map/ppermute | solution.py:31
  17.3 17.5 %collective-permute-start.7 = (bf16[4,128,640]{2,1,0:T(8,128)(2,1)S(1)}, bf16[4,128,640]{2,1,0:T(8,128)(2,1)S(1)}, u32[]{:S(2)}, u32[]{:S(2)}) collective-permute-start(bf16[4,128,640]{2,1,0:T(8,128)(2,1)S(1)} %get-tuple-element.32.row), channel_id=1, source_target_pairs={{0,64},{1,65},{2,66},{3,67},{4,68},{5,69},{6,70},{7,71},{8,72},{9,... | collective-permute-start | bytes 1966088 | tf_op jit(solution)/shard_map/ppermute | solution.py:31
  18.7 5.7 %collective-permute-start.8 = (bf16[4,16,16,128]{3,2,1,0:T(8,128)(2,1)S(1)}, bf16[4,16,16,128]{3,2,1,0:T(8,128)(2,1)S(1)}, u32[]{:S(2)}, u32[]{:S(2)}) collective-permute-start(bf16[4,16,16,128]{3,2,1,0:T(8,128)(2,1)S(1)} %get-tuple-element.33.rest_0_), channel_id=1, source_target_pairs={{0,48},{1,49},{2,50},{3,51},{4,52},{5,53},{6,54},{7,55},{8,56},{9,... | collective-permute-start | bytes 786440 | tf_op jit(solution)/shard_map/ppermute | solution.py:31
  20.4 6.8 %collective-permute-start.9 = (bf16[4,16,16,128]{3,2,1,0:T(8,128)(2,1)S(1)}, bf16[4,16,16,128]{3,2,1,0:T(8,128)(2,1)S(1)}, u32[]{:S(2)}, u32[]{:S(2)}) collective-permute-start(bf16[4,16,16,128]{3,2,1,0:T(8,128)(2,1)S(1)} %get-tuple-element.33.rest_0_), channel_id=1, source_target_pairs={{0,32},{1,33},{2,34},{3,35},{4,36},{5,37},{6,38},{7,39},{8,40},{9,... | collective-permute-start | bytes 786440 | tf_op jit(solution)/shard_map/ppermute | solution.py:31
  21.6 13.1 %collective-permute-start.10 = (bf16[4,16,16,128]{3,2,1,0:T(8,128)(2,1)S(1)}, bf16[4,16,16,128]{3,2,1,0:T(8,128)(2,1)S(1)}, u32[]{:S(2)}, u32[]{:S(2)}) collective-permute-start(bf16[4,16,16,128]{3,2,1,0:T(8,128)(2,1)S(1)} %get-tuple-element.33.rest_0_), channel_id=1, source_target_pairs={{0,16},{1,17},{2,18},{3,19},{4,20},{5,21},{6,22},{7,23},{8,24},{9,... | collective-permute-start | bytes 786440 | tf_op jit(solution)/shard_map/ppermute | solution.py:31
  36.5 20.7 %collective-permute-start.14 = (bf16[12,128,640]{2,1,0:T(8,128)(2,1)}, bf16[12,128,640]{2,1,0:T(8,128)(2,1)}, u32[]{:S(2)}, u32[]{:S(2)}) collective-permute-start(bf16[12,128,640]{2,1,0:T(8,128)(2,1)} %get-tuple-element.37.rest_0_), channel_id=1, source_target_pairs={{0,8},{1,9},{2,10},{3,11},{4,12},{5,13},{6,14},{7,15},{8,0},{9,1},... | collective-permute-start | bytes 5898248 | tf_op jit(solution)/shard_map/ppermute | solution.py:31
  39.8 5.0 %collective-permute-start.11 = (bf16[4,4,16,16,128]{4,3,2,1,0:T(8,128)(2,1)S(1)}, bf16[4,4,16,16,128]{4,3,2,1,0:T(8,128)(2,1)S(1)}, u32[]{:S(2)}, u32[]{:S(2)}) collective-permute-start(bf16[4,4,16,16,128]{4,3,2,1,0:T(8,128)(2,1)S(1)} %get-tuple-element.34.mine), channel_id=1, source_target_pairs={{0,8},{1,9},{2,10},{3,11},{4,12},{5,13},{6,14},{7,15},{8,0},{9,1},... | collective-permute-start | bytes 3145736 | tf_op jit(solution)/shard_map/ppermute | solution.py:31
  39.8 9.6 %collective-permute-start.12 = (bf16[2,128,640]{2,1,0:T(8,128)(2,1)}, bf16[2,128,640]{2,1,0:T(8,128)(2,1)S(1)}, u32[]{:S(2)}, u32[]{:S(2)}) collective-permute-start(bf16[2,128,640]{2,1,0:T(8,128)(2,1)} %get-tuple-element.38), channel_id=1, source_target_pairs={{0,196},{1,197},{2,198},{3,199},{4,192},{5,193},{6,194},{7,195},{8... | collective-permute-start | bytes 983048 | tf_op jit(solution)/shard_map/ppermute | solution.py:31
  42.5 8.8 %collective-permute-start.13 = (bf16[2,128,640]{2,1,0:T(8,128)(2,1)}, bf16[2,128,640]{2,1,0:T(8,128)(2,1)S(1)}, u32[]{:S(2)}, u32[]{:S(2)}) collective-permute-start(bf16[2,128,640]{2,1,0:T(8,128)(2,1)} %get-tuple-element.39), channel_id=1, source_target_pairs={{0,64},{1,65},{2,66},{3,67},{4,68},{5,69},{6,70},{7,71},{8,72},{9,... | collective-permute-start | bytes 983048 | tf_op jit(solution)/shard_map/ppermute | solution.py:31
  44.8 0.9 copy-start.5
  48.2 14.5 %copy-start.1 = (bf16[224,1024]{1,0:T(8,128)(2,1)}, bf16[224,1024]{1,0:T(8,128)(2,1)S(1)}, u32[]{:S(2)}) copy-start(bf16[224,1024]{1,0:T(8,128)(2,1)S(1)} %get-tuple-element.44.rest_0_) | copy-start | bytes 1376260
  51.3 4.7 %collective-permute-start.15 = (bf16[2,128,640]{2,1,0:T(8,128)(2,1)S(1)}, bf16[2,128,640]{2,1,0:T(8,128)(2,1)S(1)}, u32[]{:S(2)}, u32[]{:S(2)}) collective-permute-start(bf16[2,128,640]{2,1,0:T(8,128)(2,1)S(1)} %get-tuple-element.41.rest_1_), channel_id=1, source_target_pairs={{0,8},{1,9},{2,10},{3,11},{4,12},{5,13},{6,14},{7,15},{8,0},{9,1},... | collective-permute-start | bytes 983048 | tf_op jit(solution)/shard_map/ppermute | solution.py:31
  53.2 4.0 %collective-permute-start.16 = (bf16[2,128,640]{2,1,0:T(8,128)(2,1)S(1)}, bf16[2,128,640]{2,1,0:T(8,128)(2,1)S(1)}, u32[]{:S(2)}, u32[]{:S(2)}) collective-permute-start(bf16[2,128,640]{2,1,0:T(8,128)(2,1)S(1)} %get-tuple-element.42.rest_2_), channel_id=1, source_target_pairs={{0,8},{1,9},{2,10},{3,11},{4,12},{5,13},{6,14},{7,15},{8,0},{9,1},... | collective-permute-start | bytes 983048 | tf_op jit(solution)/shard_map/ppermute | solution.py:31
  53.3 19.3 %collective-permute-start.17 = (bf16[224,1024]{1,0:T(8,128)(2,1)S(1)}, bf16[224,1024]{1,0:T(8,128)(2,1)S(1)}, u32[]{:S(2)}, u32[]{:S(2)}) collective-permute-start(bf16[224,1024]{1,0:T(8,128)(2,1)S(1)} %get-tuple-element.44.rest_0_), channel_id=1, source_target_pairs={{0,64},{1,65},{2,66},{3,67},{4,68},{5,69},{6,70},{7,71},{8,72},{9,... | collective-permute-start | bytes 1376264 | tf_op jit(solution)/shard_map/ppermute | solution.py:31
  56.0 27.1 %collective-permute-start.22 = (bf16[224,1024]{1,0:T(8,128)(2,1)S(1)}, bf16[224,1024]{1,0:T(8,128)(2,1)S(1)}, u32[]{:S(2)}, u32[]{:S(2)}) collective-permute-start(bf16[224,1024]{1,0:T(8,128)(2,1)S(1)} %get-tuple-element.44.rest_0_), channel_id=1, source_target_pairs={{0,128},{1,129},{2,130},{3,131},{4,132},{5,133},{6,134},{7,135},{8... | collective-permute-start | bytes 1376264 | tf_op jit(solution)/shard_map/ppermute | solution.py:31
  56.0 40.9 %collective-permute-start.23 = (bf16[224,1024]{1,0:T(8,128)(2,1)S(1)}, bf16[224,1024]{1,0:T(8,128)(2,1)S(1)}, u32[]{:S(2)}, u32[]{:S(2)}) collective-permute-start(bf16[224,1024]{1,0:T(8,128)(2,1)S(1)} %get-tuple-element.44.rest_0_), channel_id=1, source_target_pairs={{0,192},{1,193},{2,194},{3,195},{4,196},{5,197},{6,198},{7,199},{8... | collective-permute-start | bytes 1376264 | tf_op jit(solution)/shard_map/ppermute | solution.py:31
  72.6 6.6 %collective-permute-start.18 = (bf16[1024,128]{1,0:T(8,128)(2,1)S(1)}, bf16[1024,128]{1,0:T(8,128)(2,1)S(1)}, u32[]{:S(2)}, u32[]{:S(2)}) collective-permute-start(bf16[1024,128]{1,0:T(8,128)(2,1)S(1)} %hold.1.own), channel_id=1, source_target_pairs={{0,48},{1,49},{2,50},{3,51},{4,52},{5,53},{6,54},{7,55},{8,56},{9,... | collective-permute-start | bytes 786440 | tf_op jit(solution)/shard_map/ppermute | solution.py:31
  74.0 7.5 %collective-permute-start.19 = (bf16[1024,128]{1,0:T(8,128)(2,1)S(1)}, bf16[1024,128]{1,0:T(8,128)(2,1)S(1)}, u32[]{:S(2)}, u32[]{:S(2)}) collective-permute-start(bf16[1024,128]{1,0:T(8,128)(2,1)S(1)} %hold.1.own), channel_id=1, source_target_pairs={{0,16},{1,17},{2,18},{3,19},{4,20},{5,21},{6,22},{7,23},{8,24},{9,... | collective-permute-start | bytes 786440 | tf_op jit(solution)/shard_map/ppermute | solution.py:31
  81.5 15.4 %collective-permute-start.20 = (bf16[512,128]{1,0:T(8,128)(2,1)S(1)}, bf16[512,128]{1,0:T(8,128)(2,1)S(1)}, u32[]{:S(2)}, u32[]{:S(2)}) collective-permute-start(bf16[512,128]{1,0:T(8,128)(2,1)S(1)} %get-tuple-element.45), channel_id=1, source_target_pairs={{0,48},{1,49},{2,50},{3,51},{4,52},{5,53},{6,54},{7,55},{8,56},{9,... | collective-permute-start | bytes 393224 | tf_op jit(solution)/shard_map/ppermute | solution.py:31
  81.9 15.0 %collective-permute-start.21 = (bf16[512,128]{1,0:T(8,128)(2,1)S(1)}, bf16[512,128]{1,0:T(8,128)(2,1)S(1)}, u32[]{:S(2)}, u32[]{:S(2)}) collective-permute-start(bf16[512,128]{1,0:T(8,128)(2,1)S(1)} %get-tuple-element.46), channel_id=1, source_target_pairs={{0,16},{1,17},{2,18},{3,19},{4,20},{5,21},{6,22},{7,23},{8,24},{9,... | collective-permute-start | bytes 393224 | tf_op jit(solution)/shard_map/ppermute | solution.py:31
  97.0 3.6 %collective-permute-start.24 = (bf16[4,1024,128]{2,1,0:T(8,128)(2,1)S(1)}, bf16[4,1024,128]{2,1,0:T(8,128)(2,1)S(1)}, u32[]{:S(2)}, u32[]{:S(2)}) collective-permute-start(bf16[4,1024,128]{2,1,0:T(8,128)(2,1)S(1)} %third.1.mine), channel_id=1, source_target_pairs={{0,8},{1,9},{2,10},{3,11},{4,12},{5,13},{6,14},{7,15},{8,0},{9,1},... | collective-permute-start | bytes 3145736 | tf_op jit(solution)/shard_map/ppermute | solution.py:31
  100.6 1.0 copy-start.2
  104.0 6.9 %collective-permute-start.25 = (bf16[2,224,256]{2,1,0:T(8,128)(2,1)S(1)}, bf16[2,224,256]{2,1,0:T(8,128)(2,1)S(1)}, u32[]{:S(2)}, u32[]{:S(2)}) collective-permute-start(bf16[2,224,256]{2,1,0:T(8,128)(2,1)S(1)} %get-tuple-element.48), channel_id=1, source_target_pairs={{0,1},{1,2},{2,3},{3,0},{4,5},{5,6},{6,7},{7,4},{8,9},{9,10},{10,1... | collective-permute-start | bytes 688136 | tf_op jit(solution)/shard_map/ppermute | solution.py:31
  105.4 6.5 %collective-permute-start.26 = (bf16[2,224,256]{2,1,0:T(8,128)(2,1)S(1)}, bf16[2,224,256]{2,1,0:T(8,128)(2,1)S(1)}, u32[]{:S(2)}, u32[]{:S(2)}) collective-permute-start(bf16[2,224,256]{2,1,0:T(8,128)(2,1)S(1)} %get-tuple-element.49), channel_id=1, source_target_pairs={{0,3},{1,0},{2,1},{3,2},{4,7},{5,4},{6,5},{7,6},{8,11},{9,8},{10,9... | collective-permute-start | bytes 688136 | tf_op jit(solution)/shard_map/ppermute | solution.py:31
  112.0 5.6 %collective-permute-start.27 = (bf16[2,224,256]{2,1,0:T(8,128)(2,1)S(1)}, bf16[2,224,256]{2,1,0:T(8,128)(2,1)S(1)}, u32[]{:S(2)}, u32[]{:S(2)}) collective-permute-start(bf16[2,224,256]{2,1,0:T(8,128)(2,1)S(1)} %get-tuple-element.50), channel_id=1, source_target_pairs={{0,1},{1,2},{2,3},{3,0},{4,5},{5,6},{6,7},{7,4},{8,9},{9,10},{10,1... | collective-permute-start | bytes 688136 | tf_op jit(solution)/shard_map/ppermute | solution.py:31
  113.1 6.0 %collective-permute-start.28 = (bf16[2,224,256]{2,1,0:T(8,128)(2,1)S(1)}, bf16[2,224,256]{2,1,0:T(8,128)(2,1)S(1)}, u32[]{:S(2)}, u32[]{:S(2)}) collective-permute-start(bf16[2,224,256]{2,1,0:T(8,128)(2,1)S(1)} %get-tuple-element.52), channel_id=1, source_target_pairs={{0,3},{1,0},{2,1},{3,2},{4,7},{5,4},{6,5},{7,6},{8,11},{9,8},{10,9... | collective-permute-start | bytes 688136 | tf_op jit(solution)/shard_map/ppermute | solution.py:31
  119.8 9.4 %collective-permute-start.31 = (bf16[2,224,256]{2,1,0:T(8,128)(2,1)S(1)}, bf16[2,224,256]{2,1,0:T(8,128)(2,1)S(1)}, u32[]{:S(2)}, u32[]{:S(2)}) collective-permute-start(bf16[2,224,256]{2,1,0:T(8,128)(2,1)S(1)} %get-tuple-element.55), channel_id=1, source_target_pairs={{0,1},{1,2},{2,3},{3,0},{4,5},{5,6},{6,7},{7,4},{8,9},{9,10},{10,1... | collective-permute-start | bytes 688136 | tf_op jit(solution)/shard_map/ppermute | solution.py:31
  121.3 7.9 %collective-permute-start.32 = (bf16[2,224,256]{2,1,0:T(8,128)(2,1)S(1)}, bf16[2,224,256]{2,1,0:T(8,128)(2,1)S(1)}, u32[]{:S(2)}, u32[]{:S(2)}) collective-permute-start(bf16[2,224,256]{2,1,0:T(8,128)(2,1)S(1)} %get-tuple-element.56), channel_id=1, source_target_pairs={{0,3},{1,0},{2,1},{3,2},{4,7},{5,4},{6,5},{7,6},{8,11},{9,8},{10,9... | collective-permute-start | bytes 688136 | tf_op jit(solution)/shard_map/ppermute | solution.py:31
  121.4 14.4 %collective-permute-start.29 = (bf16[224,256]{1,0:T(8,128)(2,1)S(1)}, bf16[224,256]{1,0:T(8,128)(2,1)S(1)}, u32[]{:S(2)}, u32[]{:S(2)}) collective-permute-start(bf16[224,256]{1,0:T(8,128)(2,1)S(1)} %get-tuple-element.53), channel_id=1, source_target_pairs={{0,4},{1,36},{2,6},{3,38},{4,0},{5,32},{6,2},{7,34},{8,12},{9,44},... | collective-permute-start | bytes 344072 | tf_op jit(solution)/shard_map/ppermute | solution.py:31
  125.7 12.0 %collective-permute-start.30 = (bf16[224,256]{1,0:T(8,128)(2,1)S(1)}, bf16[224,256]{1,0:T(8,128)(2,1)S(1)}, u32[]{:S(2)}, u32[]{:S(2)}) collective-permute-start(bf16[224,256]{1,0:T(8,128)(2,1)S(1)} %get-tuple-element.54), channel_id=1, source_target_pairs={{0,20},{1,52},{2,22},{3,54},{4,16},{5,48},{6,18},{7,50},{8,28},{9,... | collective-permute-start | bytes 344072 | tf_op jit(solution)/shard_map/ppermute | solution.py:31
  129.9 9.2 %collective-permute-start.33 = (bf16[224,256]{1,0:T(8,128)(2,1)S(1)}, bf16[224,256]{1,0:T(8,128)(2,1)S(1)}, u32[]{:S(2)}, u32[]{:S(2)}) collective-permute-start(bf16[224,256]{1,0:T(8,128)(2,1)S(1)} %get-tuple-element.57), channel_id=1, source_target_pairs={{0,0},{1,32},{2,2},{3,34},{4,4},{5,36},{6,6},{7,38},{8,8},{9,40},{... | collective-permute-start | bytes 344072 | tf_op jit(solution)/shard_map/ppermute | solution.py:31
  134.5 7.9 %collective-permute-start.34 = (bf16[224,256]{1,0:T(8,128)(2,1)S(1)}, bf16[224,256]{1,0:T(8,128)(2,1)S(1)}, u32[]{:S(2)}, u32[]{:S(2)}) collective-permute-start(bf16[224,256]{1,0:T(8,128)(2,1)S(1)} %get-tuple-element.58), channel_id=1, source_target_pairs={{0,16},{1,48},{2,18},{3,50},{4,20},{5,52},{6,22},{7,54},{8,24},{9,... | collective-permute-start | bytes 344072 | tf_op jit(solution)/shard_map/ppermute | solution.py:31
  142.5 3.4 %collective-permute-start.35 = (bf16[2,224,128]{2,1,0:T(8,128)(2,1)S(1)}, bf16[2,224,128]{2,1,0:T(8,128)(2,1)S(1)}, u32[]{:S(2)}, u32[]{:S(2)}) collective-permute-start(bf16[2,224,128]{2,1,0:T(8,128)(2,1)S(1)} %get-tuple-element.60), channel_id=1, source_target_pairs={{0,8},{1,9},{2,10},{3,11},{4,12},{5,13},{6,14},{7,15},{8,0},{9,1},... | collective-permute-start | bytes 344072 | tf_op jit(solution)/shard_map/ppermute | solution.py:31

commit v3 on v2

--- a/solution.py
+++ b/solution.py
@@ -91,19 +91,15 @@
     return copies
 
 
-def keys_kernel(latent_in, rope_in, docs_in, out, rope_key, docs, sems):
-    copies = fetched(
-        [(latent_in, out.at[:, 0:KV_RANK]), (rope_in, rope_key), (docs_in, docs)], sems
-    )
+def keys_kernel(latent_in, tail_in, out, sems):
+    copies = fetched([(latent_in, out.at[:, 0:KV_RANK])], sems)
+    tail = jnp.transpose(tail_in[...].astype(jnp.float32))
+    lane = lax.broadcasted_iota(jnp.int32, (128, 128), 1)
+    same = (lane - ROPE_DIM).astype(jnp.float32) == tail
+    marks = jnp.where(same, 1.0, jnp.where(lane == ROPE_DIM + 4, tail, 0.0))
+    out[:, KV_RANK:WIDE] = jnp.where(lane < ROPE_DIM, tail, marks).astype(jnp.bfloat16)
     for copy in copies:
         copy.wait()
-    rope = jnp.transpose(rope_key[...].astype(jnp.float32))
-    doc = doc_columns(docs[...])
-    lane = lax.broadcasted_iota(jnp.int32, (128, 128), 1)
-    place = (lane - ROPE_DIM).astype(jnp.float32)
-    tail = jnp.where(place == doc, 1.0, jnp.where(lane == ROPE_DIM + 4, doc, 0.0))
-    tail = jnp.where(lane < ROPE_DIM, jnp.concatenate([rope, rope], axis=1), tail)
-    out[:, KV_RANK:WIDE] = tail.astype(jnp.bfloat16)
 
 
 def first_kernel(*refs):
@@ -366,18 +362,16 @@
     place = jnp.stack([z, x, core, ctx, segment_ids[0]]).astype(jnp.int32)
     docs = segment_ids.reshape(1, 128)
 
+    tail = jnp.broadcast_to(docs.astype(jnp.bfloat16), (ROPE_DIM, 128))
+    tail = jnp.concatenate([rope_key.T, tail])
     (block,) = call(
         keys_kernel,
         [((128, WIDE), jnp.bfloat16)],
-        [HBM] * 3,
-        [
-            pltpu.VMEM((ROPE_DIM, 128), jnp.bfloat16),
-            pltpu.VMEM((1, 128), jnp.int32),
-            pltpu.SemaphoreType.DMA((3,)),
-        ],
+        [HBM, VMEM],
+        [pltpu.SemaphoreType.DMA((1,))],
         limit=8,
         name="keys",
-    )(latent, rope_key.T, docs)
+    )(latent, tail)
     up = w_uk.reshape(8, 4, 4, 128).transpose(0, 2, 1, 3).reshape(8, 16, 128)
     up = jnp.concatenate([up, w_uv])
     ring = gather_ring(block)

time: 148 us -> 147 us (level)
  waiting for transfers between devices: 73.2 us -> 71.5 us
  Pallas kernels: 17.7 us -> 19.3 us
    pallas_call x1, Pallas kernels: 5.45 us -> 7.21 us  [per_device(): call(attention_kernel, [((1024, 128), jnp.bfloat16), ((8, 128), jnp.float...]
    ppermute x36, waiting for transfers between devices: 73.2 us -> 71.5 us  [moved(): return lax.ppermute(array, AXES, pairs)]
    unnamed x18 -> x14, local copies, waits for them, and re-layouts: 4.21 us -> 2.85 us
  transfers between devices with their start and end apart: 36 -> 36, of which waited for: 22 -> 22; matrix products, arithmetic and copies ran while one was open for 1% -> 1% of each run, Pallas kernels for 7% -> 9%
where the time goes in v3:
time: 147 us
  waiting for transfers between devices  71.5 us (49%)
  starting transfers between devices  50.3 us (34%)
  Pallas kernels  19.3 us (13%)
  local copies, waits for them, and re-layouts  3.06 us (2%)
  other arithmetic  2.24 us (2%)
    ppermute x36, waiting for transfers between devices, moved(): return lax.ppermute(array, AXES, pairs)  71.5 us
    ppermute x36, starting transfers between devices, moved(): return lax.ppermute(array, AXES, pairs)  50.3 us
    pallas_call x1, Pallas kernels, per_device(): call(attention_kernel, [((1024, 128), jnp.bfloat16), ((8, 128), jnp.float...  7.21 us
  transfers between devices with their start and end apart: 36, of which 22 were waited for; matrix products, arithmetic and copies ran while one was open for 1% of the time, Pallas kernels for 9%

profile of v3, /device:TPU:41, one launch (start us, length us, event | category | flops | bytes accessed | tf_op | source)
XLA Modules:
  0.0 147.1 jit_solution(3060034457403189110)
XLA Ops:
  0.6 0.7 convert_element_type.4
  1.3 0.7 pad_maximum_fusion.1.tail_in
  2.0 0.9 copy-done.4
  3.1 2.6 %collective-permute-start = (bf16[128,640]{1,0:T(8,128)(2,1)S(1)}, bf16[128,640]{1,0:T(8,128)(2,1)S(1)}, u32[]{:S(2)}, u32[]{:S(2)}) collective-permute-start(bf16[128,640]{1,0:T(8,128)(2,1)S(1)} %keys.1.refs_0_), channel_id=1, source_target_pairs={{0,48},{1,49},{2,50},{3,51},{4,52},{5,53},{6,54},{7,55},{8,56},{9,... | collective-permute-start | bytes 491528 | tf_op jit(solution)/shard_map/ppermute | solution.py:31
  5.6 0.5 collective-permute-start.1
  6.1 0.6 collective-permute-start.2
  6.7 0.8 pad_maximum_fusion.refs_4_
  7.7 3.1 %collective-permute-start.4 = (bf16[16,16,128]{2,1,0:T(8,128)(2,1)S(1)}, bf16[16,16,128]{2,1,0:T(8,128)(2,1)S(1)}, u32[]{:S(2)}, u32[]{:S(2)}) collective-permute-start(bf16[16,16,128]{2,1,0:T(8,128)(2,1)S(1)} %pad_maximum_fusion.refs_4_), channel_id=1, source_target_pairs={{0,128},{1,129},{2,130},{3,131},{4,132},{5,133},{6,134},{7,135},{8... | collective-permute-start | bytes 196616 | tf_op jit(solution)/shard_map/ppermute | solution.py:31
  10.8 1.8 %collective-permute-start.5 = (bf16[16,16,128]{2,1,0:T(8,128)(2,1)S(1)}, bf16[16,16,128]{2,1,0:T(8,128)(2,1)S(1)}, u32[]{:S(2)}, u32[]{:S(2)}) collective-permute-start(bf16[16,16,128]{2,1,0:T(8,128)(2,1)S(1)} %pad_maximum_fusion.refs_4_), channel_id=1, source_target_pairs={{0,192},{1,193},{2,194},{3,195},{4,196},{5,197},{6,198},{7,199},{8... | collective-permute-start | bytes 196616 | tf_op jit(solution)/shard_map/ppermute | solution.py:31
  12.6 0.7 collective-permute-done.4.refs_6_
  13.3 3.0 %collective-permute-done.5.refs_7_ = bf16[16,16,128]{2,1,0:T(8,128)(2,1)S(1)} collective-permute-done((bf16[16,16,128]{2,1,0:T(8,128)(2,1)S(1)}, bf16[16,16,128]{2,1,0:T(8,128)(2,1)S(1)}, u32[]{:S(2)}, u32[]{:S(2)}) %collective-permute-start.5) | collective-permute-done | bytes 65568 | tf_op jit(solution)/shard_map/ppermute | solution.py:31
  16.3 0.4 collective-permute-done.2.refs_3_
  16.8 0.4 collective-permute-start.6
  17.2 1.4 collective-permute-start.7
  18.6 1.7 %collective-permute-start.8 = (bf16[4,16,16,128]{3,2,1,0:T(8,128)(2,1)S(1)}, bf16[4,16,16,128]{3,2,1,0:T(8,128)(2,1)S(1)}, u32[]{:S(2)}, u32[]{:S(2)}) collective-permute-start(bf16[4,16,16,128]{3,2,1,0:T(8,128)(2,1)S(1)} %get-tuple-element.33.rest_0_), channel_id=1, source_target_pairs={{0,48},{1,49},{2,50},{3,51},{4,52},{5,53},{6,54},{7,55},{8,56},{9,... | collective-permute-start | bytes 786440 | tf_op jit(solution)/shard_map/ppermute | solution.py:31
  20.3 1.2 collective-permute-start.9
  21.5 2.8 %collective-permute-done.8.rest_1_ = bf16[4,16,16,128]{3,2,1,0:T(8,128)(2,1)S(1)} collective-permute-done((bf16[4,16,16,128]{3,2,1,0:T(8,128)(2,1)S(1)}, bf16[4,16,16,128]{3,2,1,0:T(8,128)(2,1)S(1)}, u32[]{:S(2)}, u32[]{:S(2)}) %collective-permute-start.8) | collective-permute-done | bytes 262176 | tf_op jit(solution)/shard_map/ppermute | solution.py:31
  24.4 2.8 %collective-permute-done.9.rest_2_ = bf16[4,16,16,128]{3,2,1,0:T(8,128)(2,1)S(1)} collective-permute-done((bf16[4,16,16,128]{3,2,1,0:T(8,128)(2,1)S(1)}, bf16[4,16,16,128]{3,2,1,0:T(8,128)(2,1)S(1)}, u32[]{:S(2)}, u32[]{:S(2)}) %collective-permute-start.9) | collective-permute-done | bytes 262176 | tf_op jit(solution)/shard_map/ppermute | solution.py:31
  27.1 7.5 %collective-permute-done.10.rest_3_ = bf16[4,16,16,128]{3,2,1,0:T(8,128)(2,1)S(1)} collective-permute-done((bf16[4,16,16,128]{3,2,1,0:T(8,128)(2,1)S(1)}, bf16[4,16,16,128]{3,2,1,0:T(8,128)(2,1)S(1)}, u32[]{:S(2)}, u32[]{:S(2)}) %collective-permute-start.10) | collective-permute-done | bytes 262176 | tf_op jit(solution)/shard_map/ppermute | solution.py:31
  34.7 1.7 %second.1 = (bf16[2,128,640]{2,1,0:T(8,128)(2,1)}, bf16[2,128,640]{2,1,0:T(8,128)(2,1)}, bf16[12,128,640]{2,1,0:T(8,128)(2,1)}, bf16[4,4,16,16,128]{4,3,2,1,0:T(8,128)(2,1)S(1)}) custom-call(bf16[4,128,640]{2,1,0:T(8,128)(2,1)S(1)} %get-tuple-element.32.row, bf16[4,128,640]{2,1,0:T(8,128)(2,1)S(1)} %collective-permute-done.6.plus, ...), custom_call_target="tpu_custom_call" | custom-call | bytes 3145728 | tf_op jit(solution)/shard_map/second/pallas_call | solution.py:387
  36.4 3.3 %collective-permute-start.14 = (bf16[12,128,640]{2,1,0:T(8,128)(2,1)}, bf16[12,128,640]{2,1,0:T(8,128)(2,1)}, u32[]{:S(2)}, u32[]{:S(2)}) collective-permute-start(bf16[12,128,640]{2,1,0:T(8,128)(2,1)} %get-tuple-element.37.rest_0_), channel_id=1, source_target_pairs={{0,8},{1,9},{2,10},{3,11},{4,12},{5,13},{6,14},{7,15},{8,0},{9,1},... | collective-permute-start | bytes 5898248 | tf_op jit(solution)/shard_map/ppermute | solution.py:31
  39.7 2.7 %collective-permute-start.12 = (bf16[2,128,640]{2,1,0:T(8,128)(2,1)}, bf16[2,128,640]{2,1,0:T(8,128)(2,1)S(1)}, u32[]{:S(2)}, u32[]{:S(2)}) collective-permute-start(bf16[2,128,640]{2,1,0:T(8,128)(2,1)} %get-tuple-element.38), channel_id=1, source_target_pairs={{0,196},{1,197},{2,198},{3,199},{4,192},{5,193},{6,194},{7,195},{8... | collective-permute-start | bytes 983048 | tf_op jit(solution)/shard_map/ppermute | solution.py:31
  42.5 2.2 %collective-permute-done.11.theirs = bf16[4,4,16,16,128]{4,3,2,1,0:T(8,128)(2,1)S(1)} collective-permute-done((bf16[4,4,16,16,128]{4,3,2,1,0:T(8,128)(2,1)S(1)}, bf16[4,4,16,16,128]{4,3,2,1,0:T(8,128)(2,1)S(1)}, u32[]{:S(2)}, u32[]{:S(2)}) %collective-permute-start.11) | collective-permute-done | bytes 1048608 | tf_op jit(solution)/shard_map/ppermute | solution.py:31
  44.7 0.9 copy-done.5
  45.6 2.5 %queries.1 = (bf16[1024,640]{1,0:T(8,128)(2,1)S(1)}, bf16[8,512,128]{2,1,0:T(8,128)(2,1)S(1)}, bf16[224,1024]{1,0:T(8,128)(2,1)S(1)}, f32[8,128]{1,0:T(8,128)S(1)}) custom-call(s32[5]{0:T(128)S(1)} %stack.50.place, bf16[128,1024]{1,0:T(8,128)(2,1)S(1)} %copy-done.3, bf16[128,512]{1,0:T(8,128)(2,1)S(1)} %copy-done.5, bf16[224,1024]{1,0:T(8,128)(2,1)S(1)} %bitcast.20, ...), custom_call_target="tpu_custom_call" | custom-call | flops 700000000 | bytes 3145728 | tf_op jit(solution)/shard_map/queries/pallas_call | solution.py:402
  48.1 1.2 collective-permute-done.12.low_in
  49.3 1.9 %collective-permute-done.13.high_in = bf16[2,128,640]{2,1,0:T(8,128)(2,1)S(1)} collective-permute-done((bf16[2,128,640]{2,1,0:T(8,128)(2,1)}, bf16[2,128,640]{2,1,0:T(8,128)(2,1)S(1)}, u32[]{:S(2)}, u32[]{:S(2)}) %collective-permute-start.13) | collective-permute-done | bytes 327712 | tf_op jit(solution)/shard_map/ppermute | solution.py:31
  51.2 1.9 %collective-permute-start.15 = (bf16[2,128,640]{2,1,0:T(8,128)(2,1)S(1)}, bf16[2,128,640]{2,1,0:T(8,128)(2,1)S(1)}, u32[]{:S(2)}, u32[]{:S(2)}) collective-permute-start(bf16[2,128,640]{2,1,0:T(8,128)(2,1)S(1)} %get-tuple-element.41.rest_1_), channel_id=1, source_target_pairs={{0,8},{1,9},{2,10},{3,11},{4,12},{5,13},{6,14},{7,15},{8,0},{9,1},... | collective-permute-start | bytes 983048 | tf_op jit(solution)/shard_map/ppermute | solution.py:31
  53.2 2.7 %collective-permute-start.17 = (bf16[224,1024]{1,0:T(8,128)(2,1)S(1)}, bf16[224,1024]{1,0:T(8,128)(2,1)S(1)}, u32[]{:S(2)}, u32[]{:S(2)}) collective-permute-start(bf16[224,1024]{1,0:T(8,128)(2,1)S(1)} %get-tuple-element.44.rest_0_), channel_id=1, source_target_pairs={{0,64},{1,65},{2,66},{3,67},{4,68},{5,69},{6,70},{7,71},{8,72},{9,... | collective-permute-start | bytes 1376264 | tf_op jit(solution)/shard_map/ppermute | solution.py:31
  55.9 1.2 collective-permute-start.23
  57.1 7.2 %attention.1 = (bf16[1024,128]{1,0:T(8,128)(2,1)S(1)}, f32[8,128]{1,0:T(8,128)}) custom-call(s32[5]{0:T(128)S(1)} %stack.50.place, bf16[1024,640]{1,0:T(8,128)(2,1)S(1)} %get-tuple-element.35.query, bf16[8,512,128]{2,1,0:T(8,128)(2,1)S(1)} %get-tuple-element.36.up_value, bf16[12,128,640]{2,1,0:T(8,128)(2,1)} %get-tuple-element.37.rest_0_, ...), custom_call_target="tpu_custom_call" | custom-call | flops 10000000000 | bytes 3145728 | tf_op jit(solution)/shard_map/attention/pallas_call | solution.py:431
  64.3 8.2 %collective-permute-done.17.weight.rest_1_ = bf16[224,1024]{1,0:T(8,128)(2,1)S(1)} collective-permute-done((bf16[224,1024]{1,0:T(8,128)(2,1)S(1)}, bf16[224,1024]{1,0:T(8,128)(2,1)S(1)}, u32[]{:S(2)}, u32[]{:S(2)}) %collective-permute-start.17) | collective-permute-done | bytes 458784 | tf_op jit(solution)/shard_map/ppermute | solution.py:31
  72.5 1.4 collective-permute-start.18
  74.1 5.1 %collective-permute-done.18.right = bf16[1024,128]{1,0:T(8,128)(2,1)S(1)} collective-permute-done((bf16[1024,128]{1,0:T(8,128)(2,1)S(1)}, bf16[1024,128]{1,0:T(8,128)(2,1)S(1)}, u32[]{:S(2)}, u32[]{:S(2)}) %collective-permute-start.18) | collective-permute-done | bytes 262176 | tf_op jit(solution)/shard_map/ppermute | solution.py:31
  79.2 2.2 %collective-permute-done.19.left = bf16[1024,128]{1,0:T(8,128)(2,1)S(1)} collective-permute-done((bf16[1024,128]{1,0:T(8,128)(2,1)S(1)}, bf16[1024,128]{1,0:T(8,128)(2,1)S(1)}, u32[]{:S(2)}, u32[]{:S(2)}) %collective-permute-start.19) | collective-permute-done | bytes 262176 | tf_op jit(solution)/shard_map/ppermute | solution.py:31
  81.4 0.4 collective-permute-start.20
  81.8 1.2 collective-permute-start.21
  83.0 13.8 %collective-permute-done.23.rest_1_.rest_3_ = bf16[224,1024]{1,0:T(8,128)(2,1)S(1)} collective-permute-done((bf16[224,1024]{1,0:T(8,128)(2,1)S(1)}, bf16[224,1024]{1,0:T(8,128)(2,1)S(1)}, u32[]{:S(2)}, u32[]{:S(2)}) %collective-permute-start.23) | collective-permute-done | bytes 458784 | tf_op jit(solution)/shard_map/ppermute | solution.py:31
  96.9 1.3 collective-permute-start.24
  98.3 2.2 %collective-permute-done.24.theirs = bf16[4,1024,128]{2,1,0:T(8,128)(2,1)S(1)} collective-permute-done((bf16[4,1024,128]{2,1,0:T(8,128)(2,1)S(1)}, bf16[4,1024,128]{2,1,0:T(8,128)(2,1)S(1)}, u32[]{:S(2)}, u32[]{:S(2)}) %collective-permute-start.24) | collective-permute-done | bytes 1048608 | tf_op jit(solution)/shard_map/ppermute | solution.py:31
  100.5 1.0 copy-done.2
  101.5 2.3 %project.1 = (bf16[2,224,256]{2,1,0:T(8,128)(2,1)S(1)}, bf16[2,224,256]{2,1,0:T(8,128)(2,1)S(1)}, bf16[2,2,224,1024]{3,2,1,0:T(8,128)(2,1)S(1)}) custom-call(s32[6]{0:T(128)S(1)} %stack.48.place, bf16[4,1024,128]{2,1,0:T(8,128)(2,1)S(1)} %third.1.mine, bf16[4,1024,128]{2,1,0:T(8,128)(2,1)S(1)} %collective-permute-done.24.theirs, ...), custom_call_target="tpu_custom_call" | custom-call | flops 470000000 | bytes 3145728 | tf_op jit(solution)/shard_map/project/pallas_call | solution.py:461
  103.9 1.4 collective-permute-start.25
  105.3 0.2 collective-permute-start.26
  105.4 2.2 %others.1.terms = bf16[6,2,224,256]{3,2,1,0:T(8,128)(2,1)S(1)} custom-call(s32[6]{0:T(128)S(1)} %stack.48.place, bf16[4,1024,128]{2,1,0:T(8,128)(2,1)S(1)} %third.1.mine, bf16[4,1024,128]{2,1,0:T(8,128)(2,1)S(1)} %collective-permute-done.24.theirs, bf16[2,2,224,1024]{3,2,1,0:T(8,128)(2,1)S(1)} %get-tuple-element.47.weights), custom_call_target="tpu_custom_call" | custom-call | flops 1410000000 | bytes 3145728 | tf_op jit(solution)/shard_map/others/pallas_call | solution.py:470
  107.6 3.2 %collective-permute-done.25.far_give = bf16[2,224,256]{2,1,0:T(8,128)(2,1)S(1)} collective-permute-done((bf16[2,224,256]{2,1,0:T(8,128)(2,1)S(1)}, bf16[2,224,256]{2,1,0:T(8,128)(2,1)S(1)}, u32[]{:S(2)}, u32[]{:S(2)}) %collective-permute-start.25) | collective-permute-done | bytes 229408 | tf_op jit(solution)/shard_map/ppermute | solution.py:31
  110.8 1.0 collective-permute-done.26.left_give
  111.9 1.1 collective-permute-start.27
  113.0 0.5 collective-permute-start.28
  113.5 4.0 %collective-permute-done.27.left = bf16[2,224,256]{2,1,0:T(8,128)(2,1)S(1)} collective-permute-done((bf16[2,224,256]{2,1,0:T(8,128)(2,1)S(1)}, bf16[2,224,256]{2,1,0:T(8,128)(2,1)S(1)}, u32[]{:S(2)}, u32[]{:S(2)}) %collective-permute-start.27) | collective-permute-done | bytes 229408 | tf_op jit(solution)/shard_map/ppermute | solution.py:31
  117.5 1.5 %collective-permute-done.28.far_keep = bf16[2,224,256]{2,1,0:T(8,128)(2,1)S(1)} collective-permute-done((bf16[2,224,256]{2,1,0:T(8,128)(2,1)S(1)}, bf16[2,224,256]{2,1,0:T(8,128)(2,1)S(1)}, u32[]{:S(2)}, u32[]{:S(2)}) %collective-permute-start.28) | collective-permute-done | bytes 229408 | tf_op jit(solution)/shard_map/ppermute | solution.py:31
  119.0 0.7 give.1
  119.8 1.5 %collective-permute-start.31 = (bf16[2,224,256]{2,1,0:T(8,128)(2,1)S(1)}, bf16[2,224,256]{2,1,0:T(8,128)(2,1)S(1)}, u32[]{:S(2)}, u32[]{:S(2)}) collective-permute-start(bf16[2,224,256]{2,1,0:T(8,128)(2,1)S(1)} %get-tuple-element.55), channel_id=1, source_target_pairs={{0,1},{1,2},{2,3},{3,0},{4,5},{5,6},{6,7},{7,4},{8,9},{9,10},{10,1... | collective-permute-start | bytes 688136 | tf_op jit(solution)/shard_map/ppermute | solution.py:31
  121.3 4.3 %collective-permute-start.29 = (bf16[224,256]{1,0:T(8,128)(2,1)S(1)}, bf16[224,256]{1,0:T(8,128)(2,1)S(1)}, u32[]{:S(2)}, u32[]{:S(2)}) collective-permute-start(bf16[224,256]{1,0:T(8,128)(2,1)S(1)} %get-tuple-element.53), channel_id=1, source_target_pairs={{0,4},{1,36},{2,6},{3,38},{4,0},{5,32},{6,2},{7,34},{8,12},{9,44},... | collective-permute-start | bytes 344072 | tf_op jit(solution)/shard_map/ppermute | solution.py:31
  125.6 3.5 %collective-permute-start.30 = (bf16[224,256]{1,0:T(8,128)(2,1)S(1)}, bf16[224,256]{1,0:T(8,128)(2,1)S(1)}, u32[]{:S(2)}, u32[]{:S(2)}) collective-permute-start(bf16[224,256]{1,0:T(8,128)(2,1)S(1)} %get-tuple-element.54), channel_id=1, source_target_pairs={{0,20},{1,52},{2,22},{3,54},{4,16},{5,48},{6,18},{7,50},{8,28},{9,... | collective-permute-start | bytes 344072 | tf_op jit(solution)/shard_map/ppermute | solution.py:31
  129.1 0.7 keep.1
  129.8 4.5 %collective-permute-start.33 = (bf16[224,256]{1,0:T(8,128)(2,1)S(1)}, bf16[224,256]{1,0:T(8,128)(2,1)S(1)}, u32[]{:S(2)}, u32[]{:S(2)}) collective-permute-start(bf16[224,256]{1,0:T(8,128)(2,1)S(1)} %get-tuple-element.57), channel_id=1, source_target_pairs={{0,0},{1,32},{2,2},{3,34},{4,4},{5,36},{6,6},{7,38},{8,8},{9,40},{... | collective-permute-start | bytes 344072 | tf_op jit(solution)/shard_map/ppermute | solution.py:31
  134.4 1.3 collective-permute-start.34
  135.7 2.3 %collective-permute-done.30.give_cross = bf16[224,256]{1,0:T(8,128)(2,1)S(1)} collective-permute-done((bf16[224,256]{1,0:T(8,128)(2,1)S(1)}, bf16[224,256]{1,0:T(8,128)(2,1)S(1)}, u32[]{:S(2)}, u32[]{:S(2)}) %collective-permute-start.30) | collective-permute-done | bytes 114720 | tf_op jit(solution)/shard_map/ppermute | solution.py:31
  137.9 1.1 collective-permute-done.33.keep_same
  139.0 3.3 %collective-permute-done.34.keep_cross = bf16[224,256]{1,0:T(8,128)(2,1)S(1)} collective-permute-done((bf16[224,256]{1,0:T(8,128)(2,1)S(1)}, bf16[224,256]{1,0:T(8,128)(2,1)S(1)}, u32[]{:S(2)}, u32[]{:S(2)}) %collective-permute-start.34) | collective-permute-done | bytes 114720 | tf_op jit(solution)/shard_map/ppermute | solution.py:31
  142.4 2.3 %collective-permute-start.35 = (bf16[2,224,128]{2,1,0:T(8,128)(2,1)S(1)}, bf16[2,224,128]{2,1,0:T(8,128)(2,1)S(1)}, u32[]{:S(2)}, u32[]{:S(2)}) collective-permute-start(bf16[2,224,128]{2,1,0:T(8,128)(2,1)S(1)} %get-tuple-element.60), channel_id=1, source_target_pairs={{0,8},{1,9},{2,10},{3,11},{4,12},{5,13},{6,14},{7,15},{8,0},{9,1},... | collective-permute-start | bytes 344072 | tf_op jit(solution)/shard_map/ppermute | solution.py:31
  144.8 1.0 collective-permute-done.35.theirs
  145.7 1.4 finish.1
  (45 shorter events, 1.3 us)
Async XLA Ops:
  2.0 0.9 copy-start.4
  3.1 13.2 %collective-permute-start = (bf16[128,640]{1,0:T(8,128)(2,1)S(1)}, bf16[128,640]{1,0:T(8,128)(2,1)S(1)}, u32[]{:S(2)}, u32[]{:S(2)}) collective-permute-start(bf16[128,640]{1,0:T(8,128)(2,1)S(1)} %keys.1.refs_0_), channel_id=1, source_target_pairs={{0,48},{1,49},{2,50},{3,51},{4,52},{5,53},{6,54},{7,55},{8,56},{9,... | collective-permute-start | bytes 491528 | tf_op jit(solution)/shard_map/ppermute | solution.py:31
  5.6 10.7 %collective-permute-start.1 = (bf16[128,640]{1,0:T(8,128)(2,1)S(1)}, bf16[128,640]{1,0:T(8,128)(2,1)S(1)}, u32[]{:S(2)}, u32[]{:S(2)}) collective-permute-start(bf16[128,640]{1,0:T(8,128)(2,1)S(1)} %keys.1.refs_0_), channel_id=1, source_target_pairs={{0,32},{1,33},{2,34},{3,35},{4,36},{5,37},{6,38},{7,39},{8,40},{9,... | collective-permute-start | bytes 491528 | tf_op jit(solution)/shard_map/ppermute | solution.py:31
  6.1 10.6 %collective-permute-start.2 = (bf16[128,640]{1,0:T(8,128)(2,1)S(1)}, bf16[128,640]{1,0:T(8,128)(2,1)S(1)}, u32[]{:S(2)}, u32[]{:S(2)}) collective-permute-start(bf16[128,640]{1,0:T(8,128)(2,1)S(1)} %keys.1.refs_0_), channel_id=1, source_target_pairs={{0,16},{1,17},{2,18},{3,19},{4,20},{5,21},{6,22},{7,23},{8,24},{9,... | collective-permute-start | bytes 491528 | tf_op jit(solution)/shard_map/ppermute | solution.py:31
  7.5 34.9 %copy-start.6 = (s32[128]{0:T(128)S(1)}, s32[128]{0:T(128)}, u32[]{:S(2)}) copy-start(s32[128]{0:T(128)} %param.12) | copy-start | bytes 1540
  7.5 37.1 %copy-start = (bf16[1024,224]{0,1:T(8,128)(2,1)S(1)}, bf16[1024,224]{0,1:T(8,128)(2,1)}, u32[]{:S(2)}) copy-start(bf16[1024,224]{0,1:T(8,128)(2,1)} %param.15) | copy-start | bytes 1376260
  7.5 37.1 %copy-start.3 = (bf16[128,1024]{1,0:T(8,128)(2,1)S(1)}, bf16[128,1024]{1,0:T(8,128)(2,1)}, u32[]{:S(2)}) copy-start(bf16[128,1024]{1,0:T(8,128)(2,1)} %q_nope_in.1) | copy-start | bytes 786436
  7.6 3.2 %collective-permute-start.3 = (bf16[16,16,128]{2,1,0:T(8,128)(2,1)S(1)}, bf16[16,16,128]{2,1,0:T(8,128)(2,1)S(1)}, u32[]{:S(2)}, u32[]{:S(2)}) collective-permute-start(bf16[16,16,128]{2,1,0:T(8,128)(2,1)S(1)} %pad_maximum_fusion.refs_4_), channel_id=1, source_target_pairs={{0,64},{1,65},{2,66},{3,67},{4,68},{5,69},{6,70},{7,71},{8,72},{9,... | collective-permute-start | bytes 196616 | tf_op jit(solution)/shard_map/ppermute | solution.py:31
  7.7 5.6 %collective-permute-start.4 = (bf16[16,16,128]{2,1,0:T(8,128)(2,1)S(1)}, bf16[16,16,128]{2,1,0:T(8,128)(2,1)S(1)}, u32[]{:S(2)}, u32[]{:S(2)}) collective-permute-start(bf16[16,16,128]{2,1,0:T(8,128)(2,1)S(1)} %pad_maximum_fusion.refs_4_), channel_id=1, source_target_pairs={{0,128},{1,129},{2,130},{3,131},{4,132},{5,133},{6,134},{7,135},{8... | collective-permute-start | bytes 196616 | tf_op jit(solution)/shard_map/ppermute | solution.py:31
  10.8 5.5 %collective-permute-start.5 = (bf16[16,16,128]{2,1,0:T(8,128)(2,1)S(1)}, bf16[16,16,128]{2,1,0:T(8,128)(2,1)S(1)}, u32[]{:S(2)}, u32[]{:S(2)}) collective-permute-start(bf16[16,16,128]{2,1,0:T(8,128)(2,1)S(1)} %pad_maximum_fusion.refs_4_), channel_id=1, source_target_pairs={{0,192},{1,193},{2,194},{3,195},{4,196},{5,197},{6,198},{7,199},{8... | collective-permute-start | bytes 196616 | tf_op jit(solution)/shard_map/ppermute | solution.py:31
  16.8 17.8 %collective-permute-start.6 = (bf16[4,128,640]{2,1,0:T(8,128)(2,1)S(1)}, bf16[4,128,640]{2,1,0:T(8,128)(2,1)S(1)}, u32[]{:S(2)}, u32[]{:S(2)}) collective-permute-start(bf16[4,128,640]{2,1,0:T(8,128)(2,1)S(1)} %get-tuple-element.32.row), channel_id=1, source_target_pairs={{0,196},{1,197},{2,198},{3,199},{4,192},{5,193},{6,194},{7,195},{8... | collective-permute-start | bytes 1966088 | tf_op jit(solution)/shard_map/ppermute | solution.py:31
  17.2 17.5 %collective-permute-start.7 = (bf16[4,128,640]{2,1,0:T(8,128)(2,1)S(1)}, bf16[4,128,640]{2,1,0:T(8,128)(2,1)S(1)}, u32[]{:S(2)}, u32[]{:S(2)}) collective-permute-start(bf16[4,128,640]{2,1,0:T(8,128)(2,1)S(1)} %get-tuple-element.32.row), channel_id=1, source_target_pairs={{0,64},{1,65},{2,66},{3,67},{4,68},{5,69},{6,70},{7,71},{8,72},{9,... | collective-permute-start | bytes 1966088 | tf_op jit(solution)/shard_map/ppermute | solution.py:31
  18.6 5.7 %collective-permute-start.8 = (bf16[4,16,16,128]{3,2,1,0:T(8,128)(2,1)S(1)}, bf16[4,16,16,128]{3,2,1,0:T(8,128)(2,1)S(1)}, u32[]{:S(2)}, u32[]{:S(2)}) collective-permute-start(bf16[4,16,16,128]{3,2,1,0:T(8,128)(2,1)S(1)} %get-tuple-element.33.rest_0_), channel_id=1, source_target_pairs={{0,48},{1,49},{2,50},{3,51},{4,52},{5,53},{6,54},{7,55},{8,56},{9,... | collective-permute-start | bytes 786440 | tf_op jit(solution)/shard_map/ppermute | solution.py:31
  20.3 6.8 %collective-permute-start.9 = (bf16[4,16,16,128]{3,2,1,0:T(8,128)(2,1)S(1)}, bf16[4,16,16,128]{3,2,1,0:T(8,128)(2,1)S(1)}, u32[]{:S(2)}, u32[]{:S(2)}) collective-permute-start(bf16[4,16,16,128]{3,2,1,0:T(8,128)(2,1)S(1)} %get-tuple-element.33.rest_0_), channel_id=1, source_target_pairs={{0,32},{1,33},{2,34},{3,35},{4,36},{5,37},{6,38},{7,39},{8,40},{9,... | collective-permute-start | bytes 786440 | tf_op jit(solution)/shard_map/ppermute | solution.py:31
  21.5 13.1 %collective-permute-start.10 = (bf16[4,16,16,128]{3,2,1,0:T(8,128)(2,1)S(1)}, bf16[4,16,16,128]{3,2,1,0:T(8,128)(2,1)S(1)}, u32[]{:S(2)}, u32[]{:S(2)}) collective-permute-start(bf16[4,16,16,128]{3,2,1,0:T(8,128)(2,1)S(1)} %get-tuple-element.33.rest_0_), channel_id=1, source_target_pairs={{0,16},{1,17},{2,18},{3,19},{4,20},{5,21},{6,22},{7,23},{8,24},{9,... | collective-permute-start | bytes 786440 | tf_op jit(solution)/shard_map/ppermute | solution.py:31
  36.4 20.7 %collective-permute-start.14 = (bf16[12,128,640]{2,1,0:T(8,128)(2,1)}, bf16[12,128,640]{2,1,0:T(8,128)(2,1)}, u32[]{:S(2)}, u32[]{:S(2)}) collective-permute-start(bf16[12,128,640]{2,1,0:T(8,128)(2,1)} %get-tuple-element.37.rest_0_), channel_id=1, source_target_pairs={{0,8},{1,9},{2,10},{3,11},{4,12},{5,13},{6,14},{7,15},{8,0},{9,1},... | collective-permute-start | bytes 5898248 | tf_op jit(solution)/shard_map/ppermute | solution.py:31
  39.7 5.0 %collective-permute-start.11 = (bf16[4,4,16,16,128]{4,3,2,1,0:T(8,128)(2,1)S(1)}, bf16[4,4,16,16,128]{4,3,2,1,0:T(8,128)(2,1)S(1)}, u32[]{:S(2)}, u32[]{:S(2)}) collective-permute-start(bf16[4,4,16,16,128]{4,3,2,1,0:T(8,128)(2,1)S(1)} %get-tuple-element.34.mine), channel_id=1, source_target_pairs={{0,8},{1,9},{2,10},{3,11},{4,12},{5,13},{6,14},{7,15},{8,0},{9,1},... | collective-permute-start | bytes 3145736 | tf_op jit(solution)/shard_map/ppermute | solution.py:31
  39.7 9.6 %collective-permute-start.12 = (bf16[2,128,640]{2,1,0:T(8,128)(2,1)}, bf16[2,128,640]{2,1,0:T(8,128)(2,1)S(1)}, u32[]{:S(2)}, u32[]{:S(2)}) collective-permute-start(bf16[2,128,640]{2,1,0:T(8,128)(2,1)} %get-tuple-element.38), channel_id=1, source_target_pairs={{0,196},{1,197},{2,198},{3,199},{4,192},{5,193},{6,194},{7,195},{8... | collective-permute-start | bytes 983048 | tf_op jit(solution)/shard_map/ppermute | solution.py:31
  42.4 8.8 %collective-permute-start.13 = (bf16[2,128,640]{2,1,0:T(8,128)(2,1)}, bf16[2,128,640]{2,1,0:T(8,128)(2,1)S(1)}, u32[]{:S(2)}, u32[]{:S(2)}) collective-permute-start(bf16[2,128,640]{2,1,0:T(8,128)(2,1)} %get-tuple-element.39), channel_id=1, source_target_pairs={{0,64},{1,65},{2,66},{3,67},{4,68},{5,69},{6,70},{7,71},{8,72},{9,... | collective-permute-start | bytes 983048 | tf_op jit(solution)/shard_map/ppermute | solution.py:31
  44.7 0.9 copy-start.5
  48.1 16.2 %copy-start.1 = (bf16[224,1024]{1,0:T(8,128)(2,1)}, bf16[224,1024]{1,0:T(8,128)(2,1)S(1)}, u32[]{:S(2)}) copy-start(bf16[224,1024]{1,0:T(8,128)(2,1)S(1)} %get-tuple-element.44.rest_0_) | copy-start | bytes 1376260
  51.2 4.7 %collective-permute-start.15 = (bf16[2,128,640]{2,1,0:T(8,128)(2,1)S(1)}, bf16[2,128,640]{2,1,0:T(8,128)(2,1)S(1)}, u32[]{:S(2)}, u32[]{:S(2)}) collective-permute-start(bf16[2,128,640]{2,1,0:T(8,128)(2,1)S(1)} %get-tuple-element.41.rest_1_), channel_id=1, source_target_pairs={{0,8},{1,9},{2,10},{3,11},{4,12},{5,13},{6,14},{7,15},{8,0},{9,1},... | collective-permute-start | bytes 983048 | tf_op jit(solution)/shard_map/ppermute | solution.py:31
  53.1 4.0 %collective-permute-start.16 = (bf16[2,128,640]{2,1,0:T(8,128)(2,1)S(1)}, bf16[2,128,640]{2,1,0:T(8,128)(2,1)S(1)}, u32[]{:S(2)}, u32[]{:S(2)}) collective-permute-start(bf16[2,128,640]{2,1,0:T(8,128)(2,1)S(1)} %get-tuple-element.42.rest_2_), channel_id=1, source_target_pairs={{0,8},{1,9},{2,10},{3,11},{4,12},{5,13},{6,14},{7,15},{8,0},{9,1},... | collective-permute-start | bytes 983048 | tf_op jit(solution)/shard_map/ppermute | solution.py:31
  53.2 19.3 %collective-permute-start.17 = (bf16[224,1024]{1,0:T(8,128)(2,1)S(1)}, bf16[224,1024]{1,0:T(8,128)(2,1)S(1)}, u32[]{:S(2)}, u32[]{:S(2)}) collective-permute-start(bf16[224,1024]{1,0:T(8,128)(2,1)S(1)} %get-tuple-element.44.rest_0_), channel_id=1, source_target_pairs={{0,64},{1,65},{2,66},{3,67},{4,68},{5,69},{6,70},{7,71},{8,72},{9,... | collective-permute-start | bytes 1376264 | tf_op jit(solution)/shard_map/ppermute | solution.py:31
  55.9 27.1 %collective-permute-start.22 = (bf16[224,1024]{1,0:T(8,128)(2,1)S(1)}, bf16[224,1024]{1,0:T(8,128)(2,1)S(1)}, u32[]{:S(2)}, u32[]{:S(2)}) collective-permute-start(bf16[224,1024]{1,0:T(8,128)(2,1)S(1)} %get-tuple-element.44.rest_0_), channel_id=1, source_target_pairs={{0,128},{1,129},{2,130},{3,131},{4,132},{5,133},{6,134},{7,135},{8... | collective-permute-start | bytes 1376264 | tf_op jit(solution)/shard_map/ppermute | solution.py:31
  55.9 40.9 %collective-permute-start.23 = (bf16[224,1024]{1,0:T(8,128)(2,1)S(1)}, bf16[224,1024]{1,0:T(8,128)(2,1)S(1)}, u32[]{:S(2)}, u32[]{:S(2)}) collective-permute-start(bf16[224,1024]{1,0:T(8,128)(2,1)S(1)} %get-tuple-element.44.rest_0_), channel_id=1, source_target_pairs={{0,192},{1,193},{2,194},{3,195},{4,196},{5,197},{6,198},{7,199},{8... | collective-permute-start | bytes 1376264 | tf_op jit(solution)/shard_map/ppermute | solution.py:31
  72.5 6.6 %collective-permute-start.18 = (bf16[1024,128]{1,0:T(8,128)(2,1)S(1)}, bf16[1024,128]{1,0:T(8,128)(2,1)S(1)}, u32[]{:S(2)}, u32[]{:S(2)}) collective-permute-start(bf16[1024,128]{1,0:T(8,128)(2,1)S(1)} %hold.1.own), channel_id=1, source_target_pairs={{0,48},{1,49},{2,50},{3,51},{4,52},{5,53},{6,54},{7,55},{8,56},{9,... | collective-permute-start | bytes 786440 | tf_op jit(solution)/shard_map/ppermute | solution.py:31
  73.9 7.5 %collective-permute-start.19 = (bf16[1024,128]{1,0:T(8,128)(2,1)S(1)}, bf16[1024,128]{1,0:T(8,128)(2,1)S(1)}, u32[]{:S(2)}, u32[]{:S(2)}) collective-permute-start(bf16[1024,128]{1,0:T(8,128)(2,1)S(1)} %hold.1.own), channel_id=1, source_target_pairs={{0,16},{1,17},{2,18},{3,19},{4,20},{5,21},{6,22},{7,23},{8,24},{9,... | collective-permute-start | bytes 786440 | tf_op jit(solution)/shard_map/ppermute | solution.py:31
  81.4 15.4 %collective-permute-start.20 = (bf16[512,128]{1,0:T(8,128)(2,1)S(1)}, bf16[512,128]{1,0:T(8,128)(2,1)S(1)}, u32[]{:S(2)}, u32[]{:S(2)}) collective-permute-start(bf16[512,128]{1,0:T(8,128)(2,1)S(1)} %get-tuple-element.45), channel_id=1, source_target_pairs={{0,48},{1,49},{2,50},{3,51},{4,52},{5,53},{6,54},{7,55},{8,56},{9,... | collective-permute-start | bytes 393224 | tf_op jit(solution)/shard_map/ppermute | solution.py:31
  81.8 15.0 %collective-permute-start.21 = (bf16[512,128]{1,0:T(8,128)(2,1)S(1)}, bf16[512,128]{1,0:T(8,128)(2,1)S(1)}, u32[]{:S(2)}, u32[]{:S(2)}) collective-permute-start(bf16[512,128]{1,0:T(8,128)(2,1)S(1)} %get-tuple-element.46), channel_id=1, source_target_pairs={{0,16},{1,17},{2,18},{3,19},{4,20},{5,21},{6,22},{7,23},{8,24},{9,... | collective-permute-start | bytes 393224 | tf_op jit(solution)/shard_map/ppermute | solution.py:31
  96.9 3.6 %collective-permute-start.24 = (bf16[4,1024,128]{2,1,0:T(8,128)(2,1)S(1)}, bf16[4,1024,128]{2,1,0:T(8,128)(2,1)S(1)}, u32[]{:S(2)}, u32[]{:S(2)}) collective-permute-start(bf16[4,1024,128]{2,1,0:T(8,128)(2,1)S(1)} %third.1.mine), channel_id=1, source_target_pairs={{0,8},{1,9},{2,10},{3,11},{4,12},{5,13},{6,14},{7,15},{8,0},{9,1},... | collective-permute-start | bytes 3145736 | tf_op jit(solution)/shard_map/ppermute | solution.py:31
  100.5 1.0 copy-start.2
  103.9 6.9 %collective-permute-start.25 = (bf16[2,224,256]{2,1,0:T(8,128)(2,1)S(1)}, bf16[2,224,256]{2,1,0:T(8,128)(2,1)S(1)}, u32[]{:S(2)}, u32[]{:S(2)}) collective-permute-start(bf16[2,224,256]{2,1,0:T(8,128)(2,1)S(1)} %get-tuple-element.48), channel_id=1, source_target_pairs={{0,1},{1,2},{2,3},{3,0},{4,5},{5,6},{6,7},{7,4},{8,9},{9,10},{10,1... | collective-permute-start | bytes 688136 | tf_op jit(solution)/shard_map/ppermute | solution.py:31
  105.3 6.5 %collective-permute-start.26 = (bf16[2,224,256]{2,1,0:T(8,128)(2,1)S(1)}, bf16[2,224,256]{2,1,0:T(8,128)(2,1)S(1)}, u32[]{:S(2)}, u32[]{:S(2)}) collective-permute-start(bf16[2,224,256]{2,1,0:T(8,128)(2,1)S(1)} %get-tuple-element.49), channel_id=1, source_target_pairs={{0,3},{1,0},{2,1},{3,2},{4,7},{5,4},{6,5},{7,6},{8,11},{9,8},{10,9... | collective-permute-start | bytes 688136 | tf_op jit(solution)/shard_map/ppermute | solution.py:31
  111.9 5.6 %collective-permute-start.27 = (bf16[2,224,256]{2,1,0:T(8,128)(2,1)S(1)}, bf16[2,224,256]{2,1,0:T(8,128)(2,1)S(1)}, u32[]{:S(2)}, u32[]{:S(2)}) collective-permute-start(bf16[2,224,256]{2,1,0:T(8,128)(2,1)S(1)} %get-tuple-element.50), channel_id=1, source_target_pairs={{0,1},{1,2},{2,3},{3,0},{4,5},{5,6},{6,7},{7,4},{8,9},{9,10},{10,1... | collective-permute-start | bytes 688136 | tf_op jit(solution)/shard_map/ppermute | solution.py:31
  113.0 6.0 %collective-permute-start.28 = (bf16[2,224,256]{2,1,0:T(8,128)(2,1)S(1)}, bf16[2,224,256]{2,1,0:T(8,128)(2,1)S(1)}, u32[]{:S(2)}, u32[]{:S(2)}) collective-permute-start(bf16[2,224,256]{2,1,0:T(8,128)(2,1)S(1)} %get-tuple-element.52), channel_id=1, source_target_pairs={{0,3},{1,0},{2,1},{3,2},{4,7},{5,4},{6,5},{7,6},{8,11},{9,8},{10,9... | collective-permute-start | bytes 688136 | tf_op jit(solution)/shard_map/ppermute | solution.py:31
  119.8 9.4 %collective-permute-start.31 = (bf16[2,224,256]{2,1,0:T(8,128)(2,1)S(1)}, bf16[2,224,256]{2,1,0:T(8,128)(2,1)S(1)}, u32[]{:S(2)}, u32[]{:S(2)}) collective-permute-start(bf16[2,224,256]{2,1,0:T(8,128)(2,1)S(1)} %get-tuple-element.55), channel_id=1, source_target_pairs={{0,1},{1,2},{2,3},{3,0},{4,5},{5,6},{6,7},{7,4},{8,9},{9,10},{10,1... | collective-permute-start | bytes 688136 | tf_op jit(solution)/shard_map/ppermute | solution.py:31
  121.2 7.9 %collective-permute-start.32 = (bf16[2,224,256]{2,1,0:T(8,128)(2,1)S(1)}, bf16[2,224,256]{2,1,0:T(8,128)(2,1)S(1)}, u32[]{:S(2)}, u32[]{:S(2)}) collective-permute-start(bf16[2,224,256]{2,1,0:T(8,128)(2,1)S(1)} %get-tuple-element.56), channel_id=1, source_target_pairs={{0,3},{1,0},{2,1},{3,2},{4,7},{5,4},{6,5},{7,6},{8,11},{9,8},{10,9... | collective-permute-start | bytes 688136 | tf_op jit(solution)/shard_map/ppermute | solution.py:31
  121.3 14.4 %collective-permute-start.29 = (bf16[224,256]{1,0:T(8,128)(2,1)S(1)}, bf16[224,256]{1,0:T(8,128)(2,1)S(1)}, u32[]{:S(2)}, u32[]{:S(2)}) collective-permute-start(bf16[224,256]{1,0:T(8,128)(2,1)S(1)} %get-tuple-element.53), channel_id=1, source_target_pairs={{0,4},{1,36},{2,6},{3,38},{4,0},{5,32},{6,2},{7,34},{8,12},{9,44},... | collective-permute-start | bytes 344072 | tf_op jit(solution)/shard_map/ppermute | solution.py:31
  125.6 12.3 %collective-permute-start.30 = (bf16[224,256]{1,0:T(8,128)(2,1)S(1)}, bf16[224,256]{1,0:T(8,128)(2,1)S(1)}, u32[]{:S(2)}, u32[]{:S(2)}) collective-permute-start(bf16[224,256]{1,0:T(8,128)(2,1)S(1)} %get-tuple-element.54), channel_id=1, source_target_pairs={{0,20},{1,52},{2,22},{3,54},{4,16},{5,48},{6,18},{7,50},{8,28},{9,... | collective-permute-start | bytes 344072 | tf_op jit(solution)/shard_map/ppermute | solution.py:31
  129.8 9.2 %collective-permute-start.33 = (bf16[224,256]{1,0:T(8,128)(2,1)S(1)}, bf16[224,256]{1,0:T(8,128)(2,1)S(1)}, u32[]{:S(2)}, u32[]{:S(2)}) collective-permute-start(bf16[224,256]{1,0:T(8,128)(2,1)S(1)} %get-tuple-element.57), channel_id=1, source_target_pairs={{0,0},{1,32},{2,2},{3,34},{4,4},{5,36},{6,6},{7,38},{8,8},{9,40},{... | collective-permute-start | bytes 344072 | tf_op jit(solution)/shard_map/ppermute | solution.py:31
  134.4 8.0 %collective-permute-start.34 = (bf16[224,256]{1,0:T(8,128)(2,1)S(1)}, bf16[224,256]{1,0:T(8,128)(2,1)S(1)}, u32[]{:S(2)}, u32[]{:S(2)}) collective-permute-start(bf16[224,256]{1,0:T(8,128)(2,1)S(1)} %get-tuple-element.58), channel_id=1, source_target_pairs={{0,16},{1,48},{2,18},{3,50},{4,20},{5,52},{6,22},{7,54},{8,24},{9,... | collective-permute-start | bytes 344072 | tf_op jit(solution)/shard_map/ppermute | solution.py:31
  142.4 3.3 %collective-permute-start.35 = (bf16[2,224,128]{2,1,0:T(8,128)(2,1)S(1)}, bf16[2,224,128]{2,1,0:T(8,128)(2,1)S(1)}, u32[]{:S(2)}, u32[]{:S(2)}) collective-permute-start(bf16[2,224,128]{2,1,0:T(8,128)(2,1)S(1)} %get-tuple-element.60), channel_id=1, source_target_pairs={{0,8},{1,9},{2,10},{3,11},{4,12},{5,13},{6,14},{7,15},{8,0},{9,1},... | collective-permute-start | bytes 344072 | tf_op jit(solution)/shard_map/ppermute | solution.py:31
